TPU v7x, 512 devices: a whole 4x8x8 slice. The times are simulated.
512 devices in a mesh: pipe: 128 (over z_lo, y, x, core), seq: 4 (over z_hi).
Axes of the slice: x: 4, y: 8, z: 8 (z_hi: 4, z_lo: 2; z = z_hi * 2 + z_lo), core: 2. Of those that a mesh axis runs over, the one named last changes fastest.
Arguments:
- patches: bfloat16 [128, 512, 1152], P('pipe', 'seq'), may hold values from -3 to 3
- qkv_weight: bfloat16 [128, 1152, 3, 1152], P('pipe', None, None, 'seq'), may hold values from -0.1875 to 0.1875
- out_weight: bfloat16 [128, 1152, 1152], P('pipe', 'seq'), may hold values from -0.1875 to 0.1875
- modulation: float32 [128, 3, 1152], P('pipe'), may hold values from -1.6 to 1.6
- stale_keys: bfloat16 [128, 1024, 1152], P('pipe', None, 'seq'), may hold values from -900 to 900
- stale_values: bfloat16 [128, 1024, 1152], P('pipe', None, 'seq'), may hold values from -6 to 6
- offsets: int32 [128, 2], P('pipe'), may hold values from 0 to 1
Outputs:
- leaving: bfloat16 [128, 512, 1152], P('pipe', 'seq')
All inputs are finite; a program needn't handle non-finite values.
Results may differ from a plain program's by a relative error of at most 0.033.
Values may be sent and summed in bfloat16 or wider, within the bound.
No kernel may reach another device: no remote copies, remote signals or barrier semaphores. Data moves between devices by JAX's collectives and lax.ppermute only.
A program may use at most 64 MiB of HBM per device.

v0:
```python
import math

import jax
import jax.numpy as jnp
from jax import lax
from jax.sharding import PartitionSpec as P

HEAD_DIM = 72
TICKS = 2


def shifted(array, axis, by):
    count = lax.axis_size(axis)
    return lax.ppermute(array, axis, [(i, (i + by) % count) for i in range(count)])


def normalize(rows, shift, scale):
    values = rows.astype(jnp.float32)
    center = jnp.mean(values, axis=-1, keepdims=True)
    spread = jnp.mean((values - center) * (values - center), axis=-1, keepdims=True)
    normed = (values - center) * lax.rsqrt(spread + 1e-06)
    return (normed * (1.0 + scale) + shift).astype(jnp.bfloat16)


def attend(query, keys, values):
    scores = jnp.einsum("qhd,khd->hqk", query, keys, preferred_element_type=jnp.float32)
    probs = jax.nn.softmax(scores * (1.0 / math.sqrt(HEAD_DIM)), axis=-1).astype(jnp.bfloat16)
    mixed = jnp.einsum("hqk,khd->qhd", probs, values, preferred_element_type=jnp.float32)
    return mixed.astype(jnp.bfloat16)


def body(patches, qkv_weight, out_weight, modulation, stale_keys, stale_values, offsets):
    own_rows = patches[0]
    local = own_rows.shape[0]
    group_size = lax.axis_size("seq")
    count = local * group_size
    width = qkv_weight.shape[3]
    heads_here = width // HEAD_DIM
    w_flat = qkv_weight[0].reshape(qkv_weight.shape[1], 3 * width)
    w_out = out_weight[0]
    shift = modulation[0, 0]
    scale = modulation[0, 1]
    gate = modulation[0, 2]
    keys = stale_keys[0]
    values = stale_values[0]

    def finish(hidden_rows, mixed):
        attended = lax.psum_scatter(
            jnp.dot(mixed, w_out, preferred_element_type=jnp.float32).astype(jnp.bfloat16),
            "seq",
            scatter_dimension=0,
            tiled=True,
        ).astype(jnp.float32)
        return (hidden_rows.astype(jnp.float32) + gate * attended).astype(jnp.bfloat16)

    current = own_rows
    for step in range(TICKS):
        qkv = jnp.dot(
            normalize(lax.all_gather(current, "seq", axis=0, tiled=True), shift, scale),
            w_flat,
            preferred_element_type=jnp.float32,
        )
        qkv = qkv.astype(jnp.bfloat16).reshape(count, 3, width)
        start = offsets[0, step] * count
        keys = lax.dynamic_update_slice(keys, qkv[:, 1], (start, jnp.int32(0)))
        values = lax.dynamic_update_slice(values, qkv[:, 2], (start, jnp.int32(0)))
        mixed = attend(
            qkv[:, 0].reshape(count, heads_here, HEAD_DIM),
            keys.reshape(keys.shape[0], heads_here, HEAD_DIM),
            values.reshape(values.shape[0], heads_here, HEAD_DIM),
        ).reshape(count, width)
        if step + 1 == TICKS:
            hidden_rows = current
            current = finish(hidden_rows, mixed)
        else:
            produced = finish(current, mixed)
            current = shifted(produced, "pipe", 1)
    return current[None]


def solution(mesh):
    placed = (
        P("pipe", "seq", None),
        P("pipe", None, None, "seq"),
        P("pipe", "seq", None),
        P("pipe", None, None),
        P("pipe", None, "seq"),
        P("pipe", None, "seq"),
        P("pipe", None),
    )
    return jax.shard_map(
        body, mesh=mesh, in_specs=placed, out_specs=P("pipe", "seq", None), check_vma=False
    )
```

profile of v0, /device:TPU:1, one launch (start us, length us, event | category | flops | bytes accessed | tf_op | source)
XLA Modules:
  0.0 220.8 jit_solution(4786078649344690922)
XLA Ops:
  6.5 0.0 copy-start
  6.5 0.0 copy-start.8
  6.5 0.0 copy-start.9
  6.5 0.0 all-gather.6.cloned.1.call-start
  6.5 0.7 all-gather.6.cloned.1.call-update
  7.3 0.0 reduce-scatter.3.cloned.1.call-start
  7.3 0.0 copy-done.9
  7.4 0.6 fusion.51
  8.6 0.0 copy-done.8
  8.6 46.2 %all-gather.6.cloned.1.call-done = bf16[1,512,1152]{2,1,0:T(8,128)(2,1)} async-done(((bf16[1,128,1152]{2,1,0:T(8,128)(2,1)}), bf16[1,512,1152]{2,1,0:T(8,128)(2,1)}) %all-gather.6.cloned.1.call-update) | async-done | bytes 1179664 | tf_op jit(solution)/shard_map/all_gather | solution.py:59
  54.8 0.0 copy-start.1
  54.8 1.6 convert_reduce_fusion
  56.4 1.7 fusion.21
  58.1 0.0 copy-done
  58.1 0.0 copy-done.1
  58.1 0.0 copy-start.6
  58.1 0.0 copy-start.7
  58.2 1.5 convolution_convert_fusion.3
  59.7 0.0 copy-done.6
  59.7 0.0 copy-done.7
  59.7 0.1 fusion.47
  59.8 5.0 %fusion.52 = (f32[4,512]{1,0:T(4,128)S(1)}, f32[4,512,1024]{2,1,0:T(8,128)}) fusion(bf16[512,4,72]{0,2,1:T(8,128)(2,1)S(1)} %bitcast.88, bf16[1024,4,72]{0,2,1:T(8,128)(2,1)S(1)} %bitcast.82), kind=kOutput, calls=%fused_computation.71 | convolution fusion | flops 308282368 | bytes 9281536 | tf_op jit(solution)/shard_map/sub | solution.py:27
  64.8 0.0 copy-start.10
  64.8 4.9 %fusion.26 = bf16[4,72,512]{2,1,0:T(8,128)(2,1)S(1)} fusion(bf16[1024,4,72]{0,2,1:T(8,128)(2,1)S(1)} %bitcast.85, f32[4,512,1024]{2,1,0:T(8,128)} %get-tuple-element.15, f32[4,512]{1,0:T(4,128)S(1)} %get-tuple-element.14), kind=kOutput, calls=%fused_computation.36 | convolution fusion | flops 306331648 | bytes 9281536 | tf_op jit(solution)/shard_map/hqk,khd->qhd/dot_general | solution.py:28
  69.7 0.0 copy-start.3
  69.7 0.0 copy-done.10
  69.7 1.9 convolution_convert_fusion.1
  71.6 0.0 reduce-scatter.3.cloned.1.call-update
  71.6 0.0 all-gather.4.cloned.1.call-start
  71.7 37.3 %reduce-scatter.3.cloned.1.call-done = bf16[128,1152]{1,0:T(8,128)(2,1)} async-done(((bf16[512,1152]{1,0:T(8,128)(2,1)}), bf16[128,1152]{1,0:T(8,128)(2,1)}) %reduce-scatter.3.cloned.1.call-update) | async-done | bytes 294928 | tf_op jit(solution)/shard_map/reduce_scatter | solution.py:48
  109.0 0.0 copy-done.3
  109.0 1.1 fusion.43
  110.1 3.7 %collective-permute-start = (bf16[128,1152]{1,0:T(8,128)(2,1)S(1)}, bf16[128,1152]{1,0:T(8,128)(2,1)S(1)}, u32[]{:S(2)}, u32[]{:S(2)}) collective-permute-start(bf16[128,1152]{1,0:T(8,128)(2,1)S(1)} %fusion.43), channel_id=1, source_target_pairs={{0,4},{4,8},{8,12},{12,16},{16,20},{20,24},{24,28},{28,32},{32,36}... | collective-permute-start | bytes 884744 | tf_op jit(solution)/shard_map/ppermute | solution.py:14
  113.8 3.6 %collective-permute-done = bf16[128,1152]{1,0:T(8,128)(2,1)S(1)} collective-permute-done((bf16[128,1152]{1,0:T(8,128)(2,1)S(1)}, bf16[128,1152]{1,0:T(8,128)(2,1)S(1)}, u32[]{:S(2)}, u32[]{:S(2)}) %collective-permute-start) | collective-permute-done | bytes 294944 | tf_op jit(solution)/shard_map/ppermute | solution.py:14
  117.4 0.0 copy-start.4
  117.4 0.7 copy-done.4
  118.1 0.0 all-gather.4.cloned.1.call-update
  118.2 0.0 reduce-scatter.5.cloned.1.call-start
  118.8 39.4 %all-gather.4.cloned.1.call-done = bf16[512,1152]{1,0:T(8,128)(2,1)} async-done(((bf16[128,1152]{1,0:T(8,128)(2,1)}), bf16[512,1152]{1,0:T(8,128)(2,1)}) %all-gather.4.cloned.1.call-update) | async-done | bytes 1179664 | tf_op jit(solution)/shard_map/all_gather | solution.py:59
  158.2 0.0 copy-start.2
  158.2 1.6 convert_reduce_fusion.1
  159.8 1.7 fusion.14
  161.5 0.0 copy-done.2
  161.5 1.5 convolution_convert_fusion.2
  163.1 0.1 fusion.45
  163.2 5.0 %fusion.53 = (f32[4,512]{1,0:T(4,128)S(1)}, f32[4,512,1024]{2,1,0:T(8,128)}) fusion(bf16[512,4,72]{0,2,1:T(8,128)(2,1)S(1)} %bitcast.89, bf16[1024,4,72]{0,2,1:T(8,128)(2,1)S(1)} %bitcast.83), kind=kOutput, calls=%fused_computation.72 | convolution fusion | flops 308282368 | bytes 9281536 | tf_op jit(solution)/shard_map/sub | solution.py:27
  168.1 0.0 copy-start.11
  168.1 4.9 %fusion.25 = bf16[4,72,512]{2,1,0:T(8,128)(2,1)S(1)} fusion(bf16[1024,4,72]{0,2,1:T(8,128)(2,1)S(1)} %bitcast.86, f32[4,512,1024]{2,1,0:T(8,128)} %get-tuple-element.17, f32[4,512]{1,0:T(4,128)S(1)} %get-tuple-element.16), kind=kOutput, calls=%fused_computation.35 | convolution fusion | flops 306331648 | bytes 9281536 | tf_op jit(solution)/shard_map/hqk,khd->qhd/dot_general | solution.py:28
  173.1 0.0 copy-start.5
  173.1 0.0 copy-done.11
  173.1 1.9 convolution_convert_fusion
  175.0 0.0 reduce-scatter.5.cloned.1.call-update
  175.0 37.5 %reduce-scatter.5.cloned.1.call-done = bf16[128,1152]{1,0:T(8,128)(2,1)} async-done(((bf16[512,1152]{1,0:T(8,128)(2,1)}), bf16[128,1152]{1,0:T(8,128)(2,1)}) %reduce-scatter.5.cloned.1.call-update) | async-done | bytes 294928 | tf_op jit(solution)/shard_map/reduce_scatter | solution.py:48
  212.5 0.0 copy-done.5
  212.5 1.8 fusion.44
  (7 shorter events, 0.1 us)
Async XLA Ops:
  6.5 51.6 %copy-start = (bf16[1,1152,3,288]{1,3,2,0:T(8,128)(2,1)S(1)}, bf16[1,1152,3,288]{1,3,2,0:T(8,128)(2,1)}, u32[]{:S(2)}) copy-start(bf16[1,1152,3,288]{1,3,2,0:T(8,128)(2,1)} %param.8) | copy-start | bytes 5971972
  6.5 2.0 copy-start.8
  6.5 0.8 copy-start.9
  6.5 48.2 %all-gather.6.cloned.1.call-start = ((), (), s32[]{:S(2)}) async-start(), calls=%async_computation.5 | async-start | bytes 1474560 | tf_op jit(solution)/shard_map/all_gather | solution.py:59
  7.3 101.8 %reduce-scatter.3.cloned.1.call-start = ((), (), s32[]{:S(2)}) async-start(), calls=%async_computation.2 | async-start | bytes 1474560 | tf_op jit(solution)/shard_map/reduce_scatter | solution.py:48
  54.8 3.3 %copy-start.1 = (bf16[1,512,1152]{2,1,0:T(8,128)(2,1)S(1)}, bf16[1,512,1152]{2,1,0:T(8,128)(2,1)}, u32[]{:S(2)}) copy-start(bf16[1,512,1152]{2,1,0:T(8,128)(2,1)} %all-gather.6.cloned.1.call-done) | copy-start | bytes 3538948
  58.1 1.6 copy-start.6
  58.1 1.6 copy-start.7
  64.8 5.0 %copy-start.10 = (bf16[1,288,1152]{2,1,0:T(8,128)(2,1)S(1)}, bf16[1,288,1152]{2,1,0:T(8,128)(2,1)}, u32[]{:S(2)}) copy-start(bf16[1,288,1152]{2,1,0:T(8,128)(2,1)} %param.9) | copy-start | bytes 1990660
  69.7 39.3 %copy-start.3 = (bf16[1,128,1152]{2,1,0:T(8,128)(2,1)S(1)}, bf16[1,128,1152]{2,1,0:T(8,128)(2,1)}, u32[]{:S(2)}) copy-start(bf16[1,128,1152]{2,1,0:T(8,128)(2,1)} %param.7) | copy-start | bytes 884740
  71.6 86.6 %all-gather.4.cloned.1.call-start = ((), (), s32[]{:S(2)}) async-start(), calls=%async_computation.3 | async-start | bytes 1474560 | tf_op jit(solution)/shard_map/all_gather | solution.py:59
  110.1 7.3 %collective-permute-start = (bf16[128,1152]{1,0:T(8,128)(2,1)S(1)}, bf16[128,1152]{1,0:T(8,128)(2,1)S(1)}, u32[]{:S(2)}, u32[]{:S(2)}) collective-permute-start(bf16[128,1152]{1,0:T(8,128)(2,1)S(1)} %fusion.43), channel_id=1, source_target_pairs={{0,4},{4,8},{8,12},{12,16},{16,20},{20,24},{24,28},{28,32},{32,36}... | collective-permute-start | bytes 884744 | tf_op jit(solution)/shard_map/ppermute | solution.py:14
  117.4 0.7 copy-start.4
  118.2 94.3 %reduce-scatter.5.cloned.1.call-start = ((), (), s32[]{:S(2)}) async-start(), calls=%async_computation.4 | async-start | bytes 1474560 | tf_op jit(solution)/shard_map/reduce_scatter | solution.py:48
  158.2 3.3 %copy-start.2 = (bf16[512,1152]{1,0:T(8,128)(2,1)S(1)}, bf16[512,1152]{1,0:T(8,128)(2,1)}, u32[]{:S(2)}) copy-start(bf16[512,1152]{1,0:T(8,128)(2,1)} %all-gather.4.cloned.1.call-done) | copy-start | bytes 3538948
  168.1 5.0 %copy-start.11 = (bf16[1,288,1152]{2,1,0:T(8,128)(2,1)S(1)}, bf16[1,288,1152]{2,1,0:T(8,128)(2,1)}, u32[]{:S(2)}) copy-start(bf16[1,288,1152]{2,1,0:T(8,128)(2,1)} %param.9) | copy-start | bytes 1990660
  173.1 39.4 %copy-start.5 = (bf16[128,1152]{1,0:T(8,128)(2,1)S(1)}, bf16[128,1152]{1,0:T(8,128)(2,1)}, u32[]{:S(2)}) copy-start(bf16[128,1152]{1,0:T(8,128)(2,1)} %copy-done.4) | copy-start | bytes 884740
Sparse Core Ops, SparseCore 0:
  9.5 45.2 all-gather.5
  71.8 37.2 reduce-scatter.2
  118.3 39.8 all-gather.3
  175.1 37.3 reduce-scatter.4
where the time goes:
time: 221 us
  waiting for transfers between devices  165 us (75%)
  matrix products  26.6 us (12%)
  between operations  14.5 us (7%)
  other arithmetic  9.55 us (4%)
  starting transfers between devices  3.79 us (2%)
    all_gather x2, waiting for transfers between devices, body(): lax.all_gather(current, 'seq', axis=0, tiled=True)  85.6 us
    reduce_scatter x2, waiting for transfers between devices, finish(): lax.psum_scatter(jnp.dot(mixed, w_out, preferred_element_type=jnp.float32...  74.9 us
    sub x2, matrix products, attend(): jax.nn.softmax(scores * (1.0 / math.sqrt(HEAD_DIM)), axis=-1)  9.94 us
    dot_general x2, matrix products, attend(): jnp.einsum('hqk,khd->qhd', probs, values, preferred_element_type=jnp.floa...  9.87 us
  transfers between devices with their start and end apart: 5, of which 5 were waited for; matrix products, arithmetic and copies ran while one was open for 0% of the time, Pallas kernels for 0%

commit v1 on v0

v1 whole, which is shorter than its diff:
```python
import functools
import math

import jax
import jax.numpy as jnp
from jax import lax
from jax.experimental import pallas as pl
from jax.experimental.pallas import tpu as pltpu
from jax.sharding import PartitionSpec as P

HEAD_DIM = 72
TICKS = 2
AXES = ("pipe", "seq")
EXPONENT = math.log2(math.e) / math.sqrt(HEAD_DIM)


def partner(kind, section, member):
    if (kind + section) % 2 == 0:
        return member ^ 1
    return 3 - member


def exchange(array, kind, by=0):
    sections, members = lax.axis_size("pipe"), lax.axis_size("seq")
    moves = []
    for section in range(sections):
        target = (section + by) % sections
        for member in range(members):
            source = member if kind is None else partner(kind, target, member)
            moves.append((section * members + source, target * members + member))
    return lax.ppermute(array, AXES, moves)


def dot(a, b, contract_a, contract_b):
    return lax.dot_general(
        a, b, (((contract_a,), (contract_b,)), ((), ())), preferred_element_type=jnp.float32
    )


def normalize(rows, shift, scale):
    values = rows.astype(jnp.float32)
    center = jnp.mean(values, axis=-1, keepdims=True)
    values = values - center
    spread = jnp.mean(values * values, axis=-1, keepdims=True)
    return (values * lax.rsqrt(spread + 1e-06) * (1.0 + scale) + shift).astype(jnp.bfloat16)


def block_kernel(
    own_ref, one_ref, two_ref, far_a_ref, far_b_ref, mods_ref, w_ref, ko_ref, vo_ref, wo_ref,
    p_own, p_one_a, p_one_b, p_two_a, p_two_b, p_far_a, p_far_b, kn_ref, vn_ref,
    normed, qkv, mixed,
):
    rows = own_ref.shape[0]
    half = rows // 2
    width = wo_ref.shape[0]
    at = 0
    for ref in (own_ref, one_ref, two_ref, far_a_ref, far_b_ref):
        normed[at : at + ref.shape[0]] = normalize(ref[...], mods_ref[0:1], mods_ref[1:2])
        at += ref.shape[0]
    qkv[...] = dot(w_ref[...], normed[...], 1, 1)
    kn_ref[...] = qkv[width : 2 * width].astype(jnp.bfloat16)
    vn_ref[...] = qkv[2 * width :].astype(jnp.bfloat16)
    ko = ko_ref[...].astype(jnp.float32)
    vo = vo_ref[...].astype(jnp.float32)
    for h in range(width // HEAD_DIM):
        lo, hi = h * HEAD_DIM, (h + 1) * HEAD_DIM
        q = qkv[lo:hi].astype(jnp.bfloat16)
        kn = qkv[width + lo : width + hi].astype(jnp.bfloat16)
        vn = qkv[2 * width + lo : 2 * width + hi].astype(jnp.bfloat16)
        s1 = dot(kn, q, 0, 0)
        s2 = dot(ko[lo:hi].astype(jnp.bfloat16), q, 0, 0)
        top = jnp.maximum(jnp.max(s1, 0, keepdims=True), jnp.max(s2, 0, keepdims=True))
        e1 = jnp.exp2((s1 - top) * EXPONENT)
        e2 = jnp.exp2((s2 - top) * EXPONENT)
        total = jnp.sum(e1, 0, keepdims=True) + jnp.sum(e2, 0, keepdims=True)
        out = dot(vn, e1.astype(jnp.bfloat16), 1, 0)
        out += dot(vo[lo:hi].astype(jnp.bfloat16), e2.astype(jnp.bfloat16), 1, 0)
        mixed[lo:hi] = out * (1.0 / total)
    partial = dot(mixed[...].astype(jnp.bfloat16), wo_ref[...], 0, 0)
    p_own[...] = partial[:rows]
    at = rows
    for ref in (p_one_a, p_one_b, p_two_a, p_two_b, p_far_a, p_far_b):
        ref[...] = partial[at : at + half].astype(jnp.bfloat16)
        at += half


def block(parts, mods, w, ko, vo, wo):
    rows, features = parts[0].shape
    half = rows // 2
    count = rows * 4
    width = wo.shape[0]
    piece = jax.ShapeDtypeStruct((half, features), jnp.bfloat16)
    cache = jax.ShapeDtypeStruct((width, count), jnp.bfloat16)
    return pl.pallas_call(
        block_kernel,
        out_shape=[jax.ShapeDtypeStruct((rows, features), jnp.float32)] + [piece] * 6 + [cache] * 2,
        scratch_shapes=[
            pltpu.VMEM((count, features), jnp.bfloat16),
            pltpu.VMEM((3 * width, count), jnp.float32),
            pltpu.VMEM((width, count), jnp.float32),
        ],
        compiler_params=pltpu.CompilerParams(vmem_limit_bytes=40 * 2**20),
        cost_estimate=pl.CostEstimate(
            flops=2 * count * features * width * 4 + 8 * count * count * width,
            bytes_accessed=8 * 2**20,
            transcendentals=8 * count * count,
        ),
    )(*parts, mods, w, ko, vo, wo)


def gathered(rows, by):
    half = rows.shape[0] // 2
    two = exchange(rows, 1, by)
    one = exchange(rows, 0, by)
    own = exchange(rows, None, by) if by else rows
    far_a = exchange(two[:half], 0)
    far_b = exchange(one[half:], 1)
    return own, one, two, far_a, far_b


def summed(own, one_a, one_b, two_a, two_b, far_a, far_b):
    from_one = exchange(far_a, 0)
    from_two = exchange(far_b, 1)
    early_a = exchange(one_a, 0)
    early_b = exchange(two_b, 1)
    late_b = exchange(one_b + from_two, 0)
    late_a = exchange(two_a + from_one, 1)
    others_a = early_a.astype(jnp.float32) + late_a.astype(jnp.float32)
    others_b = early_b.astype(jnp.float32) + late_b.astype(jnp.float32)
    return own + jnp.concatenate([others_a, others_b], axis=0)


def body(patches, qkv_weight, out_weight, modulation, stale_keys, stale_values, offsets):
    width = qkv_weight.shape[3]
    features = qkv_weight.shape[1]
    w = jnp.transpose(qkv_weight[0], (1, 2, 0)).reshape(3 * width, features)
    wo = out_weight[0]
    mods = modulation[0]
    gate = mods[2]
    keys = jnp.transpose(stale_keys[0])
    values = jnp.transpose(stale_values[0])
    count = patches.shape[1] * lax.axis_size("seq")

    def kept(cache, step):
        return lax.dynamic_slice(cache, (0, (1 - offsets[0, step]) * count), (width, count))

    current = patches[0]
    parts = gathered(current, 0)
    ko, vo = kept(keys, 0), kept(values, 0)
    for step in range(TICKS):
        *partial, kn, vn = block(parts, mods, w, ko, vo, wo)
        hidden = parts[0].astype(jnp.float32) + gate * summed(*partial)
        current = hidden.astype(jnp.bfloat16)
        if step + 1 < TICKS:
            same = offsets[0, step] == offsets[0, step + 1]
            ko = jnp.where(same, kept(keys, step + 1), kn)
            vo = jnp.where(same, kept(values, step + 1), vn)
            parts = gathered(current, 1)
    return current[None]


def solution(mesh):
    placed = (
        P("pipe", "seq", None),
        P("pipe", None, None, "seq"),
        P("pipe", "seq", None),
        P("pipe", None, None),
        P("pipe", None, "seq"),
        P("pipe", None, "seq"),
        P("pipe", None),
    )
    return jax.shard_map(
        body, mesh=mesh, in_specs=placed, out_specs=P("pipe", "seq", None), check_vma=False
    )
```

time: 221 us -> 151 us (0.68)
  the two profiles are of different devices: /device:TPU:1 before, /device:TPU:7 now
where the time goes in v1:
time: 151 us; the launch traced here: 150 us
  starting transfers between devices  90.9 us (60%)
  waiting for transfers between devices  32.9 us (22%)
  Pallas kernels  12.6 us (8%)
  local copies, waits for them, and re-layouts  7.5 us (5%)
  other arithmetic  3.3 us (2%)
  between operations  3.01 us (2%)
    ppermute x21, starting transfers between devices, exchange(): return lax.ppermute(array, AXES, moves)  90.9 us
    ppermute x21, waiting for transfers between devices, exchange(): return lax.ppermute(array, AXES, moves)  32.9 us
    pallas_call x2, Pallas kernels, block(): pl.pallas_call(block_kernel, out_shape=[jax.ShapeDtypeStruct((rows, featu...  12.6 us
    unnamed x11, local copies, waits for them, and re-layouts  4.34 us
  transfers between devices with their start and end apart: 21, of which 10 were waited for; matrix products, arithmetic and copies ran while one was open for 4% of the time, Pallas kernels for 0%

profile of v1, /device:TPU:7, one launch (start us, length us, event | category | flops | bytes accessed | tf_op | source)
XLA Modules:
  0.0 150.3 jit_solution(7406806724987880767)
XLA Ops:
  0.0 5.8 %collective-permute-start.1 = (bf16[128,1152]{1,0:T(8,128)(2,1)}, bf16[128,1152]{1,0:T(8,128)(2,1)S(1)}, u32[]{:S(2)}, u32[]{:S(2)}) collective-permute-start(bf16[128,1152]{1,0:T(8,128)(2,1)} %bitcast.32), channel_id=1, source_target_pairs={{3,0},{2,1},{1,2},{0,3},{5,4},{4,5},{7,6},{6,7},{11,8},{10,9},{9,1... | collective-permute-start | bytes 884744 | tf_op jit(solution)/shard_map/ppermute | solution.py:31
  5.8 7.0 %collective-permute-start = (bf16[128,1152]{1,0:T(8,128)(2,1)}, bf16[128,1152]{1,0:T(8,128)(2,1)S(1)}, u32[]{:S(2)}, u32[]{:S(2)}) collective-permute-start(bf16[128,1152]{1,0:T(8,128)(2,1)} %bitcast.33), channel_id=1, source_target_pairs={{1,0},{0,1},{3,2},{2,3},{7,4},{6,5},{5,6},{4,7},{9,8},{8,9},{11,10... | collective-permute-start | bytes 884744 | tf_op jit(solution)/shard_map/ppermute | solution.py:31
  12.8 0.7 collective-permute-done.1.two_ref
  13.6 11.6 %collective-permute-start.2 = (bf16[64,1152]{1,0:T(8,128)(2,1)S(1)}, bf16[64,1152]{1,0:T(8,128)(2,1)S(1)}, u32[]{:S(2)}, u32[]{:S(2)}) collective-permute-start(bf16[64,1152]{1,0:T(8,128)(2,1)S(1)} %slice.33), channel_id=1, source_target_pairs={{1,0},{0,1},{3,2},{2,3},{7,4},{6,5},{5,6},{4,7},{9,8},{8,9},{11,10... | collective-permute-start | bytes 442376 | tf_op jit(solution)/shard_map/ppermute | solution.py:31
  25.2 0.0 collective-permute-done.one_ref
  25.2 4.9 %collective-permute-start.3 = (bf16[64,1152]{1,0:T(8,128)(2,1)S(1)}, bf16[64,1152]{1,0:T(8,128)(2,1)S(1)}, u32[]{:S(2)}, u32[]{:S(2)}) collective-permute-start(bf16[64,1152]{1,0:T(8,128)(2,1)S(1)} %slice.34), channel_id=1, source_target_pairs={{3,0},{2,1},{1,2},{0,3},{5,4},{4,5},{7,6},{6,7},{11,8},{10,9},{9,1... | collective-permute-start | bytes 442376 | tf_op jit(solution)/shard_map/ppermute | solution.py:31
  30.2 1.3 fusion.7
  32.2 0.7 copy.10
  32.9 1.1 dynamic-slice_bitcast_fusion
  34.0 0.0 collective-permute-done.2.far_a_ref
  34.0 2.8 %collective-permute-done.3.far_b_ref = bf16[64,1152]{1,0:T(8,128)(2,1)S(1)} collective-permute-done((bf16[64,1152]{1,0:T(8,128)(2,1)S(1)}, bf16[64,1152]{1,0:T(8,128)(2,1)S(1)}, u32[]{:S(2)}, u32[]{:S(2)}) %collective-permute-start.3) | collective-permute-done | bytes 147488 | tf_op jit(solution)/shard_map/ppermute | solution.py:31
  36.8 0.0 copy-start
  36.8 1.0 copy-done
  37.8 0.0 copy-start.1
  37.8 1.6 %copy-done.1 = bf16[1,1152,3,288]{1,3,2,0:T(8,128)(2,1)S(1)} copy-done((bf16[1,1152,3,288]{1,3,2,0:T(8,128)(2,1)S(1)}, bf16[1,1152,3,288]{1,3,2,0:T(8,128)(2,1)}, u32[]{:S(2)}) %copy-start.1) | copy-done | bytes 1990680
  39.3 0.0 copy-start.3
  39.3 1.1 copy-done.3
  40.4 6.0 %shard_map.73 = (f32[128,1152]{1,0:T(8,128)S(1)}, bf16[64,1152]{1,0:T(8,128)(2,1)S(1)}, bf16[64,1152]{1,0:T(8,128)(2,1)S(1)}, bf16[64,1152]{1,0:T(8,128)(2,1)S(1...) custom-call(bf16[128,1152]{1,0:T(8,128)(2,1)S(1)} %bitcast.34, ...), custom_call_target="tpu_custom_call" | custom-call | flops 1962934272 | bytes 8388608 | tf_op jit(solution)/shard_map/pallas_call | solution.py:94
  46.4 5.3 %collective-permute-start.5 = (bf16[64,1152]{1,0:T(8,128)(2,1)S(1)}, bf16[64,1152]{1,0:T(8,128)(2,1)S(1)}, u32[]{:S(2)}, u32[]{:S(2)}) collective-permute-start(bf16[64,1152]{1,0:T(8,128)(2,1)S(1)} %get-tuple-element.24), channel_id=1, source_target_pairs={{1,0},{0,1},{3,2},{2,3},{7,4},{6,5},{5,6},{4,7},{9,8},{8,9},{11,10... | collective-permute-start | bytes 442376 | tf_op jit(solution)/shard_map/ppermute | solution.py:31
  51.7 1.9 %collective-permute-start.8 = (bf16[64,1152]{1,0:T(8,128)(2,1)S(1)}, bf16[64,1152]{1,0:T(8,128)(2,1)S(1)}, u32[]{:S(2)}, u32[]{:S(2)}) collective-permute-start(bf16[64,1152]{1,0:T(8,128)(2,1)S(1)} %get-tuple-element.27), channel_id=1, source_target_pairs={{3,0},{2,1},{1,2},{0,3},{5,4},{4,5},{7,6},{6,7},{11,8},{10,9},{9,1... | collective-permute-start | bytes 442376 | tf_op jit(solution)/shard_map/ppermute | solution.py:31
  53.6 2.1 %collective-permute-start.4 = (bf16[64,1152]{1,0:T(8,128)(2,1)S(1)}, bf16[64,1152]{1,0:T(8,128)(2,1)S(1)}, u32[]{:S(2)}, u32[]{:S(2)}) collective-permute-start(bf16[64,1152]{1,0:T(8,128)(2,1)S(1)} %get-tuple-element.22), channel_id=1, source_target_pairs={{1,0},{0,1},{3,2},{2,3},{7,4},{6,5},{5,6},{4,7},{9,8},{8,9},{11,10... | collective-permute-start | bytes 442376 | tf_op jit(solution)/shard_map/ppermute | solution.py:31
  55.8 1.0 collective-permute-done.5
  56.8 3.3 %collective-permute-start.6 = (bf16[64,1152]{1,0:T(8,128)(2,1)S(1)}, bf16[64,1152]{1,0:T(8,128)(2,1)S(1)}, u32[]{:S(2)}, u32[]{:S(2)}) collective-permute-start(bf16[64,1152]{1,0:T(8,128)(2,1)S(1)} %add.45), channel_id=1, source_target_pairs={{3,0},{2,1},{1,2},{0,3},{5,4},{4,5},{7,6},{6,7},{11,8},{10,9},{9,1... | collective-permute-start | bytes 442376 | tf_op jit(solution)/shard_map/ppermute | solution.py:31
  60.1 0.7 slice_reduce_fusion
  60.8 2.9 %collective-permute-start.7 = (bf16[64,1152]{1,0:T(8,128)(2,1)S(1)}, bf16[64,1152]{1,0:T(8,128)(2,1)S(1)}, u32[]{:S(2)}, u32[]{:S(2)}) collective-permute-start(bf16[64,1152]{1,0:T(8,128)(2,1)S(1)} %get-tuple-element.25), channel_id=1, source_target_pairs={{3,0},{2,1},{1,2},{0,3},{5,4},{4,5},{7,6},{6,7},{11,8},{10,9},{9,1... | collective-permute-start | bytes 442376 | tf_op jit(solution)/shard_map/ppermute | solution.py:31
  63.7 0.0 collective-permute-done.8
  63.8 4.3 %collective-permute-start.9 = (bf16[64,1152]{1,0:T(8,128)(2,1)S(1)}, bf16[64,1152]{1,0:T(8,128)(2,1)S(1)}, u32[]{:S(2)}, u32[]{:S(2)}) collective-permute-start(bf16[64,1152]{1,0:T(8,128)(2,1)S(1)} %add.47), channel_id=1, source_target_pairs={{1,0},{0,1},{3,2},{2,3},{7,4},{6,5},{5,6},{4,7},{9,8},{8,9},{11,10... | collective-permute-start | bytes 442376 | tf_op jit(solution)/shard_map/ppermute | solution.py:31
  68.1 0.0 collective-permute-done.4
  68.1 0.9 collective-permute-done.6
  69.0 1.6 %collective-permute-done.7 = bf16[64,1152]{1,0:T(8,128)(2,1)S(1)} collective-permute-done((bf16[64,1152]{1,0:T(8,128)(2,1)S(1)}, bf16[64,1152]{1,0:T(8,128)(2,1)S(1)}, u32[]{:S(2)}, u32[]{:S(2)}) %collective-permute-start.7) | collective-permute-done | bytes 147488 | tf_op jit(solution)/shard_map/ppermute | solution.py:31
  70.7 4.3 %collective-permute-done.9 = bf16[64,1152]{1,0:T(8,128)(2,1)S(1)} collective-permute-done((bf16[64,1152]{1,0:T(8,128)(2,1)S(1)}, bf16[64,1152]{1,0:T(8,128)(2,1)S(1)}, u32[]{:S(2)}, u32[]{:S(2)}) %collective-permute-start.9) | collective-permute-done | bytes 147488 | tf_op jit(solution)/shard_map/ppermute | solution.py:31
  75.0 0.0 copy-start.2
  75.0 0.1 fusion.2
  75.1 9.7 %collective-permute-start.12 = (bf16[128,1152]{1,0:T(8,128)(2,1)S(1)}, bf16[128,1152]{1,0:T(8,128)(2,1)S(1)}, u32[]{:S(2)}, u32[]{:S(2)}) collective-permute-start(bf16[128,1152]{1,0:T(8,128)(2,1)S(1)} %fusion.2), channel_id=1, source_target_pairs={{1,4},{0,5},{3,6},{2,7},{7,8},{6,9},{5,10},{4,11},{9,12},{8,13},{1... | collective-permute-start | bytes 884744 | tf_op jit(solution)/shard_map/ppermute | solution.py:31
  84.8 1.9 %collective-permute-start.11 = (bf16[128,1152]{1,0:T(8,128)(2,1)S(1)}, bf16[128,1152]{1,0:T(8,128)(2,1)S(1)}, u32[]{:S(2)}, u32[]{:S(2)}) collective-permute-start(bf16[128,1152]{1,0:T(8,128)(2,1)S(1)} %fusion.2), channel_id=1, source_target_pairs={{3,4},{2,5},{1,6},{0,7},{5,8},{4,9},{7,10},{6,11},{11,12},{10,13},... | collective-permute-start | bytes 884744 | tf_op jit(solution)/shard_map/ppermute | solution.py:31
  88.7 0.0 copy-start.4
  88.7 2.8 %collective-permute-start.10 = (bf16[128,1152]{1,0:T(8,128)(2,1)S(1)}, bf16[128,1152]{1,0:T(8,128)(2,1)S(1)}, u32[]{:S(2)}, u32[]{:S(2)}) collective-permute-start(bf16[128,1152]{1,0:T(8,128)(2,1)S(1)} %fusion.2), channel_id=1, source_target_pairs={{0,4},{1,5},{2,6},{3,7},{4,8},{5,9},{6,10},{7,11},{8,12},{9,13},{1... | collective-permute-start | bytes 884744 | tf_op jit(solution)/shard_map/ppermute | solution.py:31
  91.5 1.1 bitcast_select_fusion.1.ko_ref
  92.6 0.0 collective-permute-done.12.two_ref
  92.6 6.3 %collective-permute-start.13 = (bf16[64,1152]{1,0:T(8,128)(2,1)S(1)}, bf16[64,1152]{1,0:T(8,128)(2,1)S(1)}, u32[]{:S(2)}, u32[]{:S(2)}) collective-permute-start(bf16[64,1152]{1,0:T(8,128)(2,1)S(1)} %slice.35), channel_id=1, source_target_pairs={{1,0},{0,1},{3,2},{2,3},{7,4},{6,5},{5,6},{4,7},{9,8},{8,9},{11,10... | collective-permute-start | bytes 442376 | tf_op jit(solution)/shard_map/ppermute | solution.py:31
  98.9 7.7 %collective-permute-done.11.one_ref = bf16[128,1152]{1,0:T(8,128)(2,1)S(1)} collective-permute-done((bf16[128,1152]{1,0:T(8,128)(2,1)S(1)}, bf16[128,1152]{1,0:T(8,128)(2,1)S(1)}, u32[]{:S(2)}, u32[]{:S(2)}) %collective-permute-start.11) | collective-permute-done | bytes 294944 | tf_op jit(solution)/shard_map/ppermute | solution.py:31
  106.7 2.1 %collective-permute-start.14 = (bf16[64,1152]{1,0:T(8,128)(2,1)S(1)}, bf16[64,1152]{1,0:T(8,128)(2,1)S(1)}, u32[]{:S(2)}, u32[]{:S(2)}) collective-permute-start(bf16[64,1152]{1,0:T(8,128)(2,1)S(1)} %slice.36), channel_id=1, source_target_pairs={{3,0},{2,1},{1,2},{0,3},{5,4},{4,5},{7,6},{6,7},{11,8},{10,9},{9,1... | collective-permute-start | bytes 442376 | tf_op jit(solution)/shard_map/ppermute | solution.py:31
  108.8 1.1 bitcast_select_fusion.vo_ref
  109.8 0.0 collective-permute-done.10.own_ref
  109.8 0.0 collective-permute-done.13.far_a_ref
  109.8 3.6 %collective-permute-done.14.far_b_ref = bf16[64,1152]{1,0:T(8,128)(2,1)S(1)} collective-permute-done((bf16[64,1152]{1,0:T(8,128)(2,1)S(1)}, bf16[64,1152]{1,0:T(8,128)(2,1)S(1)}, u32[]{:S(2)}, u32[]{:S(2)}) %collective-permute-start.14) | collective-permute-done | bytes 147488 | tf_op jit(solution)/shard_map/ppermute | solution.py:31
  113.4 0.0 copy-done.2
  113.4 0.0 copy-done.4
  113.4 6.6 %shard_map.74 = (f32[128,1152]{1,0:T(8,128)S(1)}, bf16[64,1152]{1,0:T(8,128)(2,1)S(1)}, bf16[64,1152]{1,0:T(8,128)(2,1)S(1)}, bf16[64,1152]{1,0:T(8,128)(2,1)S(1...) custom-call(bf16[128,1152]{1,0:T(8,128)(2,1)S(1)} %collective-permut, ...), custom_call_target="tpu_custom_call" | custom-call | flops 1962934272 | bytes 8388608 | tf_op jit(solution)/shard_map/pallas_call | solution.py:94
  120.1 1.9 %collective-permute-start.16 = (bf16[64,1152]{1,0:T(8,128)(2,1)S(1)}, bf16[64,1152]{1,0:T(8,128)(2,1)S(1)}, u32[]{:S(2)}, u32[]{:S(2)}) collective-permute-start(bf16[64,1152]{1,0:T(8,128)(2,1)S(1)} %get-tuple-element.33), channel_id=1, source_target_pairs={{1,0},{0,1},{3,2},{2,3},{7,4},{6,5},{5,6},{4,7},{9,8},{8,9},{11,10... | collective-permute-start | bytes 442376 | tf_op jit(solution)/shard_map/ppermute | solution.py:31
  122.0 3.6 %collective-permute-start.19 = (bf16[64,1152]{1,0:T(8,128)(2,1)S(1)}, bf16[64,1152]{1,0:T(8,128)(2,1)S(1)}, u32[]{:S(2)}, u32[]{:S(2)}) collective-permute-start(bf16[64,1152]{1,0:T(8,128)(2,1)S(1)} %get-tuple-element.36), channel_id=1, source_target_pairs={{3,0},{2,1},{1,2},{0,3},{5,4},{4,5},{7,6},{6,7},{11,8},{10,9},{9,1... | collective-permute-start | bytes 442376 | tf_op jit(solution)/shard_map/ppermute | solution.py:31
  125.5 5.0 %collective-permute-start.15 = (bf16[64,1152]{1,0:T(8,128)(2,1)S(1)}, bf16[64,1152]{1,0:T(8,128)(2,1)S(1)}, u32[]{:S(2)}, u32[]{:S(2)}) collective-permute-start(bf16[64,1152]{1,0:T(8,128)(2,1)S(1)} %get-tuple-element.31), channel_id=1, source_target_pairs={{1,0},{0,1},{3,2},{2,3},{7,4},{6,5},{5,6},{4,7},{9,8},{8,9},{11,10... | collective-permute-start | bytes 442376 | tf_op jit(solution)/shard_map/ppermute | solution.py:31
  130.5 0.0 collective-permute-done.16
  130.6 3.1 %collective-permute-start.17 = (bf16[64,1152]{1,0:T(8,128)(2,1)S(1)}, bf16[64,1152]{1,0:T(8,128)(2,1)S(1)}, u32[]{:S(2)}, u32[]{:S(2)}) collective-permute-start(bf16[64,1152]{1,0:T(8,128)(2,1)S(1)} %add.52), channel_id=1, source_target_pairs={{3,0},{2,1},{1,2},{0,3},{5,4},{4,5},{7,6},{6,7},{11,8},{10,9},{9,1... | collective-permute-start | bytes 442376 | tf_op jit(solution)/shard_map/ppermute | solution.py:31
  133.7 3.1 %collective-permute-start.18 = (bf16[64,1152]{1,0:T(8,128)(2,1)S(1)}, bf16[64,1152]{1,0:T(8,128)(2,1)S(1)}, u32[]{:S(2)}, u32[]{:S(2)}) collective-permute-start(bf16[64,1152]{1,0:T(8,128)(2,1)S(1)} %get-tuple-element.34), channel_id=1, source_target_pairs={{3,0},{2,1},{1,2},{0,3},{5,4},{4,5},{7,6},{6,7},{11,8},{10,9},{9,1... | collective-permute-start | bytes 442376 | tf_op jit(solution)/shard_map/ppermute | solution.py:31
  136.8 0.0 collective-permute-done.19
  136.8 2.4 %collective-permute-start.20 = (bf16[64,1152]{1,0:T(8,128)(2,1)S(1)}, bf16[64,1152]{1,0:T(8,128)(2,1)S(1)}, u32[]{:S(2)}, u32[]{:S(2)}) collective-permute-start(bf16[64,1152]{1,0:T(8,128)(2,1)S(1)} %add.54), channel_id=1, source_target_pairs={{1,0},{0,1},{3,2},{2,3},{7,4},{6,5},{5,6},{4,7},{9,8},{8,9},{11,10... | collective-permute-start | bytes 442376 | tf_op jit(solution)/shard_map/ppermute | solution.py:31
  139.3 0.0 collective-permute-done.15
  139.3 0.0 collective-permute-done.17
  139.3 5.0 %collective-permute-done.18 = bf16[64,1152]{1,0:T(8,128)(2,1)S(1)} collective-permute-done((bf16[64,1152]{1,0:T(8,128)(2,1)S(1)}, bf16[64,1152]{1,0:T(8,128)(2,1)S(1)}, u32[]{:S(2)}, u32[]{:S(2)}) %collective-permute-start.18) | collective-permute-done | bytes 147488 | tf_op jit(solution)/shard_map/ppermute | solution.py:31
  144.3 5.1 %collective-permute-done.20 = bf16[64,1152]{1,0:T(8,128)(2,1)S(1)} collective-permute-done((bf16[64,1152]{1,0:T(8,128)(2,1)S(1)}, bf16[64,1152]{1,0:T(8,128)(2,1)S(1)}, u32[]{:S(2)}, u32[]{:S(2)}) %collective-permute-start.20) | collective-permute-done | bytes 147488 | tf_op jit(solution)/shard_map/ppermute | solution.py:31
  149.5 0.8 fusion.6
  (12 shorter events, 0.3 us)
Async XLA Ops:
  0.0 13.6 %collective-permute-start.1 = (bf16[128,1152]{1,0:T(8,128)(2,1)}, bf16[128,1152]{1,0:T(8,128)(2,1)S(1)}, u32[]{:S(2)}, u32[]{:S(2)}) collective-permute-start(bf16[128,1152]{1,0:T(8,128)(2,1)} %bitcast.32), channel_id=1, source_target_pairs={{3,0},{2,1},{1,2},{0,3},{5,4},{4,5},{7,6},{6,7},{11,8},{10,9},{9,1... | collective-permute-start | bytes 884744 | tf_op jit(solution)/shard_map/ppermute | solution.py:31
  5.8 19.4 %collective-permute-start = (bf16[128,1152]{1,0:T(8,128)(2,1)}, bf16[128,1152]{1,0:T(8,128)(2,1)S(1)}, u32[]{:S(2)}, u32[]{:S(2)}) collective-permute-start(bf16[128,1152]{1,0:T(8,128)(2,1)} %bitcast.33), channel_id=1, source_target_pairs={{1,0},{0,1},{3,2},{2,3},{7,4},{6,5},{5,6},{4,7},{9,8},{8,9},{11,10... | collective-permute-start | bytes 884744 | tf_op jit(solution)/shard_map/ppermute | solution.py:31
  13.6 20.4 %collective-permute-start.2 = (bf16[64,1152]{1,0:T(8,128)(2,1)S(1)}, bf16[64,1152]{1,0:T(8,128)(2,1)S(1)}, u32[]{:S(2)}, u32[]{:S(2)}) collective-permute-start(bf16[64,1152]{1,0:T(8,128)(2,1)S(1)} %slice.33), channel_id=1, source_target_pairs={{1,0},{0,1},{3,2},{2,3},{7,4},{6,5},{5,6},{4,7},{9,8},{8,9},{11,10... | collective-permute-start | bytes 442376 | tf_op jit(solution)/shard_map/ppermute | solution.py:31
  25.2 11.5 %collective-permute-start.3 = (bf16[64,1152]{1,0:T(8,128)(2,1)S(1)}, bf16[64,1152]{1,0:T(8,128)(2,1)S(1)}, u32[]{:S(2)}, u32[]{:S(2)}) collective-permute-start(bf16[64,1152]{1,0:T(8,128)(2,1)S(1)} %slice.34), channel_id=1, source_target_pairs={{3,0},{2,1},{1,2},{0,3},{5,4},{4,5},{7,6},{6,7},{11,8},{10,9},{9,1... | collective-permute-start | bytes 442376 | tf_op jit(solution)/shard_map/ppermute | solution.py:31
  36.8 1.0 copy-start
  37.8 1.6 %copy-start.1 = (bf16[1,1152,3,288]{1,3,2,0:T(8,128)(2,1)S(1)}, bf16[1,1152,3,288]{1,3,2,0:T(8,128)(2,1)}, u32[]{:S(2)}) copy-start(bf16[1,1152,3,288]{1,3,2,0:T(8,128)(2,1)} %param.8) | copy-start | bytes 5971972
  39.3 1.1 copy-start.3
  46.4 10.3 %collective-permute-start.5 = (bf16[64,1152]{1,0:T(8,128)(2,1)S(1)}, bf16[64,1152]{1,0:T(8,128)(2,1)S(1)}, u32[]{:S(2)}, u32[]{:S(2)}) collective-permute-start(bf16[64,1152]{1,0:T(8,128)(2,1)S(1)} %get-tuple-element.24), channel_id=1, source_target_pairs={{1,0},{0,1},{3,2},{2,3},{7,4},{6,5},{5,6},{4,7},{9,8},{8,9},{11,10... | collective-permute-start | bytes 442376 | tf_op jit(solution)/shard_map/ppermute | solution.py:31
  51.7 12.0 %collective-permute-start.8 = (bf16[64,1152]{1,0:T(8,128)(2,1)S(1)}, bf16[64,1152]{1,0:T(8,128)(2,1)S(1)}, u32[]{:S(2)}, u32[]{:S(2)}) collective-permute-start(bf16[64,1152]{1,0:T(8,128)(2,1)S(1)} %get-tuple-element.27), channel_id=1, source_target_pairs={{3,0},{2,1},{1,2},{0,3},{5,4},{4,5},{7,6},{6,7},{11,8},{10,9},{9,1... | collective-permute-start | bytes 442376 | tf_op jit(solution)/shard_map/ppermute | solution.py:31
  53.6 14.4 %collective-permute-start.4 = (bf16[64,1152]{1,0:T(8,128)(2,1)S(1)}, bf16[64,1152]{1,0:T(8,128)(2,1)S(1)}, u32[]{:S(2)}, u32[]{:S(2)}) collective-permute-start(bf16[64,1152]{1,0:T(8,128)(2,1)S(1)} %get-tuple-element.22), channel_id=1, source_target_pairs={{1,0},{0,1},{3,2},{2,3},{7,4},{6,5},{5,6},{4,7},{9,8},{8,9},{11,10... | collective-permute-start | bytes 442376 | tf_op jit(solution)/shard_map/ppermute | solution.py:31
  56.8 12.2 %collective-permute-start.6 = (bf16[64,1152]{1,0:T(8,128)(2,1)S(1)}, bf16[64,1152]{1,0:T(8,128)(2,1)S(1)}, u32[]{:S(2)}, u32[]{:S(2)}) collective-permute-start(bf16[64,1152]{1,0:T(8,128)(2,1)S(1)} %add.45), channel_id=1, source_target_pairs={{3,0},{2,1},{1,2},{0,3},{5,4},{4,5},{7,6},{6,7},{11,8},{10,9},{9,1... | collective-permute-start | bytes 442376 | tf_op jit(solution)/shard_map/ppermute | solution.py:31
  60.8 9.9 %collective-permute-start.7 = (bf16[64,1152]{1,0:T(8,128)(2,1)S(1)}, bf16[64,1152]{1,0:T(8,128)(2,1)S(1)}, u32[]{:S(2)}, u32[]{:S(2)}) collective-permute-start(bf16[64,1152]{1,0:T(8,128)(2,1)S(1)} %get-tuple-element.25), channel_id=1, source_target_pairs={{3,0},{2,1},{1,2},{0,3},{5,4},{4,5},{7,6},{6,7},{11,8},{10,9},{9,1... | collective-permute-start | bytes 442376 | tf_op jit(solution)/shard_map/ppermute | solution.py:31
  63.8 11.2 %collective-permute-start.9 = (bf16[64,1152]{1,0:T(8,128)(2,1)S(1)}, bf16[64,1152]{1,0:T(8,128)(2,1)S(1)}, u32[]{:S(2)}, u32[]{:S(2)}) collective-permute-start(bf16[64,1152]{1,0:T(8,128)(2,1)S(1)} %add.47), channel_id=1, source_target_pairs={{1,0},{0,1},{3,2},{2,3},{7,4},{6,5},{5,6},{4,7},{9,8},{8,9},{11,10... | collective-permute-start | bytes 442376 | tf_op jit(solution)/shard_map/ppermute | solution.py:31
  75.0 38.4 %copy-start.2 = (bf16[1,1152,3,288]{1,3,2,0:T(8,128)(2,1)S(1)}, bf16[1,1152,3,288]{1,3,2,0:T(8,128)(2,1)}, u32[]{:S(2)}) copy-start(bf16[1,1152,3,288]{1,3,2,0:T(8,128)(2,1)} %param.8) | copy-start | bytes 5971972
  75.1 17.5 %collective-permute-start.12 = (bf16[128,1152]{1,0:T(8,128)(2,1)S(1)}, bf16[128,1152]{1,0:T(8,128)(2,1)S(1)}, u32[]{:S(2)}, u32[]{:S(2)}) collective-permute-start(bf16[128,1152]{1,0:T(8,128)(2,1)S(1)} %fusion.2), channel_id=1, source_target_pairs={{1,4},{0,5},{3,6},{2,7},{7,8},{6,9},{5,10},{4,11},{9,12},{8,13},{1... | collective-permute-start | bytes 884744 | tf_op jit(solution)/shard_map/ppermute | solution.py:31
  84.8 21.8 %collective-permute-start.11 = (bf16[128,1152]{1,0:T(8,128)(2,1)S(1)}, bf16[128,1152]{1,0:T(8,128)(2,1)S(1)}, u32[]{:S(2)}, u32[]{:S(2)}) collective-permute-start(bf16[128,1152]{1,0:T(8,128)(2,1)S(1)} %fusion.2), channel_id=1, source_target_pairs={{3,4},{2,5},{1,6},{0,7},{5,8},{4,9},{7,10},{6,11},{11,12},{10,13},... | collective-permute-start | bytes 884744 | tf_op jit(solution)/shard_map/ppermute | solution.py:31
  88.7 24.7 %copy-start.4 = (bf16[1,288,1152]{2,1,0:T(8,128)(2,1)S(1)}, bf16[1,288,1152]{2,1,0:T(8,128)(2,1)}, u32[]{:S(2)}) copy-start(bf16[1,288,1152]{2,1,0:T(8,128)(2,1)} %param.9) | copy-start | bytes 1990660
  88.7 21.1 %collective-permute-start.10 = (bf16[128,1152]{1,0:T(8,128)(2,1)S(1)}, bf16[128,1152]{1,0:T(8,128)(2,1)S(1)}, u32[]{:S(2)}, u32[]{:S(2)}) collective-permute-start(bf16[128,1152]{1,0:T(8,128)(2,1)S(1)} %fusion.2), channel_id=1, source_target_pairs={{0,4},{1,5},{2,6},{3,7},{4,8},{5,9},{6,10},{7,11},{8,12},{9,13},{1... | collective-permute-start | bytes 884744 | tf_op jit(solution)/shard_map/ppermute | solution.py:31
  92.6 17.2 %collective-permute-start.13 = (bf16[64,1152]{1,0:T(8,128)(2,1)S(1)}, bf16[64,1152]{1,0:T(8,128)(2,1)S(1)}, u32[]{:S(2)}, u32[]{:S(2)}) collective-permute-start(bf16[64,1152]{1,0:T(8,128)(2,1)S(1)} %slice.35), channel_id=1, source_target_pairs={{1,0},{0,1},{3,2},{2,3},{7,4},{6,5},{5,6},{4,7},{9,8},{8,9},{11,10... | collective-permute-start | bytes 442376 | tf_op jit(solution)/shard_map/ppermute | solution.py:31
  106.7 6.8 %collective-permute-start.14 = (bf16[64,1152]{1,0:T(8,128)(2,1)S(1)}, bf16[64,1152]{1,0:T(8,128)(2,1)S(1)}, u32[]{:S(2)}, u32[]{:S(2)}) collective-permute-start(bf16[64,1152]{1,0:T(8,128)(2,1)S(1)} %slice.36), channel_id=1, source_target_pairs={{3,0},{2,1},{1,2},{0,3},{5,4},{4,5},{7,6},{6,7},{11,8},{10,9},{9,1... | collective-permute-start | bytes 442376 | tf_op jit(solution)/shard_map/ppermute | solution.py:31
  120.1 10.5 %collective-permute-start.16 = (bf16[64,1152]{1,0:T(8,128)(2,1)S(1)}, bf16[64,1152]{1,0:T(8,128)(2,1)S(1)}, u32[]{:S(2)}, u32[]{:S(2)}) collective-permute-start(bf16[64,1152]{1,0:T(8,128)(2,1)S(1)} %get-tuple-element.33), channel_id=1, source_target_pairs={{1,0},{0,1},{3,2},{2,3},{7,4},{6,5},{5,6},{4,7},{9,8},{8,9},{11,10... | collective-permute-start | bytes 442376 | tf_op jit(solution)/shard_map/ppermute | solution.py:31
  122.0 14.8 %collective-permute-start.19 = (bf16[64,1152]{1,0:T(8,128)(2,1)S(1)}, bf16[64,1152]{1,0:T(8,128)(2,1)S(1)}, u32[]{:S(2)}, u32[]{:S(2)}) collective-permute-start(bf16[64,1152]{1,0:T(8,128)(2,1)S(1)} %get-tuple-element.36), channel_id=1, source_target_pairs={{3,0},{2,1},{1,2},{0,3},{5,4},{4,5},{7,6},{6,7},{11,8},{10,9},{9,1... | collective-permute-start | bytes 442376 | tf_op jit(solution)/shard_map/ppermute | solution.py:31
  125.5 13.7 %collective-permute-start.15 = (bf16[64,1152]{1,0:T(8,128)(2,1)S(1)}, bf16[64,1152]{1,0:T(8,128)(2,1)S(1)}, u32[]{:S(2)}, u32[]{:S(2)}) collective-permute-start(bf16[64,1152]{1,0:T(8,128)(2,1)S(1)} %get-tuple-element.31), channel_id=1, source_target_pairs={{1,0},{0,1},{3,2},{2,3},{7,4},{6,5},{5,6},{4,7},{9,8},{8,9},{11,10... | collective-permute-start | bytes 442376 | tf_op jit(solution)/shard_map/ppermute | solution.py:31
  130.6 8.7 %collective-permute-start.17 = (bf16[64,1152]{1,0:T(8,128)(2,1)S(1)}, bf16[64,1152]{1,0:T(8,128)(2,1)S(1)}, u32[]{:S(2)}, u32[]{:S(2)}) collective-permute-start(bf16[64,1152]{1,0:T(8,128)(2,1)S(1)} %add.52), channel_id=1, source_target_pairs={{3,0},{2,1},{1,2},{0,3},{5,4},{4,5},{7,6},{6,7},{11,8},{10,9},{9,1... | collective-permute-start | bytes 442376 | tf_op jit(solution)/shard_map/ppermute | solution.py:31
  133.7 10.6 %collective-permute-start.18 = (bf16[64,1152]{1,0:T(8,128)(2,1)S(1)}, bf16[64,1152]{1,0:T(8,128)(2,1)S(1)}, u32[]{:S(2)}, u32[]{:S(2)}) collective-permute-start(bf16[64,1152]{1,0:T(8,128)(2,1)S(1)} %get-tuple-element.34), channel_id=1, source_target_pairs={{3,0},{2,1},{1,2},{0,3},{5,4},{4,5},{7,6},{6,7},{11,8},{10,9},{9,1... | collective-permute-start | bytes 442376 | tf_op jit(solution)/shard_map/ppermute | solution.py:31
  136.8 12.6 %collective-permute-start.20 = (bf16[64,1152]{1,0:T(8,128)(2,1)S(1)}, bf16[64,1152]{1,0:T(8,128)(2,1)S(1)}, u32[]{:S(2)}, u32[]{:S(2)}) collective-permute-start(bf16[64,1152]{1,0:T(8,128)(2,1)S(1)} %add.54), channel_id=1, source_target_pairs={{1,0},{0,1},{3,2},{2,3},{7,4},{6,5},{5,6},{4,7},{9,8},{8,9},{11,10... | collective-permute-start | bytes 442376 | tf_op jit(solution)/shard_map/ppermute | solution.py:31

commit v2 on v0

v2 whole, which is shorter than its diff:
```python
import functools
import math

import jax
import jax.numpy as jnp
from jax import lax
from jax.experimental import pallas as pl
from jax.experimental.pallas import tpu as pltpu
from jax.sharding import PartitionSpec as P

HEAD_DIM = 72
AXES = ("pipe", "seq")
VMEM_BYTES = 24 * 2**20
EXPONENT = math.log2(math.e) / math.sqrt(HEAD_DIM)


def partner(kind, section, member):
    if kind == 2:
        return member ^ 2
    if (kind + section) % 2 == 0:
        return member ^ 1
    return 3 - member


def exchange(array, kind):
    sections, members = lax.axis_size("pipe"), lax.axis_size("seq")
    moves = []
    for section in range(sections):
        for member in range(members):
            moves.append((section * members + partner(kind, section, member), section * members + member))
    return lax.ppermute(array, AXES, moves)


def advance(array, kind):
    sections, members = lax.axis_size("pipe"), lax.axis_size("seq")
    moves = []
    for section in range(sections):
        target = (section + 1) % sections
        for member in range(members):
            place = member if kind is None else partner(kind, section, member)
            moves.append((section * members + member, target * members + place))
    return lax.ppermute(array, AXES, moves)


def dot(a, b, contract_a, contract_b):
    return lax.dot_general(
        a, b, (((contract_a,), (contract_b,)), ((), ())), preferred_element_type=jnp.float32
    )


def normalize(rows, shift, scale):
    values = rows.astype(jnp.float32)
    center = jnp.mean(values, axis=-1, keepdims=True)
    values = values - center
    spread = jnp.mean(values * values, axis=-1, keepdims=True)
    return (values * lax.rsqrt(spread + 1e-06) * (1.0 + scale) + shift).astype(jnp.bfloat16)


def weighted(queries, caches, prior=None):
    scores = [dot(keys, queries, 0, 0) for keys, _ in caches]
    top = functools.reduce(jnp.maximum, [jnp.max(s, 0, keepdims=True) for s in scores])
    total = out = 0.0
    if prior is not None:
        top = jnp.maximum(top, prior[0])
        shrink = jnp.exp2((prior[0] - top) * EXPONENT)
        total, out = prior[1] * shrink, prior[2] * shrink
    for s, (_, values) in zip(scores, caches, strict=True):
        weights = jnp.exp2((s - top) * EXPONENT)
        total = total + jnp.sum(weights, 0, keepdims=True)
        out = out + dot(values, weights.astype(jnp.bfloat16), 1, 0)
    return top, total, out


def head_of(ref_or_array, h):
    return ref_or_array[h * HEAD_DIM : (h + 1) * HEAD_DIM]


def project_qkv(parts, mods_ref, w_ref, normed, qkv):
    at = 0
    for ref in parts:
        normed[at : at + ref.shape[0]] = normalize(ref[...], mods_ref[0:1], mods_ref[1:2])
        at += ref.shape[0]
    qkv[...] = dot(w_ref[...], normed[...], 1, 1)


def early_kernel(step, n_parts, *refs):
    parts, refs = refs[:n_parts], refs[n_parts:]
    n_olds = 4 if step else 0
    olds, refs = refs[:n_olds], refs[n_olds:]
    (offsets_ref, mods_ref, w_ref, stale_k_ref, stale_v_ref,
     q_ref, k_ref, v_ref, ko_ref, vo_ref, top_ref, total_ref, out_ref, normed, qkv) = refs
    width, count = ko_ref.shape
    start = pl.multiple_of((1 - offsets_ref[step]) * count, count)
    ko_ref[...] = stale_k_ref[:, pl.ds(start, count)]
    vo_ref[...] = stale_v_ref[:, pl.ds(start, count)]
    if step:
        @pl.when(offsets_ref[0] != offsets_ref[step])
        def _():
            split = olds[0].shape[1]
            ko_ref[:, :split] = olds[0][...]
            ko_ref[:, split:] = olds[1][...]
            vo_ref[:, :split] = olds[2][...]
            vo_ref[:, split:] = olds[3][...]

    project_qkv(parts, mods_ref, w_ref, normed, qkv)
    q_ref[...] = qkv[:width].astype(jnp.bfloat16)
    k_ref[...] = qkv[width : 2 * width].astype(jnp.bfloat16)
    v_ref[...] = qkv[2 * width :].astype(jnp.bfloat16)
    ko = ko_ref[...].astype(jnp.float32)
    vo = vo_ref[...].astype(jnp.float32)
    for h in range(width // HEAD_DIM):
        lo, hi = h * HEAD_DIM, (h + 1) * HEAD_DIM
        top, total, out = weighted(
            qkv[lo:hi].astype(jnp.bfloat16),
            [
                (qkv[width + lo : width + hi].astype(jnp.bfloat16), qkv[2 * width + lo : 2 * width + hi].astype(jnp.bfloat16)),
                (ko[lo:hi].astype(jnp.bfloat16), vo[lo:hi].astype(jnp.bfloat16)),
            ],
        )
        top_ref[h : h + 1] = top
        total_ref[h : h + 1] = total
        out_ref[lo:hi] = out


def early(step, parts, olds, offsets, mods, w, stale_k, stale_v):
    rows = sum(part.shape[0] for part in parts)
    features = parts[0].shape[1]
    width, count = stale_k.shape[0], stale_k.shape[1] // 2
    narrow = jax.ShapeDtypeStruct((width, rows), jnp.bfloat16)
    half = jax.ShapeDtypeStruct((width, count), jnp.bfloat16)
    stat = jax.ShapeDtypeStruct((8, rows), jnp.float32)
    vmem = pl.BlockSpec(memory_space=pltpu.VMEM)
    return pl.pallas_call(
        functools.partial(early_kernel, step, len(parts)),
        out_shape=[narrow, narrow, narrow, half, half, stat, stat, jax.ShapeDtypeStruct((width, rows), jnp.float32)],
        in_specs=[vmem] * (len(parts) + len(olds)) + [pl.BlockSpec(memory_space=pltpu.SMEM)] + [vmem] * 4,
        scratch_shapes=[pltpu.VMEM((rows, features), jnp.bfloat16), pltpu.VMEM((3 * width, rows), jnp.float32)],
        compiler_params=pltpu.CompilerParams(vmem_limit_bytes=VMEM_BYTES),
        cost_estimate=pl.CostEstimate(
            flops=2 * rows * features * width * 3 + 4 * rows * (rows + count) * width,
            bytes_accessed=4 * 2**20,
            transcendentals=4 * rows * (rows + count),
        ),
    )(*parts, *olds, offsets, mods, w, stale_k, stale_v)


def merge_heads(target, pieces, early_refs, late, ko_ref, vo_ref):
    q_ref, k_ref, v_ref, top_ref, total_ref, out_ref = early_refs
    width = k_ref.shape[0]
    f32 = [ref[...].astype(jnp.float32) for ref in (q_ref, k_ref, v_ref, ko_ref, vo_ref)]
    for h in range(width // HEAD_DIM):
        qe, ke, ve, ko, vo = (head_of(a, h).astype(jnp.bfloat16) for a in f32)
        ql, kl, vl = (head_of(a, h).astype(jnp.bfloat16) for a in late)
        at = 0
        for is_early, first, last in pieces:
            if is_early:
                prior = (
                    top_ref[h : h + 1, first:last],
                    total_ref[h : h + 1, first:last],
                    out_ref[h * HEAD_DIM : (h + 1) * HEAD_DIM, first:last],
                )
                _, total, out = weighted(qe[:, first:last], [(kl, vl)], prior)
            else:
                _, total, out = weighted(ql[:, first:last], [(ke, ve), (ko, vo), (kl, vl)])
            target[h * HEAD_DIM : (h + 1) * HEAD_DIM, at : at + last - first] = out * (1.0 / total)
            at += last - first


def late_kernel(n_parts, pieces, *refs):
    parts, refs = refs[:n_parts], refs[n_parts:]
    mods_ref, w_ref, ko_ref, vo_ref, *early_refs = refs[:10]
    sent_ref, q_ref, k_ref, v_ref, normed, qkv, mixed = refs[10:]
    width = ko_ref.shape[0]
    project_qkv(parts, mods_ref, w_ref, normed, qkv)
    q_ref[...] = qkv[:width].astype(jnp.bfloat16)
    k_ref[...] = qkv[width : 2 * width].astype(jnp.bfloat16)
    v_ref[...] = qkv[2 * width :].astype(jnp.bfloat16)
    merge_heads(mixed, pieces, early_refs, (qkv[:width], qkv[width : 2 * width], qkv[2 * width :]), ko_ref, vo_ref)
    sent_ref[...] = mixed[...].astype(jnp.bfloat16)


def work(pieces, count, width):
    return 4 * sum(last - first for _, first, last in pieces) * count * width


def late(parts, pieces, mods, w, ko, vo, early_state):
    rows = sum(part.shape[0] for part in parts)
    features = parts[0].shape[1]
    width, count = ko.shape
    columns = sum(last - first for _, first, last in pieces)
    narrow = jax.ShapeDtypeStruct((width, rows), jnp.bfloat16)
    return pl.pallas_call(
        functools.partial(late_kernel, len(parts), pieces),
        out_shape=[jax.ShapeDtypeStruct((width, columns), jnp.bfloat16), narrow, narrow, narrow],
        scratch_shapes=[
            pltpu.VMEM((rows, features), jnp.bfloat16),
            pltpu.VMEM((3 * width, rows), jnp.float32),
            pltpu.VMEM((width, columns), jnp.float32),
        ],
        compiler_params=pltpu.CompilerParams(vmem_limit_bytes=VMEM_BYTES),
        cost_estimate=pl.CostEstimate(
            flops=2 * rows * features * width * 3 + work(pieces, count, width),
            bytes_accessed=4 * 2**20,
            transcendentals=4 * columns * count,
        ),
    )(*parts, mods, w, ko, vo, *early_state)


def rest_kernel(pieces, *refs):
    ko_ref, vo_ref, *early_refs = refs[:8]
    ql_ref, kl_ref, vl_ref, kept_ref, mixed = refs[8:]
    late_arrays = [ref[...].astype(jnp.float32) for ref in (ql_ref, kl_ref, vl_ref)]
    merge_heads(mixed, pieces, early_refs, late_arrays, ko_ref, vo_ref)
    kept_ref[...] = mixed[...].astype(jnp.bfloat16)


def rest(pieces, ko, vo, early_state, late_state):
    width, count = ko.shape
    columns = sum(last - first for _, first, last in pieces)
    return pl.pallas_call(
        functools.partial(rest_kernel, pieces),
        out_shape=jax.ShapeDtypeStruct((width, columns), jnp.bfloat16),
        scratch_shapes=[pltpu.VMEM((width, columns), jnp.float32)],
        compiler_params=pltpu.CompilerParams(vmem_limit_bytes=VMEM_BYTES),
        cost_estimate=pl.CostEstimate(
            flops=work(pieces, count, width), bytes_accessed=3 * 2**20, transcendentals=4 * columns * count
        ),
    )(ko, vo, *early_state, *late_state)


def project_kernel(mine_ref, theirs_ref, w_mine_ref, w_theirs_ref, *out_refs):
    total = dot(mine_ref[...], w_mine_ref[...], 0, 0) + dot(theirs_ref[...], w_theirs_ref[...], 0, 0)
    rows = out_refs[0].shape[0]
    for i, ref in enumerate(out_refs):
        ref[...] = total[i * rows : (i + 1) * rows].astype(jnp.bfloat16)


def project(mine, theirs, w_mine, w_theirs):
    rows, features, width = mine.shape[1], w_mine.shape[1], mine.shape[0]
    return pl.pallas_call(
        project_kernel,
        out_shape=[jax.ShapeDtypeStruct((rows // 2, features), jnp.bfloat16)] * 2,
        compiler_params=pltpu.CompilerParams(vmem_limit_bytes=VMEM_BYTES),
        cost_estimate=pl.CostEstimate(
            flops=4 * rows * features * width, bytes_accessed=3 * 2**20, transcendentals=0
        ),
    )(mine, theirs, w_mine, w_theirs)


def update_kernel(hidden_ref, mods_ref, mine_ref, theirs_ref, out_ref):
    attended = mine_ref[...].astype(jnp.float32) + theirs_ref[...].astype(jnp.float32)
    out_ref[...] = (hidden_ref[...].astype(jnp.float32) + mods_ref[2:3] * attended).astype(jnp.bfloat16)


def update(hidden, mods, mine, theirs):
    return pl.pallas_call(
        update_kernel,
        out_shape=jax.ShapeDtypeStruct(hidden.shape, jnp.bfloat16),
        compiler_params=pltpu.CompilerParams(vmem_limit_bytes=VMEM_BYTES),
        cost_estimate=pl.CostEstimate(flops=4 * hidden.size, bytes_accessed=8 * hidden.size, transcendentals=0),
    )(hidden, mods, mine, theirs)


def body(patches, qkv_weight, out_weight, modulation, stale_keys, stale_values, offsets):
    width = qkv_weight.shape[3]
    features = qkv_weight.shape[1]
    w = jnp.transpose(qkv_weight[0], (1, 2, 0)).reshape(3 * width, features)
    w_mine = out_weight[0]
    mods = modulation[0]
    stale = (jnp.transpose(stale_keys[0]), jnp.transpose(stale_values[0]))
    slots = offsets[0]
    own = patches[0]
    rows = own.shape[0]

    with jax.named_scope("first_gather"):
        zero = exchange(own, 0)
        one = exchange(own, 1)
        far = exchange(zero, 1)
    w_sent, zero, one = lax.optimization_barrier((w_mine, zero, one))
    with jax.named_scope("first_tick"):
        q, k, v, ko, vo, *stats = early(0, (zero, own, one), (), slots, mods, w, *stale)
        w_theirs = exchange(w_sent, 0)
        state = (q, k, v, *stats)
        sent, *late_state = late((far,), ((True, 0, rows), (False, 0, rows)), mods, w, ko, vo, state)
        theirs = exchange(sent, 0)
        kept = rest(((True, rows, 3 * rows),), ko, vo, state, late_state)
        mine_own, mine_one = project(kept, theirs, w_mine, w_theirs)
        olds = (k, late_state[1], v, late_state[2])
    with jax.named_scope("sum_and_shift"):
        next_one = update(one, mods, mine_one, exchange(mine_own, 1))
        next_own = update(own, mods, mine_own, exchange(mine_one, 1))
        straight_one, crossing_one = advance(next_one, None), advance(next_one, 0)
        straight_own, crossing_own = advance(next_own, None), advance(next_own, 0)
    with jax.named_scope("second_tick"):
        q, k, v, ko, vo, *stats = early(1, (straight_one, crossing_one), olds, slots, mods, w, *stale)
        state = (q, k, v, *stats)
        sent, *late_state = late((straight_own, crossing_own), ((True, 0, 2 * rows),), mods, w, ko, vo, state)
        theirs = exchange(sent, 0)
        kept = rest(((False, 0, 2 * rows),), ko, vo, state, late_state)
        mine_own, mine_one = project(kept, theirs, w_mine, w_theirs)
        return update(straight_own, mods, mine_own, exchange(mine_one, 1))[None]


def solution(mesh):
    placed = (
        P("pipe", "seq", None),
        P("pipe", None, None, "seq"),
        P("pipe", "seq", None),
        P("pipe", None, None),
        P("pipe", None, "seq"),
        P("pipe", None, "seq"),
        P("pipe", None),
    )
    return jax.shard_map(
        body, mesh=mesh, in_specs=placed, out_specs=P("pipe", "seq", None), check_vma=False
    )
```

time: 221 us -> 138 us (0.62)
  the two profiles are of different devices: /device:TPU:1 before, /device:TPU:6 now
where the time goes in v2:
time: 138 us
  waiting for transfers between devices  58.5 us (42%)
  starting transfers between devices  51.5 us (37%)
  Pallas kernels  21.4 us (16%)
  local copies, waits for them, and re-layouts  6.05 us (4%)
    ppermute x9, waiting for transfers between devices, exchange(): return lax.ppermute(array, AXES, moves)  54 us
    ppermute x9, starting transfers between devices, exchange(): return lax.ppermute(array, AXES, moves)  39.7 us
    ppermute x4, starting transfers between devices, advance(): return lax.ppermute(array, AXES, moves)  11.9 us
    pallas_call x2, Pallas kernels, early(): pl.pallas_call(functools.partial(early_kernel, step, len(parts)), out_sha...  9.44 us
    unnamed x23, local copies, waits for them, and re-layouts  6.05 us
    pallas_call x2, Pallas kernels, late(): pl.pallas_call(functools.partial(late_kernel, len(parts), pieces), out_sh...  6 us
    ppermute x4, waiting for transfers between devices, advance(): return lax.ppermute(array, AXES, moves)  4.54 us
    pallas_call x2, Pallas kernels, rest(): pl.pallas_call(functools.partial(rest_kernel, pieces), out_shape=jax.Shap...  3.11 us
  transfers between devices with their start and end apart: 13, of which 9 were waited for; matrix products, arithmetic and copies ran while one was open for 1% of the time, Pallas kernels for 12%

profile of v2, /device:TPU:6, one launch (start us, length us, event | category | flops | bytes accessed | tf_op | source)
XLA Modules:
  0.0 137.7 jit_solution(13679157290148374314)
XLA Ops:
  0.0 10.9 %collective-permute-start.1 = (bf16[128,1152]{1,0:T(8,128)(2,1)}, bf16[128,1152]{1,0:T(8,128)(2,1)S(1)}, u32[]{:S(2)}, u32[]{:S(2)}) collective-permute-start(bf16[128,1152]{1,0:T(8,128)(2,1)} %bitcast.36), channel_id=1, source_target_pairs={{3,0},{2,1},{1,2},{0,3},{5,4},{4,5},{7,6},{6,7},{11,8},{10,9},{9,1... | collective-permute-start | bytes 884744 | tf_op jit(solution)/shard_map/first_gather/ppermute | solution.py:31
  10.9 2.5 %collective-permute-start = (bf16[128,1152]{1,0:T(8,128)(2,1)}, bf16[128,1152]{1,0:T(8,128)(2,1)S(1)}, u32[]{:S(2)}, u32[]{:S(2)}) collective-permute-start(bf16[128,1152]{1,0:T(8,128)(2,1)} %bitcast.37), channel_id=1, source_target_pairs={{1,0},{0,1},{3,2},{2,3},{7,4},{6,5},{5,6},{4,7},{9,8},{8,9},{11,10... | collective-permute-start | bytes 884744 | tf_op jit(solution)/shard_map/first_gather/ppermute | solution.py:31
  13.4 10.4 %collective-permute-done.1.refs_2_.hidden_ref = bf16[128,1152]{1,0:T(8,128)(2,1)S(1)} collective-permute-done((bf16[128,1152]{1,0:T(8,128)(2,1)}, bf16[128,1152]{1,0:T(8,128)(2,1)S(1)}, u32[]{:S(2)}, u32[]{:S(2)}) %collective-permute-start.1) | collective-permute-done | bytes 294944 | tf_op jit(solution)/shard_map/first_gather/ppermute | solution.py:31
  23.8 0.0 collective-permute-done.refs_0_
  23.8 2.1 %collective-permute-start.4 = (bf16[288,1152]{1,0:T(8,128)(2,1)}, bf16[288,1152]{1,0:T(8,128)(2,1)S(1)}, u32[]{:S(2)}, u32[]{:S(2)}) collective-permute-start(bf16[288,1152]{1,0:T(8,128)(2,1)} %bitcast.22), channel_id=1, source_target_pairs={{1,0},{0,1},{3,2},{2,3},{7,4},{6,5},{5,6},{4,7},{9,8},{8,9},{11,10... | collective-permute-start | bytes 1990664 | tf_op jit(solution)/shard_map/first_tick/ppermute | solution.py:31
  25.9 6.4 %collective-permute-start.2 = (bf16[128,1152]{1,0:T(8,128)(2,1)S(1)}, bf16[128,1152]{1,0:T(8,128)(2,1)S(1)}, u32[]{:S(2)}, u32[]{:S(2)}) collective-permute-start(bf16[128,1152]{1,0:T(8,128)(2,1)S(1)} %collective-permute-done.refs_0_), channel_id=1, source_target_pairs={{3,0},{2,1},{1,2},{0,3},{5,4},{4,5},{7,6},{6,7},{11,8},{10,9},{9,1... | collective-permute-start | bytes 884744 | tf_op jit(solution)/shard_map/first_gather/ppermute | solution.py:31
  32.3 0.7 copy.10
  33.0 0.0 copy-start
  33.0 1.6 %copy-done = bf16[1,1152,3,288]{1,3,2,0:T(8,128)(2,1)S(1)} copy-done((bf16[1,1152,3,288]{1,3,2,0:T(8,128)(2,1)S(1)}, bf16[1,1152,3,288]{1,3,2,0:T(8,128)(2,1)}, u32[]{:S(2)}) %copy-start) | copy-done | bytes 1990680
  34.5 0.0 copy-start.3
  34.5 1.1 copy-done.3
  35.6 0.0 copy-start.5
  35.6 1.1 copy-done.5
  36.7 0.0 copy-start.7
  36.7 1.0 copy-done.7
  37.6 0.0 copy-start.9
  37.6 0.7 copy-done.9
  38.3 0.0 copy-start.1
  38.3 4.8 %first_tick.4 = (bf16[288,384]{1,0:T(8,128)(2,1)S(1)}, bf16[288,384]{1,0:T(8,128)(2,1)S(1)}, bf16[288,384]{1,0:T(8,128)(2,1)S(1)}, bf16[288,512]{1,0:T(8,128)(2,...) custom-call(bf16[128,1152]{1,0:T(8,128)(2,1)S(1)} %collective-permut, ...), custom_call_target="tpu_custom_call" | custom-call | flops 1160773632 | bytes 4194304 | tf_op jit(solution)/shard_map/first_tick/pallas_call | solution.py:133
  43.1 5.8 %collective-permute-done.2.refs_0_ = bf16[128,1152]{1,0:T(8,128)(2,1)S(1)} collective-permute-done((bf16[128,1152]{1,0:T(8,128)(2,1)S(1)}, bf16[128,1152]{1,0:T(8,128)(2,1)S(1)}, u32[]{:S(2)}, u32[]{:S(2)}) %collective-permute-start.2) | collective-permute-done | bytes 294944 | tf_op jit(solution)/shard_map/first_gather/ppermute | solution.py:31
  48.9 0.0 copy-done.1
  48.9 3.6 %first_tick.5 = (bf16[288,256]{1,0:T(8,128)(2,1)S(1)}, bf16[288,128]{1,0:T(8,128)(2,1)S(1)}, bf16[288,128]{1,0:T(8,128)(2,1)S(1)}, bf16[288,128]{1,0:T(8,128)(2,1)S(1)}) custom-call(bf16[128,1152]{1,0:T(8,128)(2,1)S(1)} %collective-permute-done.2.refs_0_, f32[3,1152]{1,0:T(4,128)S(1)} %bitcast.26, bf16[864,1152]{1,0:T(8,128)(2,1)S(1)} %bitcast.19, ...), custom_call_target="tpu_custom_call" | custom-call | flops 405798912 | bytes 4194304 | tf_op jit(solution)/shard_map/first_tick/pallas_call | solution.py:192
  52.5 0.0 copy-start.2
  52.5 4.4 %collective-permute-start.3 = (bf16[288,256]{1,0:T(8,128)(2,1)S(1)}, bf16[288,256]{1,0:T(8,128)(2,1)S(1)}, u32[]{:S(2)}, u32[]{:S(2)}) collective-permute-start(bf16[288,256]{1,0:T(8,128)(2,1)S(1)} %get-tuple-element.49), channel_id=1, source_target_pairs={{1,0},{0,1},{3,2},{2,3},{7,4},{6,5},{5,6},{4,7},{9,8},{8,9},{11,10... | collective-permute-start | bytes 442376 | tf_op jit(solution)/shard_map/first_tick/ppermute | solution.py:31
  57.0 0.0 copy-start.8
  57.0 1.0 first_tick.6.mine_ref
  58.0 0.0 copy-start.4
  58.0 0.0 copy-start.6
  58.0 0.0 copy-start.10
  58.0 2.6 %collective-permute-done.3.theirs_ref = bf16[288,256]{1,0:T(8,128)(2,1)S(1)} collective-permute-done((bf16[288,256]{1,0:T(8,128)(2,1)S(1)}, bf16[288,256]{1,0:T(8,128)(2,1)S(1)}, u32[]{:S(2)}, u32[]{:S(2)}) %collective-permute-start.3) | collective-permute-done | bytes 147488 | tf_op jit(solution)/shard_map/first_tick/ppermute | solution.py:31
  60.7 0.0 collective-permute-done.4.w_theirs_ref
  60.7 0.0 copy-done.2
  60.7 0.9 first_tick.7
  61.6 6.4 %collective-permute-start.7 = (bf16[128,1152]{1,0:T(8,128)(2,1)S(1)}, bf16[128,1152]{1,0:T(8,128)(2,1)S(1)}, u32[]{:S(2)}, u32[]{:S(2)}) collective-permute-start(bf16[128,1152]{1,0:T(8,128)(2,1)S(1)} %get-tuple-element.51.mine_ref), channel_id=1, source_target_pairs={{3,0},{2,1},{1,2},{0,3},{5,4},{4,5},{7,6},{6,7},{11,8},{10,9},{9,1... | collective-permute-start | bytes 884744 | tf_op jit(solution)/shard_map/sum_and_shift/ppermute | solution.py:31
  68.0 1.9 %collective-permute-start.5 = (bf16[128,1152]{1,0:T(8,128)(2,1)S(1)}, bf16[128,1152]{1,0:T(8,128)(2,1)S(1)}, u32[]{:S(2)}, u32[]{:S(2)}) collective-permute-start(bf16[128,1152]{1,0:T(8,128)(2,1)S(1)} %get-tuple-element.52.mine_ref), channel_id=1, source_target_pairs={{3,0},{2,1},{1,2},{0,3},{5,4},{4,5},{7,6},{6,7},{11,8},{10,9},{9,1... | collective-permute-start | bytes 884744 | tf_op jit(solution)/shard_map/sum_and_shift/ppermute | solution.py:31
  69.9 6.1 %collective-permute-done.7.theirs_ref = bf16[128,1152]{1,0:T(8,128)(2,1)S(1)} collective-permute-done((bf16[128,1152]{1,0:T(8,128)(2,1)S(1)}, bf16[128,1152]{1,0:T(8,128)(2,1)S(1)}, u32[]{:S(2)}, u32[]{:S(2)}) %collective-permute-start.7) | collective-permute-done | bytes 294944 | tf_op jit(solution)/shard_map/sum_and_shift/ppermute | solution.py:31
  76.0 0.1 sum_and_shift.3
  76.1 1.9 %collective-permute-start.9 = (bf16[128,1152]{1,0:T(8,128)(2,1)S(1)}, bf16[128,1152]{1,0:T(8,128)(2,1)S(1)}, u32[]{:S(2)}, u32[]{:S(2)}) collective-permute-start(bf16[128,1152]{1,0:T(8,128)(2,1)S(1)} %sum_and_shift.3), channel_id=1, source_target_pairs={{0,5},{1,4},{2,7},{3,6},{4,11},{5,10},{6,9},{7,8},{8,13},{9,12},{1... | collective-permute-start | bytes 884744 | tf_op jit(solution)/shard_map/sum_and_shift/ppermute | solution.py:42
  78.1 6.1 %collective-permute-start.8 = (bf16[128,1152]{1,0:T(8,128)(2,1)S(1)}, bf16[128,1152]{1,0:T(8,128)(2,1)S(1)}, u32[]{:S(2)}, u32[]{:S(2)}) collective-permute-start(bf16[128,1152]{1,0:T(8,128)(2,1)S(1)} %sum_and_shift.3), channel_id=1, source_target_pairs={{0,4},{1,5},{2,6},{3,7},{4,8},{5,9},{6,10},{7,11},{8,12},{9,13},{1... | collective-permute-start | bytes 884744 | tf_op jit(solution)/shard_map/sum_and_shift/ppermute | solution.py:42
  84.2 17.5 %collective-permute-done.5.theirs_ref = bf16[128,1152]{1,0:T(8,128)(2,1)S(1)} collective-permute-done((bf16[128,1152]{1,0:T(8,128)(2,1)S(1)}, bf16[128,1152]{1,0:T(8,128)(2,1)S(1)}, u32[]{:S(2)}, u32[]{:S(2)}) %collective-permute-start.5) | collective-permute-done | bytes 294944 | tf_op jit(solution)/shard_map/sum_and_shift/ppermute | solution.py:31
  101.7 0.0 copy-done.8
  101.7 0.1 sum_and_shift.2
  101.8 1.9 %collective-permute-start.10 = (bf16[128,1152]{1,0:T(8,128)(2,1)S(1)}, bf16[128,1152]{1,0:T(8,128)(2,1)S(1)}, u32[]{:S(2)}, u32[]{:S(2)}) collective-permute-start(bf16[128,1152]{1,0:T(8,128)(2,1)S(1)} %sum_and_shift.2), channel_id=1, source_target_pairs={{0,5},{1,4},{2,7},{3,6},{4,11},{5,10},{6,9},{7,8},{8,13},{9,12},{1... | collective-permute-start | bytes 884744 | tf_op jit(solution)/shard_map/sum_and_shift/ppermute | solution.py:42
  103.8 1.9 %collective-permute-start.6 = (bf16[128,1152]{1,0:T(8,128)(2,1)S(1)}, bf16[128,1152]{1,0:T(8,128)(2,1)S(1)}, u32[]{:S(2)}, u32[]{:S(2)}) collective-permute-start(bf16[128,1152]{1,0:T(8,128)(2,1)S(1)} %sum_and_shift.2), channel_id=1, source_target_pairs={{0,4},{1,5},{2,6},{3,7},{4,8},{5,9},{6,10},{7,11},{8,12},{9,13},{1... | collective-permute-start | bytes 884744 | tf_op jit(solution)/shard_map/sum_and_shift/ppermute | solution.py:42
  105.7 0.0 collective-permute-done.9.refs_1_
  105.7 0.0 collective-permute-done.8.refs_0_
  105.7 0.0 copy-done.4
  105.7 0.0 copy-done.6
  105.7 0.0 copy-done.10
  105.8 4.7 %second_tick.5 = (bf16[288,256]{1,0:T(8,128)(2,1)S(1)}, bf16[288,256]{1,0:T(8,128)(2,1)S(1)}, bf16[288,256]{1,0:T(8,128)(2,1)S(1)}, bf16[288,512]{1,0:T(8,128)(2...) custom-call(bf16[128,1152]{1,0:T(8,128)(2,1)S(1)} %collective-permut, ...), custom_call_target="tpu_custom_call" | custom-call | flops 736100352 | bytes 4194304 | tf_op jit(solution)/shard_map/second_tick/pallas_call | solution.py:133
  110.4 4.1 %collective-permute-done.10.refs_1_ = bf16[128,1152]{1,0:T(8,128)(2,1)S(1)} collective-permute-done((bf16[128,1152]{1,0:T(8,128)(2,1)S(1)}, bf16[128,1152]{1,0:T(8,128)(2,1)S(1)}, u32[]{:S(2)}, u32[]{:S(2)}) %collective-permute-start.10) | collective-permute-done | bytes 294944 | tf_op jit(solution)/shard_map/sum_and_shift/ppermute | solution.py:42
  114.6 0.4 collective-permute-done.6.refs_0_.hidden_ref
  115.0 2.4 %second_tick.6 = (bf16[288,256]{1,0:T(8,128)(2,1)S(1)}, bf16[288,256]{1,0:T(8,128)(2,1)S(1)}, bf16[288,256]{1,0:T(8,128)(2,1)S(1)}, bf16[288,256]{1,0:T(8,128)(2,1)S(1)}) custom-call(bf16[128,1152]{1,0:T(8,128)(2,1)S(1)} %collective-permute-done.6.refs_0_.hidden_ref, bf16[128,1152]{1,0:T(8,128)(2,1)S(1)} %collective-permute-done.10.refs_1_, ...), custom_call_target="tpu_custom_call" | custom-call | flops 660602880 | bytes 4194304 | tf_op jit(solution)/shard_map/second_tick/pallas_call | solution.py:192
  117.4 1.9 %collective-permute-start.11 = (bf16[288,256]{1,0:T(8,128)(2,1)S(1)}, bf16[288,256]{1,0:T(8,128)(2,1)S(1)}, u32[]{:S(2)}, u32[]{:S(2)}) collective-permute-start(bf16[288,256]{1,0:T(8,128)(2,1)S(1)} %get-tuple-element.64), channel_id=1, source_target_pairs={{1,0},{0,1},{3,2},{2,3},{7,4},{6,5},{5,6},{4,7},{9,8},{8,9},{11,10... | collective-permute-start | bytes 442376 | tf_op jit(solution)/shard_map/second_tick/ppermute | solution.py:31
  119.3 2.1 %second_tick.7.mine_ref = bf16[288,256]{1,0:T(8,128)(2,1)S(1)} custom-call(bf16[288,512]{1,0:T(8,128)(2,1)S(1)} %get-tuple-element.53.refs_4_.refs_0_, bf16[288,512]{1,0:T(8,128)(2,1)S(1)} %get-tuple-element.54.refs_5_.refs_1_, bf16[288,256]{1,0:T(8,128)(2,1)S(1)} %get-tuple-element.55.refs_6_.refs_2_, ...), custom_call_target="tpu_custom_call" | custom-call | flops 150994944 | bytes 3145728 | tf_op jit(solution)/shard_map/second_tick/pallas_call | solution.py:220
  121.4 3.9 %collective-permute-done.11.theirs_ref = bf16[288,256]{1,0:T(8,128)(2,1)S(1)} collective-permute-done((bf16[288,256]{1,0:T(8,128)(2,1)S(1)}, bf16[288,256]{1,0:T(8,128)(2,1)S(1)}, u32[]{:S(2)}, u32[]{:S(2)}) %collective-permute-start.11) | collective-permute-done | bytes 147488 | tf_op jit(solution)/shard_map/second_tick/ppermute | solution.py:31
  125.3 0.8 second_tick.8
  126.2 3.1 %collective-permute-start.12 = (bf16[128,1152]{1,0:T(8,128)(2,1)S(1)}, bf16[128,1152]{1,0:T(8,128)(2,1)S(1)}, u32[]{:S(2)}, u32[]{:S(2)}) collective-permute-start(bf16[128,1152]{1,0:T(8,128)(2,1)S(1)} %get-tuple-element.66), channel_id=1, source_target_pairs={{3,0},{2,1},{1,2},{0,3},{5,4},{4,5},{7,6},{6,7},{11,8},{10,9},{9,1... | collective-permute-start | bytes 884744 | tf_op jit(solution)/shard_map/second_tick/ppermute | solution.py:31
  129.3 7.6 %collective-permute-done.12.theirs_ref = bf16[128,1152]{1,0:T(8,128)(2,1)S(1)} collective-permute-done((bf16[128,1152]{1,0:T(8,128)(2,1)S(1)}, bf16[128,1152]{1,0:T(8,128)(2,1)S(1)}, u32[]{:S(2)}, u32[]{:S(2)}) %collective-permute-start.12) | collective-permute-done | bytes 294944 | tf_op jit(solution)/shard_map/second_tick/ppermute | solution.py:31
  136.9 0.8 second_tick.9
Async XLA Ops:
  0.0 23.8 %collective-permute-start.1 = (bf16[128,1152]{1,0:T(8,128)(2,1)}, bf16[128,1152]{1,0:T(8,128)(2,1)S(1)}, u32[]{:S(2)}, u32[]{:S(2)}) collective-permute-start(bf16[128,1152]{1,0:T(8,128)(2,1)} %bitcast.36), channel_id=1, source_target_pairs={{3,0},{2,1},{1,2},{0,3},{5,4},{4,5},{7,6},{6,7},{11,8},{10,9},{9,1... | collective-permute-start | bytes 884744 | tf_op jit(solution)/shard_map/first_gather/ppermute | solution.py:31
  10.9 12.9 %collective-permute-start = (bf16[128,1152]{1,0:T(8,128)(2,1)}, bf16[128,1152]{1,0:T(8,128)(2,1)S(1)}, u32[]{:S(2)}, u32[]{:S(2)}) collective-permute-start(bf16[128,1152]{1,0:T(8,128)(2,1)} %bitcast.37), channel_id=1, source_target_pairs={{1,0},{0,1},{3,2},{2,3},{7,4},{6,5},{5,6},{4,7},{9,8},{8,9},{11,10... | collective-permute-start | bytes 884744 | tf_op jit(solution)/shard_map/first_gather/ppermute | solution.py:31
  23.8 36.9 %collective-permute-start.4 = (bf16[288,1152]{1,0:T(8,128)(2,1)}, bf16[288,1152]{1,0:T(8,128)(2,1)S(1)}, u32[]{:S(2)}, u32[]{:S(2)}) collective-permute-start(bf16[288,1152]{1,0:T(8,128)(2,1)} %bitcast.22), channel_id=1, source_target_pairs={{1,0},{0,1},{3,2},{2,3},{7,4},{6,5},{5,6},{4,7},{9,8},{8,9},{11,10... | collective-permute-start | bytes 1990664 | tf_op jit(solution)/shard_map/first_tick/ppermute | solution.py:31
  25.9 23.0 %collective-permute-start.2 = (bf16[128,1152]{1,0:T(8,128)(2,1)S(1)}, bf16[128,1152]{1,0:T(8,128)(2,1)S(1)}, u32[]{:S(2)}, u32[]{:S(2)}) collective-permute-start(bf16[128,1152]{1,0:T(8,128)(2,1)S(1)} %collective-permute-done.refs_0_), channel_id=1, source_target_pairs={{3,0},{2,1},{1,2},{0,3},{5,4},{4,5},{7,6},{6,7},{11,8},{10,9},{9,1... | collective-permute-start | bytes 884744 | tf_op jit(solution)/shard_map/first_gather/ppermute | solution.py:31
  33.0 1.6 %copy-start = (bf16[1,1152,3,288]{1,3,2,0:T(8,128)(2,1)S(1)}, bf16[1,1152,3,288]{1,3,2,0:T(8,128)(2,1)}, u32[]{:S(2)}) copy-start(bf16[1,1152,3,288]{1,3,2,0:T(8,128)(2,1)} %param.8) | copy-start | bytes 5971972
  34.5 1.1 copy-start.3
  35.6 1.1 copy-start.5
  36.7 1.0 copy-start.7
  37.6 0.7 copy-start.9
  38.3 10.6 %copy-start.1 = (bf16[1,1152,3,288]{1,3,2,0:T(8,128)(2,1)S(1)}, bf16[1,1152,3,288]{1,3,2,0:T(8,128)(2,1)}, u32[]{:S(2)}) copy-start(bf16[1,1152,3,288]{1,3,2,0:T(8,128)(2,1)} %param.8) | copy-start | bytes 5971972
  52.5 8.2 %copy-start.2 = (bf16[1,288,1152]{2,1,0:T(8,128)(2,1)S(1)}, bf16[1,288,1152]{2,1,0:T(8,128)(2,1)}, u32[]{:S(2)}) copy-start(bf16[1,288,1152]{2,1,0:T(8,128)(2,1)} %param.9) | copy-start | bytes 1990660
  52.5 8.2 %collective-permute-start.3 = (bf16[288,256]{1,0:T(8,128)(2,1)S(1)}, bf16[288,256]{1,0:T(8,128)(2,1)S(1)}, u32[]{:S(2)}, u32[]{:S(2)}) collective-permute-start(bf16[288,256]{1,0:T(8,128)(2,1)S(1)} %get-tuple-element.49), channel_id=1, source_target_pairs={{1,0},{0,1},{3,2},{2,3},{7,4},{6,5},{5,6},{4,7},{9,8},{8,9},{11,10... | collective-permute-start | bytes 442376 | tf_op jit(solution)/shard_map/first_tick/ppermute | solution.py:31
  57.0 44.7 %copy-start.8 = (bf16[1,128,1152]{2,1,0:T(8,128)(2,1)S(1)}, bf16[1,128,1152]{2,1,0:T(8,128)(2,1)}, u32[]{:S(2)}) copy-start(bf16[1,128,1152]{2,1,0:T(8,128)(2,1)} %param.7) | copy-start | bytes 884740
  58.0 47.7 %copy-start.4 = (bf16[1,1024,288]{1,2,0:T(8,128)(2,1)S(1)}, bf16[1,1024,288]{1,2,0:T(8,128)(2,1)}, u32[]{:S(2)}) copy-start(bf16[1,1024,288]{1,2,0:T(8,128)(2,1)} %param.11) | copy-start | bytes 1769476
  58.0 47.7 %copy-start.6 = (bf16[1,1024,288]{1,2,0:T(8,128)(2,1)S(1)}, bf16[1,1024,288]{1,2,0:T(8,128)(2,1)}, u32[]{:S(2)}) copy-start(bf16[1,1024,288]{1,2,0:T(8,128)(2,1)} %param.12) | copy-start | bytes 1769476
  58.0 47.7 %copy-start.10 = (s32[1,2]{1,0:T(1,128)S(1)}, s32[1,2]{1,0:T(1,128)}, u32[]{:S(2)}) copy-start(s32[1,2]{1,0:T(1,128)} %param.13) | copy-start | bytes 28
  61.6 14.5 %collective-permute-start.7 = (bf16[128,1152]{1,0:T(8,128)(2,1)S(1)}, bf16[128,1152]{1,0:T(8,128)(2,1)S(1)}, u32[]{:S(2)}, u32[]{:S(2)}) collective-permute-start(bf16[128,1152]{1,0:T(8,128)(2,1)S(1)} %get-tuple-element.51.mine_ref), channel_id=1, source_target_pairs={{3,0},{2,1},{1,2},{0,3},{5,4},{4,5},{7,6},{6,7},{11,8},{10,9},{9,1... | collective-permute-start | bytes 884744 | tf_op jit(solution)/shard_map/sum_and_shift/ppermute | solution.py:31
  68.0 33.7 %collective-permute-start.5 = (bf16[128,1152]{1,0:T(8,128)(2,1)S(1)}, bf16[128,1152]{1,0:T(8,128)(2,1)S(1)}, u32[]{:S(2)}, u32[]{:S(2)}) collective-permute-start(bf16[128,1152]{1,0:T(8,128)(2,1)S(1)} %get-tuple-element.52.mine_ref), channel_id=1, source_target_pairs={{3,0},{2,1},{1,2},{0,3},{5,4},{4,5},{7,6},{6,7},{11,8},{10,9},{9,1... | collective-permute-start | bytes 884744 | tf_op jit(solution)/shard_map/sum_and_shift/ppermute | solution.py:31
  76.1 29.6 %collective-permute-start.9 = (bf16[128,1152]{1,0:T(8,128)(2,1)S(1)}, bf16[128,1152]{1,0:T(8,128)(2,1)S(1)}, u32[]{:S(2)}, u32[]{:S(2)}) collective-permute-start(bf16[128,1152]{1,0:T(8,128)(2,1)S(1)} %sum_and_shift.3), channel_id=1, source_target_pairs={{0,5},{1,4},{2,7},{3,6},{4,11},{5,10},{6,9},{7,8},{8,13},{9,12},{1... | collective-permute-start | bytes 884744 | tf_op jit(solution)/shard_map/sum_and_shift/ppermute | solution.py:42
  78.1 27.6 %collective-permute-start.8 = (bf16[128,1152]{1,0:T(8,128)(2,1)S(1)}, bf16[128,1152]{1,0:T(8,128)(2,1)S(1)}, u32[]{:S(2)}, u32[]{:S(2)}) collective-permute-start(bf16[128,1152]{1,0:T(8,128)(2,1)S(1)} %sum_and_shift.3), channel_id=1, source_target_pairs={{0,4},{1,5},{2,6},{3,7},{4,8},{5,9},{6,10},{7,11},{8,12},{9,13},{1... | collective-permute-start | bytes 884744 | tf_op jit(solution)/shard_map/sum_and_shift/ppermute | solution.py:42
  101.8 12.7 %collective-permute-start.10 = (bf16[128,1152]{1,0:T(8,128)(2,1)S(1)}, bf16[128,1152]{1,0:T(8,128)(2,1)S(1)}, u32[]{:S(2)}, u32[]{:S(2)}) collective-permute-start(bf16[128,1152]{1,0:T(8,128)(2,1)S(1)} %sum_and_shift.2), channel_id=1, source_target_pairs={{0,5},{1,4},{2,7},{3,6},{4,11},{5,10},{6,9},{7,8},{8,13},{9,12},{1... | collective-permute-start | bytes 884744 | tf_op jit(solution)/shard_map/sum_and_shift/ppermute | solution.py:42
  103.8 11.2 %collective-permute-start.6 = (bf16[128,1152]{1,0:T(8,128)(2,1)S(1)}, bf16[128,1152]{1,0:T(8,128)(2,1)S(1)}, u32[]{:S(2)}, u32[]{:S(2)}) collective-permute-start(bf16[128,1152]{1,0:T(8,128)(2,1)S(1)} %sum_and_shift.2), channel_id=1, source_target_pairs={{0,4},{1,5},{2,6},{3,7},{4,8},{5,9},{6,10},{7,11},{8,12},{9,13},{1... | collective-permute-start | bytes 884744 | tf_op jit(solution)/shard_map/sum_and_shift/ppermute | solution.py:42
  117.4 7.9 %collective-permute-start.11 = (bf16[288,256]{1,0:T(8,128)(2,1)S(1)}, bf16[288,256]{1,0:T(8,128)(2,1)S(1)}, u32[]{:S(2)}, u32[]{:S(2)}) collective-permute-start(bf16[288,256]{1,0:T(8,128)(2,1)S(1)} %get-tuple-element.64), channel_id=1, source_target_pairs={{1,0},{0,1},{3,2},{2,3},{7,4},{6,5},{5,6},{4,7},{9,8},{8,9},{11,10... | collective-permute-start | bytes 442376 | tf_op jit(solution)/shard_map/second_tick/ppermute | solution.py:31
  126.2 10.7 %collective-permute-start.12 = (bf16[128,1152]{1,0:T(8,128)(2,1)S(1)}, bf16[128,1152]{1,0:T(8,128)(2,1)S(1)}, u32[]{:S(2)}, u32[]{:S(2)}) collective-permute-start(bf16[128,1152]{1,0:T(8,128)(2,1)S(1)} %get-tuple-element.66), channel_id=1, source_target_pairs={{3,0},{2,1},{1,2},{0,3},{5,4},{4,5},{7,6},{6,7},{11,8},{10,9},{9,1... | collective-permute-start | bytes 884744 | tf_op jit(solution)/shard_map/second_tick/ppermute | solution.py:31

commit v3 on v0

v3 whole, which is shorter than its diff:
```python
import functools
import math

import jax
import jax.numpy as jnp
from jax import lax
from jax.experimental import pallas as pl
from jax.experimental.pallas import tpu as pltpu
from jax.sharding import PartitionSpec as P

HEAD_DIM = 72
AXES = ("pipe", "seq")
VMEM_BYTES = 24 * 2**20
EXPONENT = math.log2(math.e) / math.sqrt(HEAD_DIM)


def partner(kind, section, member):
    if kind == 2:
        return member ^ 2
    if (kind + section) % 2 == 0:
        return member ^ 1
    return 3 - member


def exchange(array, kind):
    sections, members = lax.axis_size("pipe"), lax.axis_size("seq")
    moves = []
    for section in range(sections):
        for member in range(members):
            moves.append((section * members + partner(kind, section, member), section * members + member))
    return lax.ppermute(array, AXES, moves)


def advance(array, kind):
    sections, members = lax.axis_size("pipe"), lax.axis_size("seq")
    moves = []
    for section in range(sections):
        target = (section + 1) % sections
        for member in range(members):
            place = member if kind is None else partner(kind, section, member)
            moves.append((section * members + member, target * members + place))
    return lax.ppermute(array, AXES, moves)


def dot(a, b, contract_a, contract_b):
    return lax.dot_general(
        a, b, (((contract_a,), (contract_b,)), ((), ())), preferred_element_type=jnp.float32
    )


def normalize(rows, shift, scale):
    values = rows.astype(jnp.float32)
    center = jnp.mean(values, axis=-1, keepdims=True)
    values = values - center
    spread = jnp.mean(values * values, axis=-1, keepdims=True)
    return (values * lax.rsqrt(spread + 1e-06) * (1.0 + scale) + shift).astype(jnp.bfloat16)


def split_heads(source, refs):
    at = 0
    for ref in refs:
        for h in range(ref.shape[0]):
            ref[h] = source[at : at + HEAD_DIM].astype(jnp.bfloat16)
            at += HEAD_DIM


def attend(heads, jobs):
    scored = []
    for h in range(heads):
        for queries, caches, prior, store in jobs:
            q, pairs = queries(h), caches(h)
            scored.append((h, [dot(keys, q, 0, 0) for keys, _ in pairs], pairs, prior, store))
    for h, scores, pairs, prior, store in scored:
        top = functools.reduce(jnp.maximum, [jnp.max(s, 0, keepdims=True) for s in scores])
        total = out = 0.0
        if prior is not None:
            old_top, old_total, old_out = prior(h)
            top = jnp.maximum(top, old_top)
            shrink = jnp.exp2((old_top - top) * EXPONENT)
            total, out = old_total * shrink, old_out * shrink
        for s, (_, values) in zip(scores, pairs, strict=True):
            weights = jnp.exp2((s - top) * EXPONENT)
            total = total + jnp.sum(weights, 0, keepdims=True)
            out = out + dot(values, weights.astype(jnp.bfloat16), 1, 0)
        store(h, top, total, out)


def call(kernel, outs, scratch, flops, exps, operands, smem=()):
    specs = [pl.BlockSpec(memory_space=pltpu.SMEM if i in smem else pltpu.VMEM) for i in range(len(operands))]
    return pl.pallas_call(
        kernel,
        out_shape=outs,
        in_specs=specs,
        scratch_shapes=scratch,
        compiler_params=pltpu.CompilerParams(vmem_limit_bytes=VMEM_BYTES),
        cost_estimate=pl.CostEstimate(flops=flops, bytes_accessed=4 * 2**20, transcendentals=exps),
    )(*operands)


def shape(dtype, *sizes):
    return jax.ShapeDtypeStruct(sizes, dtype)


def prepare_kernel(offsets_ref, mods_ref, w_ref, wo_ref, stale_k_ref, stale_v_ref, mods_out, w_out, wo_out, *kept):
    mods_out[...] = mods_ref[...]
    w_out[...] = w_ref[...]
    wo_out[...] = wo_ref[...]
    count = kept[0].shape[2]
    for step in range(2):
        start = pl.multiple_of((1 - offsets_ref[step]) * count, count)
        for stale_ref, ref in zip((stale_k_ref, stale_v_ref), kept[2 * step : 2 * step + 2], strict=True):
            split_heads(stale_ref[:, pl.ds(start, count)].astype(jnp.float32), (ref,))


def prepare(offsets, mods, w, wo, stale_k, stale_v):
    width, context = stale_k.shape
    half = shape(jnp.bfloat16, width // HEAD_DIM, HEAD_DIM, context // 2)
    same = [shape(a.dtype, *a.shape) for a in (mods, w, wo)]
    return call(prepare_kernel, same + [half] * 4, [], 0, 0, (offsets, mods, w, wo, stale_k, stale_v), (0,))


def load_rows(refs, places, mods_ref, w_ref, normed, qkv):
    at = 0
    for i, first, last in places:
        normed[at : at + last - first] = normalize(refs[i][first:last], mods_ref[0:1], mods_ref[1:2])
        at += last - first
    qkv[...] = dot(w_ref[...], normed[...], 1, 1)


def early_kernel(places, n_parts, n_olds, *refs):
    parts, refs = refs[:n_parts], refs[n_parts:]
    olds, refs = refs[:n_olds], refs[n_olds:]
    mods_ref, w_ref, ko_ref, vo_ref, *outs, normed, qkv = refs
    q_ref, k_ref, v_ref, top_ref, total_ref, out_ref, *chosen = outs
    if olds:
        offsets_ref, *olds = olds
        for stale_ref, ref, old in zip((ko_ref, vo_ref), chosen, (olds[:2], olds[2:]), strict=True):
            ref[...] = stale_ref[...]

            @pl.when(offsets_ref[0] != offsets_ref[1])
            def _(ref=ref, old=old):
                split = old[0].shape[2]
                ref[:, :, :split] = old[0][...]
                ref[:, :, split:] = old[1][...]

        ko_ref, vo_ref = chosen
    load_rows(parts, places, mods_ref, w_ref, normed, qkv)
    split_heads(qkv, (q_ref, k_ref, v_ref))

    def store(h, top, total, out):
        top_ref[h : h + 1] = top
        total_ref[h : h + 1] = total
        out_ref[h] = out

    heads = q_ref.shape[0]
    attend(heads, [(lambda h: q_ref[h], lambda h: [(k_ref[h], v_ref[h]), (ko_ref[h], vo_ref[h])], None, store)])


def early(parts, places, olds, mods, w, ko, vo):
    rows, features = sum(last - first for _, first, last in places), w.shape[1]
    heads, _, count = ko.shape
    block = shape(jnp.bfloat16, heads, HEAD_DIM, rows)
    stat = shape(jnp.float32, 8, rows)
    chosen = [shape(jnp.bfloat16, *ko.shape)] * 2 if olds else []
    return call(
        functools.partial(early_kernel, places, len(parts), len(olds)),
        [block] * 3 + [stat, stat, shape(jnp.float32, heads, HEAD_DIM, rows)] + chosen,
        [pltpu.VMEM((rows, features), jnp.bfloat16), pltpu.VMEM((w.shape[0], rows), jnp.float32)],
        2 * rows * features * w.shape[0] + 4 * rows * (rows + count) * heads * HEAD_DIM,
        heads * rows * (rows + count), (*parts, *olds, mods, w, ko, vo), (len(parts),) if olds else (),
    )


def merge_job(mixed, at, span, early_refs, late_refs):
    q_ref, _, _, top_ref, total_ref, out_ref = early_refs
    _, kl_ref, vl_ref = late_refs
    first, last = span

    def store(h, top, total, out):
        mixed[h * HEAD_DIM : (h + 1) * HEAD_DIM, at : at + last - first] = out * (1.0 / total)

    return (
        lambda h: q_ref[h, :, first:last],
        lambda h: [(kl_ref[h], vl_ref[h])],
        lambda h: (top_ref[h : h + 1, first:last], total_ref[h : h + 1, first:last], out_ref[h, :, first:last]),
        store,
    )


def whole_job(mixed, at, span, early_refs, late_refs, ko_ref, vo_ref):
    _, k_ref, v_ref, *_ = early_refs
    ql_ref, kl_ref, vl_ref = late_refs
    first, last = span

    def store(h, top, total, out):
        mixed[h * HEAD_DIM : (h + 1) * HEAD_DIM, at : at + last - first] = out * (1.0 / total)

    return (
        lambda h: ql_ref[h, :, first:last],
        lambda h: [(k_ref[h], v_ref[h]), (ko_ref[h], vo_ref[h]), (kl_ref[h], vl_ref[h])],
        None,
        store,
    )


def finish(mixed, span, early_refs, late_refs, ko_ref, vo_ref):
    size = span[1] - span[0]
    attend(
        ko_ref.shape[0],
        [
            merge_job(mixed, 0, span, early_refs, late_refs),
            whole_job(mixed, size, span, early_refs, late_refs, ko_ref, vo_ref),
        ],
    )


def late_kernel(places, n_parts, *refs):
    parts, refs = refs[:n_parts], refs[n_parts:]
    mods_ref, w_ref, ko_ref, vo_ref, *early_refs = refs[:10]
    sent_ref, *late_refs, normed, qkv, mixed = refs[10:]
    load_rows(parts, places, mods_ref, w_ref, normed, qkv)
    split_heads(qkv, late_refs)
    finish(mixed, (0, mixed.shape[1] // 2), early_refs, late_refs, ko_ref, vo_ref)
    sent_ref[...] = mixed[...].astype(jnp.bfloat16)


def late(parts, places, mods, w, ko, vo, early_state):
    rows, features = sum(last - first for _, first, last in places), w.shape[1]
    heads, _, count = ko.shape
    width = heads * HEAD_DIM
    return call(
        functools.partial(late_kernel, places, len(parts)),
        [shape(jnp.bfloat16, width, rows)] + [shape(jnp.bfloat16, heads, HEAD_DIM, rows)] * 3,
        [
            pltpu.VMEM((rows, features), jnp.bfloat16),
            pltpu.VMEM((w.shape[0], rows), jnp.float32),
            pltpu.VMEM((width, rows), jnp.float32),
        ],
        2 * rows * features * w.shape[0] + 4 * rows * count * width,
        heads * rows * count, (*parts, mods, w, ko, vo, *early_state),
    )


def rest_kernel(ko_ref, vo_ref, *refs):
    early_refs, late_refs, (kept_ref, mixed) = refs[:6], refs[6:9], refs[9:]
    columns = mixed.shape[1]
    finish(mixed, (columns // 2, columns), early_refs, late_refs, ko_ref, vo_ref)
    kept_ref[...] = mixed[...].astype(jnp.bfloat16)


def rest(ko, vo, early_state, late_state):
    heads, _, count = ko.shape
    width, rows = heads * HEAD_DIM, late_state[0].shape[2]
    return call(
        rest_kernel, shape(jnp.bfloat16, width, rows), [pltpu.VMEM((width, rows), jnp.float32)],
        64 * 4 * rows * count * width, heads * rows * count, (ko, vo, *early_state, *late_state),
    )


def block(early_parts, late_parts, places, olds, mods, w, ko, vo, also=()):
    state = early(early_parts, places[0], olds, mods, w, ko, vo)
    if olds:
        *state, ko, vo = state
    sent, *late_state = late(late_parts, places[1], mods, w, ko, vo, state)
    theirs = exchange(sent, 0)
    mine = rest(ko, vo, state, late_state)
    return mine, theirs, (state[1], late_state[1], state[2], late_state[2]), also


def both_sums(mine_ref, theirs_ref, w_mine_ref, w_theirs_ref):
    return dot(mine_ref[...], w_mine_ref[...], 0, 0) + dot(theirs_ref[...], w_theirs_ref[...], 0, 0)


def shift_kernel(spans, own_ref, other_a, other_b, mods_ref, *refs):
    *refs, straight_a, crossing_a, straight_b, crossing_b = refs
    half = straight_a.shape[0] // 2
    added = mods_ref[2:3] * both_sums(*refs)
    chunks = ((other_a, straight_a, crossing_a), (other_b, straight_b, crossing_b))
    for i, ((first, last), (other, straight, crossing)) in enumerate(zip(spans, chunks, strict=True)):
        at = 2 * i * half
        own, one = added[at : at + half], added[at + half : at + 2 * half]
        straight[:half] = (own_ref[first:last].astype(jnp.float32) + own).astype(jnp.bfloat16)
        straight[half:] = (other[:half].astype(jnp.float32) + one).astype(jnp.bfloat16)
        crossing[:half] = one.astype(jnp.bfloat16)
        crossing[half:] = own.astype(jnp.bfloat16)


def shift(spans, own, others, mods, mine, theirs, w_mine, w_theirs):
    rows, features, width = mine.shape[1], w_mine.shape[1], mine.shape[0]
    return call(
        functools.partial(shift_kernel, spans), [shape(jnp.bfloat16, rows // 2, features)] * 4, [],
        4 * rows * features * width, 0, (own, *others, mods, mine, theirs, w_mine, w_theirs),
    )


def join_kernel(crossing_ref, straight_ref, out_ref):
    total = straight_ref[...].astype(jnp.float32) + crossing_ref[...].astype(jnp.float32)
    out_ref[...] = total.astype(jnp.bfloat16)


def join(crossing, straight):
    return call(join_kernel, shape(straight.dtype, *straight.shape), [], straight.size, 0, (crossing, straight))


def last_kernel(*refs):
    *refs, kept_ref, sent_ref = refs
    rows = kept_ref.shape[0]
    total = both_sums(*refs)
    kept_ref[...] = total[:rows]
    sent_ref[...] = total[rows:].astype(jnp.bfloat16)


def project_last(mine, theirs, w_mine, w_theirs):
    rows, features, width = mine.shape[1] // 2, w_mine.shape[1], mine.shape[0]
    return call(
        last_kernel, [shape(jnp.float32, rows, features), shape(jnp.bfloat16, rows, features)], [],
        8 * rows * features * width, 0, (mine, theirs, w_mine, w_theirs),
    )


def update_kernel(places, n_parts, mods_ref, *refs):
    parts, (mine_ref, theirs_ref, out_ref) = refs[:n_parts], refs[n_parts:]
    attended = mine_ref[...].astype(jnp.float32) + theirs_ref[...].astype(jnp.float32)
    at = 0
    for i, first, last in places:
        here = slice(at, at + last - first)
        new = parts[i][first:last].astype(jnp.float32) + mods_ref[2:3] * attended[here]
        out_ref[here] = new.astype(jnp.bfloat16)
        at += last - first


def update(parts, places, mods, mine, theirs):
    return call(
        functools.partial(update_kernel, places, len(parts)),
        shape(jnp.bfloat16, *mine.shape), [], 4 * mine.size, 0, (mods, *parts, mine, theirs),
    )


def pack_kernel(first, last, own_ref, zero_ref, out_ref):
    half = last - first
    out_ref[:half] = own_ref[first:last]
    out_ref[half:] = zero_ref[...]


def pack(own, first, last, zero):
    return call(
        functools.partial(pack_kernel, first, last),
        shape(own.dtype, 2 * (last - first), own.shape[1]), [], 0, 0, (own, zero),
    )


def body(patches, qkv_weight, out_weight, modulation, stale_keys, stale_values, offsets):
    width = qkv_weight.shape[3]
    features = qkv_weight.shape[1]
    w = jnp.transpose(qkv_weight[0], (1, 2, 0)).reshape(3 * width, features)
    w_sent = out_weight[0]
    slots = offsets[0]
    own = patches[0]
    rows = own.shape[0]
    half = rows // 2
    spans = ((0, half), (half, rows))

    with jax.named_scope("first_gather"):
        zeros = [exchange(own[first:last], 0) for first, last in spans]
        packed = [pack(own, *span, zero) for span, zero in zip(spans, zeros, strict=True)]
        others = [exchange(rows_here, 1) for rows_here in packed]
        w_sent, *_ = lax.optimization_barrier((w_sent, *packed))
        w_theirs = exchange(w_sent, 0)
    with jax.named_scope("prepare"):
        mods, w, w_mine, ko, vo, ko_next, vo_next = prepare(
            slots, modulation[0], w, out_weight[0], jnp.transpose(stale_keys[0]), jnp.transpose(stale_values[0])
        )
    with jax.named_scope("first_tick"):
        places = [((0, 0, half), (1, half, rows), (2, *span), (1, 0, half)) for span in spans]
        parts = [(zero, other, own) for zero, other in zip(zeros, others, strict=True)]
        mine, theirs, olds, _ = block(*parts, places, (), mods, w, ko, vo)
        straight_a, crossing_a, straight_b, crossing_b = shift(spans, own, others, mods, mine, theirs, w_mine, w_theirs)
    with jax.named_scope("second_tick"):
        crossings = [advance(crossing, 1) for crossing in (crossing_a, crossing_b)]
        straights = [advance(straight, None) for straight in (straight_a, straight_b)]
        here = [join(crossing, straight) for crossing, straight in zip(crossings, straights, strict=True)]
        others = [exchange(rows_here, 1) for rows_here in here]
        places = [((0, half, rows), (1, half, rows), (0, 0, half), (1, 0, half))] * 2
        mine, theirs, *_ = block(here, others, places, (slots, *olds), mods, w, ko_next, vo_next)
        mine_own, mine_one = project_last(mine, theirs, w_mine, w_theirs)
        return update(here, ((0, 0, half), (1, 0, half)), mods, mine_own, exchange(mine_one, 1))[None]


def solution(mesh):
    placed = (
        P("pipe", "seq", None),
        P("pipe", None, None, "seq"),
        P("pipe", "seq", None),
        P("pipe", None, None),
        P("pipe", None, "seq"),
        P("pipe", None, "seq"),
        P("pipe", None),
    )
    return jax.shard_map(
        body, mesh=mesh, in_specs=placed, out_specs=P("pipe", "seq", None), check_vma=False
    )
```

time: 221 us -> 131 us (0.59)
  the two profiles are of different devices: /device:TPU:1 before, /device:TPU:64 now
where the time goes in v3:
time: 131 us; the launch traced here: 130 us
  starting transfers between devices  57.1 us (44%)
  waiting for transfers between devices  47.4 us (36%)
  Pallas kernels  19.1 us (15%)
  local copies, waits for them, and re-layouts  6.46 us (5%)
    ppermute x10, starting transfers between devices, exchange(): return lax.ppermute(array, AXES, moves)  43.8 us
    ppermute x10, waiting for transfers between devices, exchange(): return lax.ppermute(array, AXES, moves)  29.3 us
    pallas_call x14, Pallas kernels, call(): pl.pallas_call(kernel, out_shape=outs, in_specs=specs, scratch_shapes=scr...  19.1 us
    ppermute x4, waiting for transfers between devices, advance(): return lax.ppermute(array, AXES, moves)  18.2 us
    ppermute x4, starting transfers between devices, advance(): return lax.ppermute(array, AXES, moves)  13.2 us
    unnamed x15, local copies, waits for them, and re-layouts  5.4 us
  transfers between devices with their start and end apart: 14, of which 8 were waited for; matrix products, arithmetic and copies ran while one was open for 1% of the time, Pallas kernels for 10%

profile of v3, /device:TPU:64, one launch (start us, length us, event | category | flops | bytes accessed | tf_op | source)
XLA Modules:
  0.0 130.3 jit_solution(12543034719025681385)
XLA Ops:
  0.0 0.0 copy-start.6
  0.0 0.0 copy-start.4
  0.0 1.1 slice_bitcast_fusion
  1.1 6.1 %collective-permute-start = (bf16[64,1152]{1,0:T(8,128)(2,1)S(1)}, bf16[64,1152]{1,0:T(8,128)(2,1)S(1)}, u32[]{:S(2)}, u32[]{:S(2)}) collective-permute-start(bf16[64,1152]{1,0:T(8,128)(2,1)S(1)} %get-tuple-element.78), channel_id=1, source_target_pairs={{1,0},{0,1},{3,2},{2,3},{7,4},{6,5},{5,6},{4,7},{9,8},{8,9},{11,10... | collective-permute-start | bytes 442376 | tf_op jit(solution)/shard_map/first_gather/ppermute | solution.py:31
  7.2 1.9 %collective-permute-start.2 = (bf16[64,1152]{1,0:T(8,128)(2,1)S(1)}, bf16[64,1152]{1,0:T(8,128)(2,1)S(1)}, u32[]{:S(2)}, u32[]{:S(2)}) collective-permute-start(bf16[64,1152]{1,0:T(8,128)(2,1)S(1)} %get-tuple-element.77), channel_id=1, source_target_pairs={{1,0},{0,1},{3,2},{2,3},{7,4},{6,5},{5,6},{4,7},{9,8},{8,9},{11,10... | collective-permute-start | bytes 442376 | tf_op jit(solution)/shard_map/first_gather/ppermute | solution.py:31
  9.1 2.3 %collective-permute-done.zero_ref.refs_0_ = bf16[64,1152]{1,0:T(8,128)(2,1)S(1)} collective-permute-done((bf16[64,1152]{1,0:T(8,128)(2,1)S(1)}, bf16[64,1152]{1,0:T(8,128)(2,1)S(1)}, u32[]{:S(2)}, u32[]{:S(2)}) %collective-permute-start) | collective-permute-done | bytes 147488 | tf_op jit(solution)/shard_map/first_gather/ppermute | solution.py:31
  11.4 0.0 copy-start
  11.4 1.0 copy-done
  12.4 8.9 %collective-permute-start.1 = (bf16[128,1152]{1,0:T(8,128)(2,1)S(1)}, bf16[128,1152]{1,0:T(8,128)(2,1)S(1)}, u32[]{:S(2)}, u32[]{:S(2)}) collective-permute-start(bf16[128,1152]{1,0:T(8,128)(2,1)S(1)} %first_gather.2), channel_id=1, source_target_pairs={{3,0},{2,1},{1,2},{0,3},{5,4},{4,5},{7,6},{6,7},{11,8},{10,9},{9,1... | collective-permute-start | bytes 884744 | tf_op jit(solution)/shard_map/first_gather/ppermute | solution.py:31
  21.3 0.0 collective-permute-done.2.zero_ref.refs_0_
  21.4 0.0 copy-start.1
  21.4 2.6 %collective-permute-start.3 = (bf16[128,1152]{1,0:T(8,128)(2,1)S(1)}, bf16[128,1152]{1,0:T(8,128)(2,1)S(1)}, u32[]{:S(2)}, u32[]{:S(2)}) collective-permute-start(bf16[128,1152]{1,0:T(8,128)(2,1)S(1)} %first_gather.3), channel_id=1, source_target_pairs={{3,0},{2,1},{1,2},{0,3},{5,4},{4,5},{7,6},{6,7},{11,8},{10,9},{9,1... | collective-permute-start | bytes 884744 | tf_op jit(solution)/shard_map/first_gather/ppermute | solution.py:31
  24.0 0.7 copy.10
  24.7 0.0 copy-done.6
  24.7 0.0 copy-done.4
  24.7 0.0 copy-start.2
  24.7 1.5 %copy-done.2 = bf16[1,1152,3,288]{1,3,2,0:T(8,128)(2,1)S(1)} copy-done((bf16[1,1152,3,288]{1,3,2,0:T(8,128)(2,1)S(1)}, bf16[1,1152,3,288]{1,3,2,0:T(8,128)(2,1)}, u32[]{:S(2)}) %copy-start.2) | copy-done | bytes 1990680
  26.3 0.0 copy-start.3
  26.3 1.1 copy-done.3
  27.4 0.0 copy-start.5
  27.4 1.1 copy-done.5
  28.4 0.8 prepare.1
  29.2 3.3 %collective-permute-start.5 = (bf16[288,1152]{1,0:T(8,128)(2,1)S(1)}, bf16[288,1152]{1,0:T(8,128)(2,1)S(1)}, u32[]{:S(2)}, u32[]{:S(2)}) collective-permute-start(bf16[288,1152]{1,0:T(8,128)(2,1)S(1)} %bitcast.29), channel_id=1, source_target_pairs={{1,0},{0,1},{3,2},{2,3},{7,4},{6,5},{5,6},{4,7},{9,8},{8,9},{11,10... | collective-permute-start | bytes 1990664 | tf_op jit(solution)/shard_map/first_gather/ppermute | solution.py:31
  32.5 0.0 collective-permute-done.1.refs_1_.other_a
  32.5 0.0 copy-done.1
  32.5 3.2 %first_tick.4 = (bf16[4,72,256]{2,1,0:T(8,128)(2,1)S(1)}, bf16[4,72,256]{2,1,0:T(8,128)(2,1)S(1)}, bf16[4,72,256]{2,1,0:T(8,128)(2,1)S(1)}, f32[8,256]{1,0:T(8,1...) custom-call(bf16[64,1152]{1,0:T(8,128)(2,1)S(1)} %collective-permute-done.zero_ref.refs_0_, ...), custom_call_target="tpu_custom_call" | custom-call | flops 736100352 | bytes 4194304 | tf_op jit(solution)/shard_map/first_tick/pallas_call | solution.py:90
  35.7 0.4 collective-permute-done.3.refs_1_.other_b
  36.1 3.0 %first_tick.5 = (bf16[288,256]{1,0:T(8,128)(2,1)S(1)}, bf16[4,72,256]{2,1,0:T(8,128)(2,1)S(1)}, bf16[4,72,256]{2,1,0:T(8,128)(2,1)S(1)}, bf16[4,72,256]{2,1,0:T(8,128)(2,1)S(1)}) custom-call(bf16[64,1152]{1,0:T(8,128)(2,1)S(1)} %collective-permute-done.2.zero_ref.refs_0_, bf16[128,1152]{1,0:T(8,128)(2,1)S(1)} %collective-permute-done.3.refs_1_.other_b, ...), custom_call_target="tpu_custom_call" | custom-call | flops 660602880 | bytes 4194304 | tf_op jit(solution)/shard_map/first_tick/pallas_call | solution.py:90
  39.1 9.3 %collective-permute-start.4 = (bf16[288,256]{1,0:T(8,128)(2,1)S(1)}, bf16[288,256]{1,0:T(8,128)(2,1)S(1)}, u32[]{:S(2)}, u32[]{:S(2)}) collective-permute-start(bf16[288,256]{1,0:T(8,128)(2,1)S(1)} %get-tuple-element.54), channel_id=1, source_target_pairs={{1,0},{0,1},{3,2},{2,3},{7,4},{6,5},{5,6},{4,7},{9,8},{8,9},{11,10... | collective-permute-start | bytes 442376 | tf_op jit(solution)/shard_map/first_tick/ppermute | solution.py:31
  48.4 1.2 first_tick.6.refs_0_
  49.5 3.6 %collective-permute-done.4.refs_1_ = bf16[288,256]{1,0:T(8,128)(2,1)S(1)} collective-permute-done((bf16[288,256]{1,0:T(8,128)(2,1)S(1)}, bf16[288,256]{1,0:T(8,128)(2,1)S(1)}, u32[]{:S(2)}, u32[]{:S(2)}) %collective-permute-start.4) | collective-permute-done | bytes 147488 | tf_op jit(solution)/shard_map/first_tick/ppermute | solution.py:31
  53.1 0.0 collective-permute-done.5.refs_3_
  53.1 0.9 first_tick.7
  54.0 2.2 %collective-permute-start.8 = (bf16[128,1152]{1,0:T(8,128)(2,1)S(1)}, bf16[128,1152]{1,0:T(8,128)(2,1)S(1)}, u32[]{:S(2)}, u32[]{:S(2)}) collective-permute-start(bf16[128,1152]{1,0:T(8,128)(2,1)S(1)} %get-tuple-element.59), channel_id=1, source_target_pairs={{0,7},{1,6},{2,5},{3,4},{4,9},{5,8},{6,11},{7,10},{8,15},{9,14},{1... | collective-permute-start | bytes 884744 | tf_op jit(solution)/shard_map/second_tick/ppermute | solution.py:42
  56.2 2.8 %collective-permute-start.9 = (bf16[128,1152]{1,0:T(8,128)(2,1)S(1)}, bf16[128,1152]{1,0:T(8,128)(2,1)S(1)}, u32[]{:S(2)}, u32[]{:S(2)}) collective-permute-start(bf16[128,1152]{1,0:T(8,128)(2,1)S(1)} %get-tuple-element.60), channel_id=1, source_target_pairs={{0,4},{1,5},{2,6},{3,7},{4,8},{5,9},{6,10},{7,11},{8,12},{9,13},{1... | collective-permute-start | bytes 884744 | tf_op jit(solution)/shard_map/second_tick/ppermute | solution.py:42
  59.0 6.0 %collective-permute-start.6 = (bf16[128,1152]{1,0:T(8,128)(2,1)S(1)}, bf16[128,1152]{1,0:T(8,128)(2,1)S(1)}, u32[]{:S(2)}, u32[]{:S(2)}) collective-permute-start(bf16[128,1152]{1,0:T(8,128)(2,1)S(1)} %get-tuple-element.57), channel_id=1, source_target_pairs={{0,7},{1,6},{2,5},{3,4},{4,9},{5,8},{6,11},{7,10},{8,15},{9,14},{1... | collective-permute-start | bytes 884744 | tf_op jit(solution)/shard_map/second_tick/ppermute | solution.py:42
  65.1 2.2 %collective-permute-start.7 = (bf16[128,1152]{1,0:T(8,128)(2,1)S(1)}, bf16[128,1152]{1,0:T(8,128)(2,1)S(1)}, u32[]{:S(2)}, u32[]{:S(2)}) collective-permute-start(bf16[128,1152]{1,0:T(8,128)(2,1)S(1)} %get-tuple-element.58), channel_id=1, source_target_pairs={{0,4},{1,5},{2,6},{3,7},{4,8},{5,9},{6,10},{7,11},{8,12},{9,13},{1... | collective-permute-start | bytes 884744 | tf_op jit(solution)/shard_map/second_tick/ppermute | solution.py:42
  67.3 0.0 collective-permute-done.8.crossing_ref
  67.3 10.3 %collective-permute-done.9.straight_ref = bf16[128,1152]{1,0:T(8,128)(2,1)S(1)} collective-permute-done((bf16[128,1152]{1,0:T(8,128)(2,1)S(1)}, bf16[128,1152]{1,0:T(8,128)(2,1)S(1)}, u32[]{:S(2)}, u32[]{:S(2)}) %collective-permute-start.9) | collective-permute-done | bytes 294944 | tf_op jit(solution)/shard_map/second_tick/ppermute | solution.py:42
  77.6 0.1 second_tick.8.refs_1_
  77.7 1.9 %collective-permute-start.11 = (bf16[128,1152]{1,0:T(8,128)(2,1)S(1)}, bf16[128,1152]{1,0:T(8,128)(2,1)S(1)}, u32[]{:S(2)}, u32[]{:S(2)}) collective-permute-start(bf16[128,1152]{1,0:T(8,128)(2,1)S(1)} %second_tick.8.refs_1_), channel_id=1, source_target_pairs={{3,0},{2,1},{1,2},{0,3},{5,4},{4,5},{7,6},{6,7},{11,8},{10,9},{9,1... | collective-permute-start | bytes 884744 | tf_op jit(solution)/shard_map/second_tick/ppermute | solution.py:31
  79.6 0.0 collective-permute-done.6.crossing_ref
  79.6 7.8 %collective-permute-done.7.straight_ref = bf16[128,1152]{1,0:T(8,128)(2,1)S(1)} collective-permute-done((bf16[128,1152]{1,0:T(8,128)(2,1)S(1)}, bf16[128,1152]{1,0:T(8,128)(2,1)S(1)}, u32[]{:S(2)}, u32[]{:S(2)}) %collective-permute-start.7) | collective-permute-done | bytes 294944 | tf_op jit(solution)/shard_map/second_tick/ppermute | solution.py:42
  87.4 0.1 second_tick.7.refs_0_
  87.5 1.9 %collective-permute-start.10 = (bf16[128,1152]{1,0:T(8,128)(2,1)S(1)}, bf16[128,1152]{1,0:T(8,128)(2,1)S(1)}, u32[]{:S(2)}, u32[]{:S(2)}) collective-permute-start(bf16[128,1152]{1,0:T(8,128)(2,1)S(1)} %second_tick.7.refs_0_), channel_id=1, source_target_pairs={{3,0},{2,1},{1,2},{0,3},{5,4},{4,5},{7,6},{6,7},{11,8},{10,9},{9,1... | collective-permute-start | bytes 884744 | tf_op jit(solution)/shard_map/second_tick/ppermute | solution.py:31
  89.4 4.0 %second_tick.9 = (bf16[4,72,256]{2,1,0:T(8,128)(2,1)S(1)}, bf16[4,72,256]{2,1,0:T(8,128)(2,1)S(1)}, bf16[4,72,256]{2,1,0:T(8,128)(2,1)S(1)}, f32[8,256]{1,0:T(8,...) custom-call(bf16[128,1152]{1,0:T(8,128)(2,1)S(1)} %second_tick.7.ref, ...), custom_call_target="tpu_custom_call" | custom-call | flops 736100352 | bytes 4194304 | tf_op jit(solution)/shard_map/second_tick/pallas_call | solution.py:90
  93.4 0.0 collective-permute-done.11.refs_1_
  93.4 10.2 %collective-permute-done.10.refs_0_ = bf16[128,1152]{1,0:T(8,128)(2,1)S(1)} collective-permute-done((bf16[128,1152]{1,0:T(8,128)(2,1)S(1)}, bf16[128,1152]{1,0:T(8,128)(2,1)S(1)}, u32[]{:S(2)}, u32[]{:S(2)}) %collective-permute-start.10) | collective-permute-done | bytes 294944 | tf_op jit(solution)/shard_map/second_tick/ppermute | solution.py:31
  103.6 3.0 %second_tick.10 = (bf16[288,256]{1,0:T(8,128)(2,1)S(1)}, bf16[4,72,256]{2,1,0:T(8,128)(2,1)S(1)}, bf16[4,72,256]{2,1,0:T(8,128)(2,1)S(1)}, bf16[4,72,256]{2,1,0:T(8,128)(2,1)S(1)}) custom-call(bf16[128,1152]{1,0:T(8,128)(2,1)S(1)} %collective-permute-done.10.refs_0_, bf16[128,1152]{1,0:T(8,128)(2,1)S(1)} %collective-permute-done.11.refs_1_, ...), custom_call_target="tpu_custom_call" | custom-call | flops 660602880 | bytes 4194304 | tf_op jit(solution)/shard_map/second_tick/pallas_call | solution.py:90
  106.7 1.9 %collective-permute-start.12 = (bf16[288,256]{1,0:T(8,128)(2,1)S(1)}, bf16[288,256]{1,0:T(8,128)(2,1)S(1)}, u32[]{:S(2)}, u32[]{:S(2)}) collective-permute-start(bf16[288,256]{1,0:T(8,128)(2,1)S(1)} %get-tuple-element.74), channel_id=1, source_target_pairs={{1,0},{0,1},{3,2},{2,3},{7,4},{6,5},{5,6},{4,7},{9,8},{8,9},{11,10... | collective-permute-start | bytes 442376 | tf_op jit(solution)/shard_map/second_tick/ppermute | solution.py:31
  108.6 1.2 second_tick.11.refs_0_
  109.8 4.9 %collective-permute-done.12.refs_1_ = bf16[288,256]{1,0:T(8,128)(2,1)S(1)} collective-permute-done((bf16[288,256]{1,0:T(8,128)(2,1)S(1)}, bf16[288,256]{1,0:T(8,128)(2,1)S(1)}, u32[]{:S(2)}, u32[]{:S(2)}) %collective-permute-start.12) | collective-permute-done | bytes 147488 | tf_op jit(solution)/shard_map/second_tick/ppermute | solution.py:31
  114.7 0.9 second_tick.12
  115.6 6.1 %collective-permute-start.13 = (bf16[128,1152]{1,0:T(8,128)(2,1)S(1)}, bf16[128,1152]{1,0:T(8,128)(2,1)S(1)}, u32[]{:S(2)}, u32[]{:S(2)}) collective-permute-start(bf16[128,1152]{1,0:T(8,128)(2,1)S(1)} %get-tuple-element.76), channel_id=1, source_target_pairs={{3,0},{2,1},{1,2},{0,3},{5,4},{4,5},{7,6},{6,7},{11,8},{10,9},{9,1... | collective-permute-start | bytes 884744 | tf_op jit(solution)/shard_map/second_tick/ppermute | solution.py:31
  121.6 7.8 %collective-permute-done.13.refs_3_ = bf16[128,1152]{1,0:T(8,128)(2,1)S(1)} collective-permute-done((bf16[128,1152]{1,0:T(8,128)(2,1)S(1)}, bf16[128,1152]{1,0:T(8,128)(2,1)S(1)}, u32[]{:S(2)}, u32[]{:S(2)}) %collective-permute-start.13) | collective-permute-done | bytes 294944 | tf_op jit(solution)/shard_map/second_tick/ppermute | solution.py:31
  129.5 0.8 second_tick.13
  (2 shorter events, 0.0 us)
Async XLA Ops:
  0.0 24.7 %copy-start.6 = (s32[1,2]{1,0:T(1,128)S(1)}, s32[1,2]{1,0:T(1,128)}, u32[]{:S(2)}) copy-start(s32[1,2]{1,0:T(1,128)} %param.13) | copy-start | bytes 28
  0.0 24.7 %copy-start.4 = (bf16[1,1024,288]{1,2,0:T(8,128)(2,1)S(1)}, bf16[1,1024,288]{1,2,0:T(8,128)(2,1)}, u32[]{:S(2)}) copy-start(bf16[1,1024,288]{1,2,0:T(8,128)(2,1)} %param.11) | copy-start | bytes 1769476
  1.1 10.4 %collective-permute-start = (bf16[64,1152]{1,0:T(8,128)(2,1)S(1)}, bf16[64,1152]{1,0:T(8,128)(2,1)S(1)}, u32[]{:S(2)}, u32[]{:S(2)}) collective-permute-start(bf16[64,1152]{1,0:T(8,128)(2,1)S(1)} %get-tuple-element.78), channel_id=1, source_target_pairs={{1,0},{0,1},{3,2},{2,3},{7,4},{6,5},{5,6},{4,7},{9,8},{8,9},{11,10... | collective-permute-start | bytes 442376 | tf_op jit(solution)/shard_map/first_gather/ppermute | solution.py:31
  7.2 14.2 %collective-permute-start.2 = (bf16[64,1152]{1,0:T(8,128)(2,1)S(1)}, bf16[64,1152]{1,0:T(8,128)(2,1)S(1)}, u32[]{:S(2)}, u32[]{:S(2)}) collective-permute-start(bf16[64,1152]{1,0:T(8,128)(2,1)S(1)} %get-tuple-element.77), channel_id=1, source_target_pairs={{1,0},{0,1},{3,2},{2,3},{7,4},{6,5},{5,6},{4,7},{9,8},{8,9},{11,10... | collective-permute-start | bytes 442376 | tf_op jit(solution)/shard_map/first_gather/ppermute | solution.py:31
  11.4 1.0 copy-start
  12.4 20.1 %collective-permute-start.1 = (bf16[128,1152]{1,0:T(8,128)(2,1)S(1)}, bf16[128,1152]{1,0:T(8,128)(2,1)S(1)}, u32[]{:S(2)}, u32[]{:S(2)}) collective-permute-start(bf16[128,1152]{1,0:T(8,128)(2,1)S(1)} %first_gather.2), channel_id=1, source_target_pairs={{3,0},{2,1},{1,2},{0,3},{5,4},{4,5},{7,6},{6,7},{11,8},{10,9},{9,1... | collective-permute-start | bytes 884744 | tf_op jit(solution)/shard_map/first_gather/ppermute | solution.py:31
  21.4 11.2 %copy-start.1 = (bf16[1,128,1152]{2,1,0:T(8,128)(2,1)S(1)}, bf16[1,128,1152]{2,1,0:T(8,128)(2,1)}, u32[]{:S(2)}) copy-start(bf16[1,128,1152]{2,1,0:T(8,128)(2,1)} %param.7) | copy-start | bytes 884740
  21.4 14.7 %collective-permute-start.3 = (bf16[128,1152]{1,0:T(8,128)(2,1)S(1)}, bf16[128,1152]{1,0:T(8,128)(2,1)S(1)}, u32[]{:S(2)}, u32[]{:S(2)}) collective-permute-start(bf16[128,1152]{1,0:T(8,128)(2,1)S(1)} %first_gather.3), channel_id=1, source_target_pairs={{3,0},{2,1},{1,2},{0,3},{5,4},{4,5},{7,6},{6,7},{11,8},{10,9},{9,1... | collective-permute-start | bytes 884744 | tf_op jit(solution)/shard_map/first_gather/ppermute | solution.py:31
  24.7 1.6 %copy-start.2 = (bf16[1,1152,3,288]{1,3,2,0:T(8,128)(2,1)S(1)}, bf16[1,1152,3,288]{1,3,2,0:T(8,128)(2,1)}, u32[]{:S(2)}) copy-start(bf16[1,1152,3,288]{1,3,2,0:T(8,128)(2,1)} %param.8) | copy-start | bytes 5971972
  26.3 1.1 copy-start.3
  27.4 1.1 copy-start.5
  29.2 23.9 %collective-permute-start.5 = (bf16[288,1152]{1,0:T(8,128)(2,1)S(1)}, bf16[288,1152]{1,0:T(8,128)(2,1)S(1)}, u32[]{:S(2)}, u32[]{:S(2)}) collective-permute-start(bf16[288,1152]{1,0:T(8,128)(2,1)S(1)} %bitcast.29), channel_id=1, source_target_pairs={{1,0},{0,1},{3,2},{2,3},{7,4},{6,5},{5,6},{4,7},{9,8},{8,9},{11,10... | collective-permute-start | bytes 1990664 | tf_op jit(solution)/shard_map/first_gather/ppermute | solution.py:31
  39.1 14.0 %collective-permute-start.4 = (bf16[288,256]{1,0:T(8,128)(2,1)S(1)}, bf16[288,256]{1,0:T(8,128)(2,1)S(1)}, u32[]{:S(2)}, u32[]{:S(2)}) collective-permute-start(bf16[288,256]{1,0:T(8,128)(2,1)S(1)} %get-tuple-element.54), channel_id=1, source_target_pairs={{1,0},{0,1},{3,2},{2,3},{7,4},{6,5},{5,6},{4,7},{9,8},{8,9},{11,10... | collective-permute-start | bytes 442376 | tf_op jit(solution)/shard_map/first_tick/ppermute | solution.py:31
  54.0 13.3 %collective-permute-start.8 = (bf16[128,1152]{1,0:T(8,128)(2,1)S(1)}, bf16[128,1152]{1,0:T(8,128)(2,1)S(1)}, u32[]{:S(2)}, u32[]{:S(2)}) collective-permute-start(bf16[128,1152]{1,0:T(8,128)(2,1)S(1)} %get-tuple-element.59), channel_id=1, source_target_pairs={{0,7},{1,6},{2,5},{3,4},{4,9},{5,8},{6,11},{7,10},{8,15},{9,14},{1... | collective-permute-start | bytes 884744 | tf_op jit(solution)/shard_map/second_tick/ppermute | solution.py:42
  56.2 21.4 %collective-permute-start.9 = (bf16[128,1152]{1,0:T(8,128)(2,1)S(1)}, bf16[128,1152]{1,0:T(8,128)(2,1)S(1)}, u32[]{:S(2)}, u32[]{:S(2)}) collective-permute-start(bf16[128,1152]{1,0:T(8,128)(2,1)S(1)} %get-tuple-element.60), channel_id=1, source_target_pairs={{0,4},{1,5},{2,6},{3,7},{4,8},{5,9},{6,10},{7,11},{8,12},{9,13},{1... | collective-permute-start | bytes 884744 | tf_op jit(solution)/shard_map/second_tick/ppermute | solution.py:42
  59.0 20.6 %collective-permute-start.6 = (bf16[128,1152]{1,0:T(8,128)(2,1)S(1)}, bf16[128,1152]{1,0:T(8,128)(2,1)S(1)}, u32[]{:S(2)}, u32[]{:S(2)}) collective-permute-start(bf16[128,1152]{1,0:T(8,128)(2,1)S(1)} %get-tuple-element.57), channel_id=1, source_target_pairs={{0,7},{1,6},{2,5},{3,4},{4,9},{5,8},{6,11},{7,10},{8,15},{9,14},{1... | collective-permute-start | bytes 884744 | tf_op jit(solution)/shard_map/second_tick/ppermute | solution.py:42
  65.1 22.3 %collective-permute-start.7 = (bf16[128,1152]{1,0:T(8,128)(2,1)S(1)}, bf16[128,1152]{1,0:T(8,128)(2,1)S(1)}, u32[]{:S(2)}, u32[]{:S(2)}) collective-permute-start(bf16[128,1152]{1,0:T(8,128)(2,1)S(1)} %get-tuple-element.58), channel_id=1, source_target_pairs={{0,4},{1,5},{2,6},{3,7},{4,8},{5,9},{6,10},{7,11},{8,12},{9,13},{1... | collective-permute-start | bytes 884744 | tf_op jit(solution)/shard_map/second_tick/ppermute | solution.py:42
  77.7 15.7 %collective-permute-start.11 = (bf16[128,1152]{1,0:T(8,128)(2,1)S(1)}, bf16[128,1152]{1,0:T(8,128)(2,1)S(1)}, u32[]{:S(2)}, u32[]{:S(2)}) collective-permute-start(bf16[128,1152]{1,0:T(8,128)(2,1)S(1)} %second_tick.8.refs_1_), channel_id=1, source_target_pairs={{3,0},{2,1},{1,2},{0,3},{5,4},{4,5},{7,6},{6,7},{11,8},{10,9},{9,1... | collective-permute-start | bytes 884744 | tf_op jit(solution)/shard_map/second_tick/ppermute | solution.py:31
  87.5 16.1 %collective-permute-start.10 = (bf16[128,1152]{1,0:T(8,128)(2,1)S(1)}, bf16[128,1152]{1,0:T(8,128)(2,1)S(1)}, u32[]{:S(2)}, u32[]{:S(2)}) collective-permute-start(bf16[128,1152]{1,0:T(8,128)(2,1)S(1)} %second_tick.7.refs_0_), channel_id=1, source_target_pairs={{3,0},{2,1},{1,2},{0,3},{5,4},{4,5},{7,6},{6,7},{11,8},{10,9},{9,1... | collective-permute-start | bytes 884744 | tf_op jit(solution)/shard_map/second_tick/ppermute | solution.py:31
  106.7 8.0 %collective-permute-start.12 = (bf16[288,256]{1,0:T(8,128)(2,1)S(1)}, bf16[288,256]{1,0:T(8,128)(2,1)S(1)}, u32[]{:S(2)}, u32[]{:S(2)}) collective-permute-start(bf16[288,256]{1,0:T(8,128)(2,1)S(1)} %get-tuple-element.74), channel_id=1, source_target_pairs={{1,0},{0,1},{3,2},{2,3},{7,4},{6,5},{5,6},{4,7},{9,8},{8,9},{11,10... | collective-permute-start | bytes 442376 | tf_op jit(solution)/shard_map/second_tick/ppermute | solution.py:31
  115.6 13.9 %collective-permute-start.13 = (bf16[128,1152]{1,0:T(8,128)(2,1)S(1)}, bf16[128,1152]{1,0:T(8,128)(2,1)S(1)}, u32[]{:S(2)}, u32[]{:S(2)}) collective-permute-start(bf16[128,1152]{1,0:T(8,128)(2,1)S(1)} %get-tuple-element.76), channel_id=1, source_target_pairs={{3,0},{2,1},{1,2},{0,3},{5,4},{4,5},{7,6},{6,7},{11,8},{10,9},{9,1... | collective-permute-start | bytes 884744 | tf_op jit(solution)/shard_map/second_tick/ppermute | solution.py:31

commit v4 on v3

--- a/solution.py
+++ b/solution.py
@@ -376,9 +376,9 @@
         mine, theirs, olds, _ = block(*parts, places, (), mods, w, ko, vo)
         straight_a, crossing_a, straight_b, crossing_b = shift(spans, own, others, mods, mine, theirs, w_mine, w_theirs)
     with jax.named_scope("second_tick"):
+        straights = [advance(straight, None) for straight in (straight_a, straight_b)]
         crossings = [advance(crossing, 1) for crossing in (crossing_a, crossing_b)]
-        straights = [advance(straight, None) for straight in (straight_a, straight_b)]
-        here = [join(crossing, straight) for crossing, straight in zip(crossings, straights, strict=True)]
+        here = [join(straight, crossing) for crossing, straight in zip(crossings, straights, strict=True)]
         others = [exchange(rows_here, 1) for rows_here in here]
         places = [((0, half, rows), (1, half, rows), (0, 0, half), (1, 0, half))] * 2
         mine, theirs, *_ = block(here, others, places, (slots, *olds), mods, w, ko_next, vo_next)

time: 131 us -> 128 us (0.977)
  the two profiles are of different devices: /device:TPU:64 before, /device:TPU:128 now
where the time goes in v4:
time: 128 us
  starting transfers between devices  77.8 us (61%)
  waiting for transfers between devices  24.1 us (19%)
  Pallas kernels  19 us (15%)
  local copies, waits for them, and re-layouts  6.46 us (5%)
    ppermute x10, starting transfers between devices, exchange(): return lax.ppermute(array, AXES, moves)  61.9 us
    ppermute x10, waiting for transfers between devices, exchange(): return lax.ppermute(array, AXES, moves)  20.3 us
    pallas_call x14, Pallas kernels, call(): pl.pallas_call(kernel, out_shape=outs, in_specs=specs, scratch_shapes=scr...  19 us
    ppermute x4, starting transfers between devices, advance(): return lax.ppermute(array, AXES, moves)  15.9 us
    unnamed x15, local copies, waits for them, and re-layouts  5.4 us
    ppermute x4, waiting for transfers between devices, advance(): return lax.ppermute(array, AXES, moves)  3.83 us
  transfers between devices with their start and end apart: 14, of which 6 were waited for; matrix products, arithmetic and copies ran while one was open for 1% of the time, Pallas kernels for 11%

profile of v4, /device:TPU:128, one launch (start us, length us, event | category | flops | bytes accessed | tf_op | source)
XLA Modules:
  0.0 127.7 jit_solution(1476451866083827850)
XLA Ops:
  0.0 0.0 copy-start.6
  0.0 0.0 copy-start.4
  0.0 1.1 slice_bitcast_fusion
  1.1 6.0 %collective-permute-start = (bf16[64,1152]{1,0:T(8,128)(2,1)S(1)}, bf16[64,1152]{1,0:T(8,128)(2,1)S(1)}, u32[]{:S(2)}, u32[]{:S(2)}) collective-permute-start(bf16[64,1152]{1,0:T(8,128)(2,1)S(1)} %get-tuple-element.78), channel_id=1, source_target_pairs={{1,0},{0,1},{3,2},{2,3},{7,4},{6,5},{5,6},{4,7},{9,8},{8,9},{11,10... | collective-permute-start | bytes 442376 | tf_op jit(solution)/shard_map/first_gather/ppermute | solution.py:31
  7.1 1.9 %collective-permute-start.2 = (bf16[64,1152]{1,0:T(8,128)(2,1)S(1)}, bf16[64,1152]{1,0:T(8,128)(2,1)S(1)}, u32[]{:S(2)}, u32[]{:S(2)}) collective-permute-start(bf16[64,1152]{1,0:T(8,128)(2,1)S(1)} %get-tuple-element.77), channel_id=1, source_target_pairs={{1,0},{0,1},{3,2},{2,3},{7,4},{6,5},{5,6},{4,7},{9,8},{8,9},{11,10... | collective-permute-start | bytes 442376 | tf_op jit(solution)/shard_map/first_gather/ppermute | solution.py:31
  9.0 1.3 %collective-permute-done.zero_ref.refs_0_ = bf16[64,1152]{1,0:T(8,128)(2,1)S(1)} collective-permute-done((bf16[64,1152]{1,0:T(8,128)(2,1)S(1)}, bf16[64,1152]{1,0:T(8,128)(2,1)S(1)}, u32[]{:S(2)}, u32[]{:S(2)}) %collective-permute-start) | collective-permute-done | bytes 147488 | tf_op jit(solution)/shard_map/first_gather/ppermute | solution.py:31
  10.3 0.0 copy-start
  10.3 1.0 copy-done
  11.3 7.9 %collective-permute-start.1 = (bf16[128,1152]{1,0:T(8,128)(2,1)S(1)}, bf16[128,1152]{1,0:T(8,128)(2,1)S(1)}, u32[]{:S(2)}, u32[]{:S(2)}) collective-permute-start(bf16[128,1152]{1,0:T(8,128)(2,1)S(1)} %first_gather.2), channel_id=1, source_target_pairs={{3,0},{2,1},{1,2},{0,3},{5,4},{4,5},{7,6},{6,7},{11,8},{10,9},{9,1... | collective-permute-start | bytes 884744 | tf_op jit(solution)/shard_map/first_gather/ppermute | solution.py:31
  19.2 0.0 collective-permute-done.2.zero_ref.refs_0_
  19.2 0.0 copy-start.1
  19.2 3.4 %collective-permute-start.3 = (bf16[128,1152]{1,0:T(8,128)(2,1)S(1)}, bf16[128,1152]{1,0:T(8,128)(2,1)S(1)}, u32[]{:S(2)}, u32[]{:S(2)}) collective-permute-start(bf16[128,1152]{1,0:T(8,128)(2,1)S(1)} %first_gather.3), channel_id=1, source_target_pairs={{3,0},{2,1},{1,2},{0,3},{5,4},{4,5},{7,6},{6,7},{11,8},{10,9},{9,1... | collective-permute-start | bytes 884744 | tf_op jit(solution)/shard_map/first_gather/ppermute | solution.py:31
  22.6 0.7 copy.10
  23.4 0.0 copy-done.6
  23.4 0.0 copy-done.4
  23.4 0.0 copy-start.2
  23.4 1.5 %copy-done.2 = bf16[1,1152,3,288]{1,3,2,0:T(8,128)(2,1)S(1)} copy-done((bf16[1,1152,3,288]{1,3,2,0:T(8,128)(2,1)S(1)}, bf16[1,1152,3,288]{1,3,2,0:T(8,128)(2,1)}, u32[]{:S(2)}) %copy-start.2) | copy-done | bytes 1990680
  24.9 0.0 copy-start.3
  24.9 1.1 copy-done.3
  26.0 0.0 copy-start.5
  26.0 1.1 copy-done.5
  27.1 0.8 prepare.1
  27.9 4.0 %collective-permute-start.5 = (bf16[288,1152]{1,0:T(8,128)(2,1)S(1)}, bf16[288,1152]{1,0:T(8,128)(2,1)S(1)}, u32[]{:S(2)}, u32[]{:S(2)}) collective-permute-start(bf16[288,1152]{1,0:T(8,128)(2,1)S(1)} %bitcast.29), channel_id=1, source_target_pairs={{1,0},{0,1},{3,2},{2,3},{7,4},{6,5},{5,6},{4,7},{9,8},{8,9},{11,10... | collective-permute-start | bytes 1990664 | tf_op jit(solution)/shard_map/first_gather/ppermute | solution.py:31
  31.9 0.0 collective-permute-done.1.refs_1_.other_a
  31.9 0.0 copy-done.1
  31.9 3.2 %first_tick.4 = (bf16[4,72,256]{2,1,0:T(8,128)(2,1)S(1)}, bf16[4,72,256]{2,1,0:T(8,128)(2,1)S(1)}, bf16[4,72,256]{2,1,0:T(8,128)(2,1)S(1)}, f32[8,256]{1,0:T(8,1...) custom-call(bf16[64,1152]{1,0:T(8,128)(2,1)S(1)} %collective-permute-done.zero_ref.refs_0_, ...), custom_call_target="tpu_custom_call" | custom-call | flops 736100352 | bytes 4194304 | tf_op jit(solution)/shard_map/first_tick/pallas_call | solution.py:90
  35.1 0.0 collective-permute-done.3.refs_1_.other_b
  35.1 3.0 %first_tick.5 = (bf16[288,256]{1,0:T(8,128)(2,1)S(1)}, bf16[4,72,256]{2,1,0:T(8,128)(2,1)S(1)}, bf16[4,72,256]{2,1,0:T(8,128)(2,1)S(1)}, bf16[4,72,256]{2,1,0:T(8,128)(2,1)S(1)}) custom-call(bf16[64,1152]{1,0:T(8,128)(2,1)S(1)} %collective-permute-done.2.zero_ref.refs_0_, bf16[128,1152]{1,0:T(8,128)(2,1)S(1)} %collective-permute-done.3.refs_1_.other_b, ...), custom_call_target="tpu_custom_call" | custom-call | flops 660602880 | bytes 4194304 | tf_op jit(solution)/shard_map/first_tick/pallas_call | solution.py:90
  38.1 9.5 %collective-permute-start.4 = (bf16[288,256]{1,0:T(8,128)(2,1)S(1)}, bf16[288,256]{1,0:T(8,128)(2,1)S(1)}, u32[]{:S(2)}, u32[]{:S(2)}) collective-permute-start(bf16[288,256]{1,0:T(8,128)(2,1)S(1)} %get-tuple-element.54), channel_id=1, source_target_pairs={{1,0},{0,1},{3,2},{2,3},{7,4},{6,5},{5,6},{4,7},{9,8},{8,9},{11,10... | collective-permute-start | bytes 442376 | tf_op jit(solution)/shard_map/first_tick/ppermute | solution.py:31
  47.6 1.2 first_tick.6.refs_0_
  48.8 3.2 %collective-permute-done.4.refs_1_ = bf16[288,256]{1,0:T(8,128)(2,1)S(1)} collective-permute-done((bf16[288,256]{1,0:T(8,128)(2,1)S(1)}, bf16[288,256]{1,0:T(8,128)(2,1)S(1)}, u32[]{:S(2)}, u32[]{:S(2)}) %collective-permute-start.4) | collective-permute-done | bytes 147488 | tf_op jit(solution)/shard_map/first_tick/ppermute | solution.py:31
  52.0 0.0 collective-permute-done.5.refs_3_
  52.0 0.9 first_tick.7
  52.9 2.4 %collective-permute-start.8 = (bf16[128,1152]{1,0:T(8,128)(2,1)S(1)}, bf16[128,1152]{1,0:T(8,128)(2,1)S(1)}, u32[]{:S(2)}, u32[]{:S(2)}) collective-permute-start(bf16[128,1152]{1,0:T(8,128)(2,1)S(1)} %get-tuple-element.59), channel_id=1, source_target_pairs={{0,4},{1,5},{2,6},{3,7},{4,8},{5,9},{6,10},{7,11},{8,12},{9,13},{1... | collective-permute-start | bytes 884744 | tf_op jit(solution)/shard_map/second_tick/ppermute | solution.py:42
  55.4 3.7 %collective-permute-start.9 = (bf16[128,1152]{1,0:T(8,128)(2,1)S(1)}, bf16[128,1152]{1,0:T(8,128)(2,1)S(1)}, u32[]{:S(2)}, u32[]{:S(2)}) collective-permute-start(bf16[128,1152]{1,0:T(8,128)(2,1)S(1)} %get-tuple-element.60), channel_id=1, source_target_pairs={{0,7},{1,6},{2,5},{3,4},{4,9},{5,8},{6,11},{7,10},{8,15},{9,14},{1... | collective-permute-start | bytes 884744 | tf_op jit(solution)/shard_map/second_tick/ppermute | solution.py:42
  59.0 2.9 %collective-permute-start.6 = (bf16[128,1152]{1,0:T(8,128)(2,1)S(1)}, bf16[128,1152]{1,0:T(8,128)(2,1)S(1)}, u32[]{:S(2)}, u32[]{:S(2)}) collective-permute-start(bf16[128,1152]{1,0:T(8,128)(2,1)S(1)} %get-tuple-element.57), channel_id=1, source_target_pairs={{0,4},{1,5},{2,6},{3,7},{4,8},{5,9},{6,10},{7,11},{8,12},{9,13},{1... | collective-permute-start | bytes 884744 | tf_op jit(solution)/shard_map/second_tick/ppermute | solution.py:42
  62.0 6.8 %collective-permute-start.7 = (bf16[128,1152]{1,0:T(8,128)(2,1)S(1)}, bf16[128,1152]{1,0:T(8,128)(2,1)S(1)}, u32[]{:S(2)}, u32[]{:S(2)}) collective-permute-start(bf16[128,1152]{1,0:T(8,128)(2,1)S(1)} %get-tuple-element.58), channel_id=1, source_target_pairs={{0,7},{1,6},{2,5},{3,4},{4,9},{5,8},{6,11},{7,10},{8,15},{9,14},{1... | collective-permute-start | bytes 884744 | tf_op jit(solution)/shard_map/second_tick/ppermute | solution.py:42
  68.8 0.0 collective-permute-done.8.crossing_ref
  68.8 3.8 %collective-permute-done.9.straight_ref = bf16[128,1152]{1,0:T(8,128)(2,1)S(1)} collective-permute-done((bf16[128,1152]{1,0:T(8,128)(2,1)S(1)}, bf16[128,1152]{1,0:T(8,128)(2,1)S(1)}, u32[]{:S(2)}, u32[]{:S(2)}) %collective-permute-start.9) | collective-permute-done | bytes 294944 | tf_op jit(solution)/shard_map/second_tick/ppermute | solution.py:42
  72.7 0.1 second_tick.8.refs_1_
  72.7 11.0 %collective-permute-start.11 = (bf16[128,1152]{1,0:T(8,128)(2,1)S(1)}, bf16[128,1152]{1,0:T(8,128)(2,1)S(1)}, u32[]{:S(2)}, u32[]{:S(2)}) collective-permute-start(bf16[128,1152]{1,0:T(8,128)(2,1)S(1)} %second_tick.8.refs_1_), channel_id=1, source_target_pairs={{3,0},{2,1},{1,2},{0,3},{5,4},{4,5},{7,6},{6,7},{11,8},{10,9},{9,1... | collective-permute-start | bytes 884744 | tf_op jit(solution)/shard_map/second_tick/ppermute | solution.py:31
  83.7 0.0 collective-permute-done.6.crossing_ref
  83.7 0.0 collective-permute-done.7.straight_ref
  83.7 0.1 second_tick.7.refs_0_
  83.8 10.2 %collective-permute-start.10 = (bf16[128,1152]{1,0:T(8,128)(2,1)S(1)}, bf16[128,1152]{1,0:T(8,128)(2,1)S(1)}, u32[]{:S(2)}, u32[]{:S(2)}) collective-permute-start(bf16[128,1152]{1,0:T(8,128)(2,1)S(1)} %second_tick.7.refs_0_), channel_id=1, source_target_pairs={{3,0},{2,1},{1,2},{0,3},{5,4},{4,5},{7,6},{6,7},{11,8},{10,9},{9,1... | collective-permute-start | bytes 884744 | tf_op jit(solution)/shard_map/second_tick/ppermute | solution.py:31
  94.0 4.0 %second_tick.9 = (bf16[4,72,256]{2,1,0:T(8,128)(2,1)S(1)}, bf16[4,72,256]{2,1,0:T(8,128)(2,1)S(1)}, bf16[4,72,256]{2,1,0:T(8,128)(2,1)S(1)}, f32[8,256]{1,0:T(8,...) custom-call(bf16[128,1152]{1,0:T(8,128)(2,1)S(1)} %second_tick.7.ref, ...), custom_call_target="tpu_custom_call" | custom-call | flops 736100352 | bytes 4194304 | tf_op jit(solution)/shard_map/second_tick/pallas_call | solution.py:90
  98.0 0.0 collective-permute-done.11.refs_1_
  98.0 2.7 %collective-permute-done.10.refs_0_ = bf16[128,1152]{1,0:T(8,128)(2,1)S(1)} collective-permute-done((bf16[128,1152]{1,0:T(8,128)(2,1)S(1)}, bf16[128,1152]{1,0:T(8,128)(2,1)S(1)}, u32[]{:S(2)}, u32[]{:S(2)}) %collective-permute-start.10) | collective-permute-done | bytes 294944 | tf_op jit(solution)/shard_map/second_tick/ppermute | solution.py:31
  100.7 3.0 %second_tick.10 = (bf16[288,256]{1,0:T(8,128)(2,1)S(1)}, bf16[4,72,256]{2,1,0:T(8,128)(2,1)S(1)}, bf16[4,72,256]{2,1,0:T(8,128)(2,1)S(1)}, bf16[4,72,256]{2,1,0:T(8,128)(2,1)S(1)}) custom-call(bf16[128,1152]{1,0:T(8,128)(2,1)S(1)} %collective-permute-done.10.refs_0_, bf16[128,1152]{1,0:T(8,128)(2,1)S(1)} %collective-permute-done.11.refs_1_, ...), custom_call_target="tpu_custom_call" | custom-call | flops 660602880 | bytes 4194304 | tf_op jit(solution)/shard_map/second_tick/pallas_call | solution.py:90
  103.7 1.9 %collective-permute-start.12 = (bf16[288,256]{1,0:T(8,128)(2,1)S(1)}, bf16[288,256]{1,0:T(8,128)(2,1)S(1)}, u32[]{:S(2)}, u32[]{:S(2)}) collective-permute-start(bf16[288,256]{1,0:T(8,128)(2,1)S(1)} %get-tuple-element.74), channel_id=1, source_target_pairs={{1,0},{0,1},{3,2},{2,3},{7,4},{6,5},{5,6},{4,7},{9,8},{8,9},{11,10... | collective-permute-start | bytes 442376 | tf_op jit(solution)/shard_map/second_tick/ppermute | solution.py:31
  105.7 1.2 second_tick.11.refs_0_
  106.9 7.5 %collective-permute-done.12.refs_1_ = bf16[288,256]{1,0:T(8,128)(2,1)S(1)} collective-permute-done((bf16[288,256]{1,0:T(8,128)(2,1)S(1)}, bf16[288,256]{1,0:T(8,128)(2,1)S(1)}, u32[]{:S(2)}, u32[]{:S(2)}) %collective-permute-start.12) | collective-permute-done | bytes 147488 | tf_op jit(solution)/shard_map/second_tick/ppermute | solution.py:31
  114.4 0.9 second_tick.12
  115.2 6.0 %collective-permute-start.13 = (bf16[128,1152]{1,0:T(8,128)(2,1)S(1)}, bf16[128,1152]{1,0:T(8,128)(2,1)S(1)}, u32[]{:S(2)}, u32[]{:S(2)}) collective-permute-start(bf16[128,1152]{1,0:T(8,128)(2,1)S(1)} %get-tuple-element.76), channel_id=1, source_target_pairs={{3,0},{2,1},{1,2},{0,3},{5,4},{4,5},{7,6},{6,7},{11,8},{10,9},{9,1... | collective-permute-start | bytes 884744 | tf_op jit(solution)/shard_map/second_tick/ppermute | solution.py:31
  121.3 5.6 %collective-permute-done.13.refs_3_ = bf16[128,1152]{1,0:T(8,128)(2,1)S(1)} collective-permute-done((bf16[128,1152]{1,0:T(8,128)(2,1)S(1)}, bf16[128,1152]{1,0:T(8,128)(2,1)S(1)}, u32[]{:S(2)}, u32[]{:S(2)}) %collective-permute-start.13) | collective-permute-done | bytes 294944 | tf_op jit(solution)/shard_map/second_tick/ppermute | solution.py:31
  126.8 0.8 second_tick.13
  (2 shorter events, 0.0 us)
Async XLA Ops:
  0.0 23.4 %copy-start.6 = (s32[1,2]{1,0:T(1,128)S(1)}, s32[1,2]{1,0:T(1,128)}, u32[]{:S(2)}) copy-start(s32[1,2]{1,0:T(1,128)} %param.13) | copy-start | bytes 28
  0.0 23.4 %copy-start.4 = (bf16[1,1024,288]{1,2,0:T(8,128)(2,1)S(1)}, bf16[1,1024,288]{1,2,0:T(8,128)(2,1)}, u32[]{:S(2)}) copy-start(bf16[1,1024,288]{1,2,0:T(8,128)(2,1)} %param.11) | copy-start | bytes 1769476
  1.1 9.2 %collective-permute-start = (bf16[64,1152]{1,0:T(8,128)(2,1)S(1)}, bf16[64,1152]{1,0:T(8,128)(2,1)S(1)}, u32[]{:S(2)}, u32[]{:S(2)}) collective-permute-start(bf16[64,1152]{1,0:T(8,128)(2,1)S(1)} %get-tuple-element.78), channel_id=1, source_target_pairs={{1,0},{0,1},{3,2},{2,3},{7,4},{6,5},{5,6},{4,7},{9,8},{8,9},{11,10... | collective-permute-start | bytes 442376 | tf_op jit(solution)/shard_map/first_gather/ppermute | solution.py:31
  7.1 12.1 %collective-permute-start.2 = (bf16[64,1152]{1,0:T(8,128)(2,1)S(1)}, bf16[64,1152]{1,0:T(8,128)(2,1)S(1)}, u32[]{:S(2)}, u32[]{:S(2)}) collective-permute-start(bf16[64,1152]{1,0:T(8,128)(2,1)S(1)} %get-tuple-element.77), channel_id=1, source_target_pairs={{1,0},{0,1},{3,2},{2,3},{7,4},{6,5},{5,6},{4,7},{9,8},{8,9},{11,10... | collective-permute-start | bytes 442376 | tf_op jit(solution)/shard_map/first_gather/ppermute | solution.py:31
  10.3 1.0 copy-start
  11.3 20.6 %collective-permute-start.1 = (bf16[128,1152]{1,0:T(8,128)(2,1)S(1)}, bf16[128,1152]{1,0:T(8,128)(2,1)S(1)}, u32[]{:S(2)}, u32[]{:S(2)}) collective-permute-start(bf16[128,1152]{1,0:T(8,128)(2,1)S(1)} %first_gather.2), channel_id=1, source_target_pairs={{3,0},{2,1},{1,2},{0,3},{5,4},{4,5},{7,6},{6,7},{11,8},{10,9},{9,1... | collective-permute-start | bytes 884744 | tf_op jit(solution)/shard_map/first_gather/ppermute | solution.py:31
  19.2 12.7 %copy-start.1 = (bf16[1,128,1152]{2,1,0:T(8,128)(2,1)S(1)}, bf16[1,128,1152]{2,1,0:T(8,128)(2,1)}, u32[]{:S(2)}) copy-start(bf16[1,128,1152]{2,1,0:T(8,128)(2,1)} %param.7) | copy-start | bytes 884740
  19.2 15.9 %collective-permute-start.3 = (bf16[128,1152]{1,0:T(8,128)(2,1)S(1)}, bf16[128,1152]{1,0:T(8,128)(2,1)S(1)}, u32[]{:S(2)}, u32[]{:S(2)}) collective-permute-start(bf16[128,1152]{1,0:T(8,128)(2,1)S(1)} %first_gather.3), channel_id=1, source_target_pairs={{3,0},{2,1},{1,2},{0,3},{5,4},{4,5},{7,6},{6,7},{11,8},{10,9},{9,1... | collective-permute-start | bytes 884744 | tf_op jit(solution)/shard_map/first_gather/ppermute | solution.py:31
  23.4 1.6 %copy-start.2 = (bf16[1,1152,3,288]{1,3,2,0:T(8,128)(2,1)S(1)}, bf16[1,1152,3,288]{1,3,2,0:T(8,128)(2,1)}, u32[]{:S(2)}) copy-start(bf16[1,1152,3,288]{1,3,2,0:T(8,128)(2,1)} %param.8) | copy-start | bytes 5971972
  24.9 1.1 copy-start.3
  26.0 1.1 copy-start.5
  27.9 24.2 %collective-permute-start.5 = (bf16[288,1152]{1,0:T(8,128)(2,1)S(1)}, bf16[288,1152]{1,0:T(8,128)(2,1)S(1)}, u32[]{:S(2)}, u32[]{:S(2)}) collective-permute-start(bf16[288,1152]{1,0:T(8,128)(2,1)S(1)} %bitcast.29), channel_id=1, source_target_pairs={{1,0},{0,1},{3,2},{2,3},{7,4},{6,5},{5,6},{4,7},{9,8},{8,9},{11,10... | collective-permute-start | bytes 1990664 | tf_op jit(solution)/shard_map/first_gather/ppermute | solution.py:31
  38.1 13.9 %collective-permute-start.4 = (bf16[288,256]{1,0:T(8,128)(2,1)S(1)}, bf16[288,256]{1,0:T(8,128)(2,1)S(1)}, u32[]{:S(2)}, u32[]{:S(2)}) collective-permute-start(bf16[288,256]{1,0:T(8,128)(2,1)S(1)} %get-tuple-element.54), channel_id=1, source_target_pairs={{1,0},{0,1},{3,2},{2,3},{7,4},{6,5},{5,6},{4,7},{9,8},{8,9},{11,10... | collective-permute-start | bytes 442376 | tf_op jit(solution)/shard_map/first_tick/ppermute | solution.py:31
  52.9 15.9 %collective-permute-start.8 = (bf16[128,1152]{1,0:T(8,128)(2,1)S(1)}, bf16[128,1152]{1,0:T(8,128)(2,1)S(1)}, u32[]{:S(2)}, u32[]{:S(2)}) collective-permute-start(bf16[128,1152]{1,0:T(8,128)(2,1)S(1)} %get-tuple-element.59), channel_id=1, source_target_pairs={{0,4},{1,5},{2,6},{3,7},{4,8},{5,9},{6,10},{7,11},{8,12},{9,13},{1... | collective-permute-start | bytes 884744 | tf_op jit(solution)/shard_map/second_tick/ppermute | solution.py:42
  55.4 17.3 %collective-permute-start.9 = (bf16[128,1152]{1,0:T(8,128)(2,1)S(1)}, bf16[128,1152]{1,0:T(8,128)(2,1)S(1)}, u32[]{:S(2)}, u32[]{:S(2)}) collective-permute-start(bf16[128,1152]{1,0:T(8,128)(2,1)S(1)} %get-tuple-element.60), channel_id=1, source_target_pairs={{0,7},{1,6},{2,5},{3,4},{4,9},{5,8},{6,11},{7,10},{8,15},{9,14},{1... | collective-permute-start | bytes 884744 | tf_op jit(solution)/shard_map/second_tick/ppermute | solution.py:42
  59.0 24.7 %collective-permute-start.6 = (bf16[128,1152]{1,0:T(8,128)(2,1)S(1)}, bf16[128,1152]{1,0:T(8,128)(2,1)S(1)}, u32[]{:S(2)}, u32[]{:S(2)}) collective-permute-start(bf16[128,1152]{1,0:T(8,128)(2,1)S(1)} %get-tuple-element.57), channel_id=1, source_target_pairs={{0,4},{1,5},{2,6},{3,7},{4,8},{5,9},{6,10},{7,11},{8,12},{9,13},{1... | collective-permute-start | bytes 884744 | tf_op jit(solution)/shard_map/second_tick/ppermute | solution.py:42
  62.0 21.7 %collective-permute-start.7 = (bf16[128,1152]{1,0:T(8,128)(2,1)S(1)}, bf16[128,1152]{1,0:T(8,128)(2,1)S(1)}, u32[]{:S(2)}, u32[]{:S(2)}) collective-permute-start(bf16[128,1152]{1,0:T(8,128)(2,1)S(1)} %get-tuple-element.58), channel_id=1, source_target_pairs={{0,7},{1,6},{2,5},{3,4},{4,9},{5,8},{6,11},{7,10},{8,15},{9,14},{1... | collective-permute-start | bytes 884744 | tf_op jit(solution)/shard_map/second_tick/ppermute | solution.py:42
  72.7 25.3 %collective-permute-start.11 = (bf16[128,1152]{1,0:T(8,128)(2,1)S(1)}, bf16[128,1152]{1,0:T(8,128)(2,1)S(1)}, u32[]{:S(2)}, u32[]{:S(2)}) collective-permute-start(bf16[128,1152]{1,0:T(8,128)(2,1)S(1)} %second_tick.8.refs_1_), channel_id=1, source_target_pairs={{3,0},{2,1},{1,2},{0,3},{5,4},{4,5},{7,6},{6,7},{11,8},{10,9},{9,1... | collective-permute-start | bytes 884744 | tf_op jit(solution)/shard_map/second_tick/ppermute | solution.py:31
  83.8 16.9 %collective-permute-start.10 = (bf16[128,1152]{1,0:T(8,128)(2,1)S(1)}, bf16[128,1152]{1,0:T(8,128)(2,1)S(1)}, u32[]{:S(2)}, u32[]{:S(2)}) collective-permute-start(bf16[128,1152]{1,0:T(8,128)(2,1)S(1)} %second_tick.7.refs_0_), channel_id=1, source_target_pairs={{3,0},{2,1},{1,2},{0,3},{5,4},{4,5},{7,6},{6,7},{11,8},{10,9},{9,1... | collective-permute-start | bytes 884744 | tf_op jit(solution)/shard_map/second_tick/ppermute | solution.py:31
  103.7 10.6 %collective-permute-start.12 = (bf16[288,256]{1,0:T(8,128)(2,1)S(1)}, bf16[288,256]{1,0:T(8,128)(2,1)S(1)}, u32[]{:S(2)}, u32[]{:S(2)}) collective-permute-start(bf16[288,256]{1,0:T(8,128)(2,1)S(1)} %get-tuple-element.74), channel_id=1, source_target_pairs={{1,0},{0,1},{3,2},{2,3},{7,4},{6,5},{5,6},{4,7},{9,8},{8,9},{11,10... | collective-permute-start | bytes 442376 | tf_op jit(solution)/shard_map/second_tick/ppermute | solution.py:31
  115.2 11.6 %collective-permute-start.13 = (bf16[128,1152]{1,0:T(8,128)(2,1)S(1)}, bf16[128,1152]{1,0:T(8,128)(2,1)S(1)}, u32[]{:S(2)}, u32[]{:S(2)}) collective-permute-start(bf16[128,1152]{1,0:T(8,128)(2,1)S(1)} %get-tuple-element.76), channel_id=1, source_target_pairs={{3,0},{2,1},{1,2},{0,3},{5,4},{4,5},{7,6},{6,7},{11,8},{10,9},{9,1... | collective-permute-start | bytes 884744 | tf_op jit(solution)/shard_map/second_tick/ppermute | solution.py:31

commit v5 on v4

--- a/solution.py
+++ b/solution.py
@@ -267,54 +267,48 @@
     return mine, theirs, (state[1], late_state[1], state[2], late_state[2]), also
 
 
-def both_sums(mine_ref, theirs_ref, w_mine_ref, w_theirs_ref):
-    return dot(mine_ref[...], w_mine_ref[...], 0, 0) + dot(theirs_ref[...], w_theirs_ref[...], 0, 0)
-
-
-def shift_kernel(spans, own_ref, other_a, other_b, mods_ref, *refs):
-    *refs, straight_a, crossing_a, straight_b, crossing_b = refs
-    half = straight_a.shape[0] // 2
-    added = mods_ref[2:3] * both_sums(*refs)
-    chunks = ((other_a, straight_a, crossing_a), (other_b, straight_b, crossing_b))
-    for i, ((first, last), (other, straight, crossing)) in enumerate(zip(spans, chunks, strict=True)):
-        at = 2 * i * half
-        own, one = added[at : at + half], added[at + half : at + 2 * half]
-        straight[:half] = (own_ref[first:last].astype(jnp.float32) + own).astype(jnp.bfloat16)
-        straight[half:] = (other[:half].astype(jnp.float32) + one).astype(jnp.bfloat16)
-        crossing[:half] = one.astype(jnp.bfloat16)
-        crossing[half:] = own.astype(jnp.bfloat16)
-
-
-def shift(spans, own, others, mods, mine, theirs, w_mine, w_theirs):
-    rows, features, width = mine.shape[1], w_mine.shape[1], mine.shape[0]
-    return call(
-        functools.partial(shift_kernel, spans), [shape(jnp.bfloat16, rows // 2, features)] * 4, [],
-        4 * rows * features * width, 0, (own, *others, mods, mine, theirs, w_mine, w_theirs),
-    )
-
-
-def join_kernel(crossing_ref, straight_ref, out_ref):
+def both_sums(first, last, mine_ref, theirs_ref, w_mine_ref, w_theirs_ref):
+    mine, theirs = (ref[:, first:last] for ref in (mine_ref, theirs_ref))
+    return dot(mine, w_mine_ref[...], 0, 0) + dot(theirs, w_theirs_ref[...], 0, 0)
+
+
+def shift_kernel(chunk, own_ref, other_ref, mods_ref, *refs):
+    *refs, straight_ref, crossing_ref = refs
+    half = own_ref.shape[0]
+    added = mods_ref[2:3] * both_sums(2 * chunk * half, (2 * chunk + 2) * half, *refs)
+    straight_ref[:half] = (own_ref[...].astype(jnp.float32) + added[:half]).astype(jnp.bfloat16)
+    straight_ref[half:] = (other_ref[:half].astype(jnp.float32) + added[half:]).astype(jnp.bfloat16)
+    crossing_ref[:half] = added[half:].astype(jnp.bfloat16)
+    crossing_ref[half:] = added[:half].astype(jnp.bfloat16)
+
+
+def shift(chunk, own, other, mods, mine, theirs, w_mine, w_theirs):
+    rows, features, width = 2 * own.shape[0], w_mine.shape[1], mine.shape[0]
+    return call(
+        functools.partial(shift_kernel, chunk), [shape(jnp.bfloat16, rows, features)] * 2, [],
+        4 * rows * features * width, 0, (own, other, mods, mine, theirs, w_mine, w_theirs),
+    )
+
+
+def join_kernel(straight_ref, crossing_ref, out_ref):
     total = straight_ref[...].astype(jnp.float32) + crossing_ref[...].astype(jnp.float32)
     out_ref[...] = total.astype(jnp.bfloat16)
 
 
-def join(crossing, straight):
-    return call(join_kernel, shape(straight.dtype, *straight.shape), [], straight.size, 0, (crossing, straight))
-
-
-def last_kernel(*refs):
-    *refs, kept_ref, sent_ref = refs
-    rows = kept_ref.shape[0]
-    total = both_sums(*refs)
-    kept_ref[...] = total[:rows]
-    sent_ref[...] = total[rows:].astype(jnp.bfloat16)
-
-
-def project_last(mine, theirs, w_mine, w_theirs):
+def join(straight, crossing):
+    return call(join_kernel, shape(straight.dtype, *straight.shape), [], straight.size, 0, (straight, crossing))
+
+
+def part_kernel(first, *refs):
+    *refs, out_ref = refs
+    out_ref[...] = both_sums(first, first + out_ref.shape[0], *refs).astype(out_ref.dtype)
+
+
+def part(first, dtype, mine, theirs, w_mine, w_theirs):
     rows, features, width = mine.shape[1] // 2, w_mine.shape[1], mine.shape[0]
     return call(
-        last_kernel, [shape(jnp.float32, rows, features), shape(jnp.bfloat16, rows, features)], [],
-        8 * rows * features * width, 0, (mine, theirs, w_mine, w_theirs),
+        functools.partial(part_kernel, first), shape(dtype, rows, features), [],
+        4 * rows * features * width, 0, (mine, theirs, w_mine, w_theirs),
     )
 
 
@@ -336,16 +330,27 @@
     )
 
 
-def pack_kernel(first, last, own_ref, zero_ref, out_ref):
-    half = last - first
-    out_ref[:half] = own_ref[first:last]
-    out_ref[half:] = zero_ref[...]
-
-
-def pack(own, first, last, zero):
-    return call(
-        functools.partial(pack_kernel, first, last),
-        shape(own.dtype, 2 * (last - first), own.shape[1]), [], 0, 0, (own, zero),
+def halve_kernel(own_ref, a_ref, b_ref):
+    half = a_ref.shape[0]
+    a_ref[...] = own_ref[:half]
+    b_ref[...] = own_ref[half:]
+
+
+def halve(own):
+    rows, features = own.shape
+    return call(halve_kernel, [shape(own.dtype, rows // 2, features)] * 2, [], 0, 0, (own,))
+
+
+def pack_kernel(first, own_ref, zero_ref, out_ref):
+    half = own_ref.shape[0]
+    out_ref[:half] = own_ref[...]
+    out_ref[half:] = zero_ref[first : first + half]
+
+
+def pack(own, first, zero):
+    rows, features = own.shape
+    return call(
+        functools.partial(pack_kernel, first), shape(own.dtype, 2 * rows, features), [], 0, 0, (own, zero)
     )
 
 
@@ -361,8 +366,9 @@
     spans = ((0, half), (half, rows))
 
     with jax.named_scope("first_gather"):
-        zeros = [exchange(own[first:last], 0) for first, last in spans]
-        packed = [pack(own, *span, zero) for span, zero in zip(spans, zeros, strict=True)]
+        zero = exchange(own, 0)
+        owns = halve(own)
+        packed = [pack(own_half, first, zero) for own_half, (first, _) in zip(owns, spans, strict=True)]
         others = [exchange(rows_here, 1) for rows_here in packed]
         w_sent, *_ = lax.optimization_barrier((w_sent, *packed))
         w_theirs = exchange(w_sent, 0)
@@ -371,19 +377,23 @@
             slots, modulation[0], w, out_weight[0], jnp.transpose(stale_keys[0]), jnp.transpose(stale_values[0])
         )
     with jax.named_scope("first_tick"):
-        places = [((0, 0, half), (1, half, rows), (2, *span), (1, 0, half)) for span in spans]
-        parts = [(zero, other, own) for zero, other in zip(zeros, others, strict=True)]
+        places = [((0, *span), (1, half, rows), (2, 0, half), (1, 0, half)) for span in spans]
+        parts = [(zero, other, own_half) for other, own_half in zip(others, owns, strict=True)]
         mine, theirs, olds, _ = block(*parts, places, (), mods, w, ko, vo)
-        straight_a, crossing_a, straight_b, crossing_b = shift(spans, own, others, mods, mine, theirs, w_mine, w_theirs)
+        shifted = [
+            shift(i, own_half, other, mods, mine, theirs, w_mine, w_theirs)
+            for i, (own_half, other) in enumerate(zip(owns, others, strict=True))
+        ]
     with jax.named_scope("second_tick"):
-        straights = [advance(straight, None) for straight in (straight_a, straight_b)]
-        crossings = [advance(crossing, 1) for crossing in (crossing_a, crossing_b)]
-        here = [join(straight, crossing) for crossing, straight in zip(crossings, straights, strict=True)]
+        straights = [advance(straight, None) for straight, _ in shifted]
+        crossings = [advance(crossing, 1) for _, crossing in shifted]
+        here = [join(straight, crossing) for straight, crossing in zip(straights, crossings, strict=True)]
         others = [exchange(rows_here, 1) for rows_here in here]
         places = [((0, half, rows), (1, half, rows), (0, 0, half), (1, 0, half))] * 2
         mine, theirs, *_ = block(here, others, places, (slots, *olds), mods, w, ko_next, vo_next)
-        mine_own, mine_one = project_last(mine, theirs, w_mine, w_theirs)
-        return update(here, ((0, 0, half), (1, 0, half)), mods, mine_own, exchange(mine_one, 1))[None]
+        from_one = exchange(part(rows, jnp.bfloat16, mine, theirs, w_mine, w_theirs), 1)
+        mine_own = part(0, jnp.float32, mine, theirs, w_mine, w_theirs)
+        return update(here, ((0, 0, half), (1, 0, half)), mods, mine_own, from_one)[None]
 
 
 def solution(mesh):

time: 128 us -> 127 us (level)
  the two profiles are of different devices: /device:TPU:128 before, /device:TPU:64 now
where the time goes in v5:
time: 127 us
  starting transfers between devices  65.4 us (51%)
  waiting for transfers between devices  36.5 us (29%)
  Pallas kernels  19.4 us (15%)
  local copies, waits for them, and re-layouts  4.97 us (4%)
    ppermute x9, starting transfers between devices, exchange(): return lax.ppermute(array, AXES, moves)  45.2 us
    ppermute x9, waiting for transfers between devices, exchange(): return lax.ppermute(array, AXES, moves)  35.3 us
    ppermute x4, starting transfers between devices, advance(): return lax.ppermute(array, AXES, moves)  20.2 us
    pallas_call x17, Pallas kernels, call(): pl.pallas_call(kernel, out_shape=outs, in_specs=specs, scratch_shapes=scr...  19.4 us
    unnamed x15, local copies, waits for them, and re-layouts  4.97 us
  transfers between devices with their start and end apart: 13, of which 7 were waited for; matrix products, arithmetic and copies ran while one was open for 1% of the time, Pallas kernels for 11%

profile of v5, /device:TPU:64, one launch (start us, length us, event | category | flops | bytes accessed | tf_op | source)
XLA Modules:
  0.0 126.5 jit_solution(8084906820405118389)
XLA Ops:
  0.0 0.0 copy-start.1
  0.0 0.0 copy-start.2
  0.0 6.2 %collective-permute-start = (bf16[128,1152]{1,0:T(8,128)(2,1)}, bf16[128,1152]{1,0:T(8,128)(2,1)S(1)}, u32[]{:S(2)}, u32[]{:S(2)}) collective-permute-start(bf16[128,1152]{1,0:T(8,128)(2,1)} %bitcast.23), channel_id=1, source_target_pairs={{1,0},{0,1},{3,2},{2,3},{7,4},{6,5},{5,6},{4,7},{9,8},{8,9},{11,10... | collective-permute-start | bytes 884744 | tf_op jit(solution)/shard_map/first_gather/ppermute | solution.py:31
  6.2 0.0 copy-start.4
  6.2 1.0 copy-done.4
  7.2 6.7 %collective-permute-done.zero_ref.refs_0_ = bf16[128,1152]{1,0:T(8,128)(2,1)S(1)} collective-permute-done((bf16[128,1152]{1,0:T(8,128)(2,1)}, bf16[128,1152]{1,0:T(8,128)(2,1)S(1)}, u32[]{:S(2)}, u32[]{:S(2)}) %collective-permute-start) | collective-permute-done | bytes 294944 | tf_op jit(solution)/shard_map/first_gather/ppermute | solution.py:31
  14.0 9.1 %collective-permute-start.1 = (bf16[128,1152]{1,0:T(8,128)(2,1)S(1)}, bf16[128,1152]{1,0:T(8,128)(2,1)S(1)}, u32[]{:S(2)}, u32[]{:S(2)}) collective-permute-start(bf16[128,1152]{1,0:T(8,128)(2,1)S(1)} %first_gather.4), channel_id=1, source_target_pairs={{3,0},{2,1},{1,2},{0,3},{5,4},{4,5},{7,6},{6,7},{11,8},{10,9},{9,1... | collective-permute-start | bytes 884744 | tf_op jit(solution)/shard_map/first_gather/ppermute | solution.py:31
  23.1 1.9 %collective-permute-start.2 = (bf16[128,1152]{1,0:T(8,128)(2,1)S(1)}, bf16[128,1152]{1,0:T(8,128)(2,1)S(1)}, u32[]{:S(2)}, u32[]{:S(2)}) collective-permute-start(bf16[128,1152]{1,0:T(8,128)(2,1)S(1)} %first_gather.5), channel_id=1, source_target_pairs={{3,0},{2,1},{1,2},{0,3},{5,4},{4,5},{7,6},{6,7},{11,8},{10,9},{9,1... | collective-permute-start | bytes 884744 | tf_op jit(solution)/shard_map/first_gather/ppermute | solution.py:31
  25.0 0.7 copy.10
  25.8 0.0 copy-done.1
  25.8 0.0 copy-done.2
  25.8 0.0 copy-start
  25.8 1.5 %copy-done = bf16[1,1152,3,288]{1,3,2,0:T(8,128)(2,1)S(1)} copy-done((bf16[1,1152,3,288]{1,3,2,0:T(8,128)(2,1)S(1)}, bf16[1,1152,3,288]{1,3,2,0:T(8,128)(2,1)}, u32[]{:S(2)}) %copy-start) | copy-done | bytes 1990680
  27.3 0.0 copy-start.3
  27.3 1.1 copy-done.3
  28.4 0.0 copy-start.5
  28.4 0.7 copy-done.5
  29.0 0.8 prepare.1
  29.9 2.4 %collective-permute-start.4 = (bf16[288,1152]{1,0:T(8,128)(2,1)S(1)}, bf16[288,1152]{1,0:T(8,128)(2,1)S(1)}, u32[]{:S(2)}, u32[]{:S(2)}) collective-permute-start(bf16[288,1152]{1,0:T(8,128)(2,1)S(1)} %bitcast.20), channel_id=1, source_target_pairs={{1,0},{0,1},{3,2},{2,3},{7,4},{6,5},{5,6},{4,7},{9,8},{8,9},{11,10... | collective-permute-start | bytes 1990664 | tf_op jit(solution)/shard_map/first_gather/ppermute | solution.py:31
  32.3 0.0 collective-permute-done.1.refs_1_.other_ref
  32.3 3.1 %first_tick.5 = (bf16[4,72,256]{2,1,0:T(8,128)(2,1)S(1)}, bf16[4,72,256]{2,1,0:T(8,128)(2,1)S(1)}, bf16[4,72,256]{2,1,0:T(8,128)(2,1)S(1)}, f32[8,256]{1,0:T(8,1...) custom-call(bf16[128,1152]{1,0:T(8,128)(2,1)S(1)} %collective-permute-done.zero_ref.refs_0_, ...), custom_call_target="tpu_custom_call" | custom-call | flops 736100352 | bytes 4194304 | tf_op jit(solution)/shard_map/first_tick/pallas_call | solution.py:90
  35.4 1.4 %collective-permute-done.2.refs_1_.other_ref = bf16[128,1152]{1,0:T(8,128)(2,1)S(1)} collective-permute-done((bf16[128,1152]{1,0:T(8,128)(2,1)S(1)}, bf16[128,1152]{1,0:T(8,128)(2,1)S(1)}, u32[]{:S(2)}, u32[]{:S(2)}) %collective-permute-start.2) | collective-permute-done | bytes 294944 | tf_op jit(solution)/shard_map/first_gather/ppermute | solution.py:31
  36.8 3.0 %first_tick.6 = (bf16[288,256]{1,0:T(8,128)(2,1)S(1)}, bf16[4,72,256]{2,1,0:T(8,128)(2,1)S(1)}, bf16[4,72,256]{2,1,0:T(8,128)(2,1)S(1)}, bf16[4,72,256]{2,1,0:T(8,128)(2,1)S(1)}) custom-call(bf16[128,1152]{1,0:T(8,128)(2,1)S(1)} %collective-permute-done.zero_ref.refs_0_, bf16[128,1152]{1,0:T(8,128)(2,1)S(1)} %collective-permute-done.2.refs_1_.other_ref, ...), custom_call_target="tpu_custom_call" | custom-call | flops 660602880 | bytes 4194304 | tf_op jit(solution)/shard_map/first_tick/pallas_call | solution.py:90
  39.8 2.9 %collective-permute-start.3 = (bf16[288,256]{1,0:T(8,128)(2,1)S(1)}, bf16[288,256]{1,0:T(8,128)(2,1)S(1)}, u32[]{:S(2)}, u32[]{:S(2)}) collective-permute-start(bf16[288,256]{1,0:T(8,128)(2,1)S(1)} %get-tuple-element.56), channel_id=1, source_target_pairs={{1,0},{0,1},{3,2},{2,3},{7,4},{6,5},{5,6},{4,7},{9,8},{8,9},{11,10... | collective-permute-start | bytes 442376 | tf_op jit(solution)/shard_map/first_tick/ppermute | solution.py:31
  42.8 1.2 first_tick.7.refs_0_
  43.9 8.7 %collective-permute-done.3.refs_1_ = bf16[288,256]{1,0:T(8,128)(2,1)S(1)} collective-permute-done((bf16[288,256]{1,0:T(8,128)(2,1)S(1)}, bf16[288,256]{1,0:T(8,128)(2,1)S(1)}, u32[]{:S(2)}, u32[]{:S(2)}) %collective-permute-start.3) | collective-permute-done | bytes 147488 | tf_op jit(solution)/shard_map/first_tick/ppermute | solution.py:31
  52.7 0.0 collective-permute-done.4.refs_3_
  52.7 0.5 first_tick.9
  53.2 0.0 copy-start.6
  53.2 1.9 %collective-permute-start.7 = (bf16[128,1152]{1,0:T(8,128)(2,1)S(1)}, bf16[128,1152]{1,0:T(8,128)(2,1)S(1)}, u32[]{:S(2)}, u32[]{:S(2)}) collective-permute-start(bf16[128,1152]{1,0:T(8,128)(2,1)S(1)} %get-tuple-element.61), channel_id=1, source_target_pairs={{0,4},{1,5},{2,6},{3,7},{4,8},{5,9},{6,10},{7,11},{8,12},{9,13},{1... | collective-permute-start | bytes 884744 | tf_op jit(solution)/shard_map/second_tick/ppermute | solution.py:42
  55.2 8.8 %collective-permute-start.8 = (bf16[128,1152]{1,0:T(8,128)(2,1)S(1)}, bf16[128,1152]{1,0:T(8,128)(2,1)S(1)}, u32[]{:S(2)}, u32[]{:S(2)}) collective-permute-start(bf16[128,1152]{1,0:T(8,128)(2,1)S(1)} %get-tuple-element.62), channel_id=1, source_target_pairs={{0,7},{1,6},{2,5},{3,4},{4,9},{5,8},{6,11},{7,10},{8,15},{9,14},{1... | collective-permute-start | bytes 884744 | tf_op jit(solution)/shard_map/second_tick/ppermute | solution.py:42
  63.9 0.5 first_tick.8
  64.5 2.6 %collective-permute-start.5 = (bf16[128,1152]{1,0:T(8,128)(2,1)S(1)}, bf16[128,1152]{1,0:T(8,128)(2,1)S(1)}, u32[]{:S(2)}, u32[]{:S(2)}) collective-permute-start(bf16[128,1152]{1,0:T(8,128)(2,1)S(1)} %get-tuple-element.59), channel_id=1, source_target_pairs={{0,4},{1,5},{2,6},{3,7},{4,8},{5,9},{6,10},{7,11},{8,12},{9,13},{1... | collective-permute-start | bytes 884744 | tf_op jit(solution)/shard_map/second_tick/ppermute | solution.py:42
  67.1 6.8 %collective-permute-start.6 = (bf16[128,1152]{1,0:T(8,128)(2,1)S(1)}, bf16[128,1152]{1,0:T(8,128)(2,1)S(1)}, u32[]{:S(2)}, u32[]{:S(2)}) collective-permute-start(bf16[128,1152]{1,0:T(8,128)(2,1)S(1)} %get-tuple-element.60), channel_id=1, source_target_pairs={{0,7},{1,6},{2,5},{3,4},{4,9},{5,8},{6,11},{7,10},{8,15},{9,14},{1... | collective-permute-start | bytes 884744 | tf_op jit(solution)/shard_map/second_tick/ppermute | solution.py:42
  74.0 0.0 collective-permute-done.7.straight_ref
  74.0 0.0 collective-permute-done.8.crossing_ref
  74.0 0.1 second_tick.9.refs_1_
  74.1 6.8 %collective-permute-start.10 = (bf16[128,1152]{1,0:T(8,128)(2,1)S(1)}, bf16[128,1152]{1,0:T(8,128)(2,1)S(1)}, u32[]{:S(2)}, u32[]{:S(2)}) collective-permute-start(bf16[128,1152]{1,0:T(8,128)(2,1)S(1)} %second_tick.9.refs_1_), channel_id=1, source_target_pairs={{3,0},{2,1},{1,2},{0,3},{5,4},{4,5},{7,6},{6,7},{11,8},{10,9},{9,1... | collective-permute-start | bytes 884744 | tf_op jit(solution)/shard_map/second_tick/ppermute | solution.py:31
  80.9 0.0 collective-permute-done.5.straight_ref
  80.9 1.3 collective-permute-done.6.crossing_ref
  82.2 0.1 second_tick.8.refs_0_
  82.2 6.9 %collective-permute-start.9 = (bf16[128,1152]{1,0:T(8,128)(2,1)S(1)}, bf16[128,1152]{1,0:T(8,128)(2,1)S(1)}, u32[]{:S(2)}, u32[]{:S(2)}) collective-permute-start(bf16[128,1152]{1,0:T(8,128)(2,1)S(1)} %second_tick.8.refs_0_), channel_id=1, source_target_pairs={{3,0},{2,1},{1,2},{0,3},{5,4},{4,5},{7,6},{6,7},{11,8},{10,9},{9,1... | collective-permute-start | bytes 884744 | tf_op jit(solution)/shard_map/second_tick/ppermute | solution.py:31
  89.1 0.0 copy-done.6
  89.2 3.9 %second_tick.10 = (bf16[4,72,256]{2,1,0:T(8,128)(2,1)S(1)}, bf16[4,72,256]{2,1,0:T(8,128)(2,1)S(1)}, bf16[4,72,256]{2,1,0:T(8,128)(2,1)S(1)}, f32[8,256]{1,0:T(8...) custom-call(bf16[128,1152]{1,0:T(8,128)(2,1)S(1)} %second_tick.8.ref, ...), custom_call_target="tpu_custom_call" | custom-call | flops 736100352 | bytes 4194304 | tf_op jit(solution)/shard_map/second_tick/pallas_call | solution.py:90
  93.1 0.0 collective-permute-done.10.refs_1_
  93.1 0.7 collective-permute-done.9.refs_0_
  93.8 3.0 %second_tick.11 = (bf16[288,256]{1,0:T(8,128)(2,1)S(1)}, bf16[4,72,256]{2,1,0:T(8,128)(2,1)S(1)}, bf16[4,72,256]{2,1,0:T(8,128)(2,1)S(1)}, bf16[4,72,256]{2,1,0:T(8,128)(2,1)S(1)}) custom-call(bf16[128,1152]{1,0:T(8,128)(2,1)S(1)} %collective-permute-done.9.refs_0_, bf16[128,1152]{1,0:T(8,128)(2,1)S(1)} %collective-permute-done.10.refs_1_, ...), custom_call_target="tpu_custom_call" | custom-call | flops 660602880 | bytes 4194304 | tf_op jit(solution)/shard_map/second_tick/pallas_call | solution.py:90
  96.8 7.0 %collective-permute-start.11 = (bf16[288,256]{1,0:T(8,128)(2,1)S(1)}, bf16[288,256]{1,0:T(8,128)(2,1)S(1)}, u32[]{:S(2)}, u32[]{:S(2)}) collective-permute-start(bf16[288,256]{1,0:T(8,128)(2,1)S(1)} %get-tuple-element.76), channel_id=1, source_target_pairs={{1,0},{0,1},{3,2},{2,3},{7,4},{6,5},{5,6},{4,7},{9,8},{8,9},{11,10... | collective-permute-start | bytes 442376 | tf_op jit(solution)/shard_map/second_tick/ppermute | solution.py:31
  103.8 1.2 second_tick.12.refs_0_
  105.1 6.2 %collective-permute-done.11.refs_1_ = bf16[288,256]{1,0:T(8,128)(2,1)S(1)} collective-permute-done((bf16[288,256]{1,0:T(8,128)(2,1)S(1)}, bf16[288,256]{1,0:T(8,128)(2,1)S(1)}, u32[]{:S(2)}, u32[]{:S(2)}) %collective-permute-start.11) | collective-permute-done | bytes 147488 | tf_op jit(solution)/shard_map/second_tick/ppermute | solution.py:31
  111.3 0.5 second_tick.14
  111.8 1.9 %collective-permute-start.12 = (bf16[128,1152]{1,0:T(8,128)(2,1)S(1)}, bf16[128,1152]{1,0:T(8,128)(2,1)S(1)}, u32[]{:S(2)}, u32[]{:S(2)}) collective-permute-start(bf16[128,1152]{1,0:T(8,128)(2,1)S(1)} %second_tick.14), channel_id=1, source_target_pairs={{3,0},{2,1},{1,2},{0,3},{5,4},{4,5},{7,6},{6,7},{11,8},{10,9},{9,1... | collective-permute-start | bytes 884744 | tf_op jit(solution)/shard_map/second_tick/ppermute | solution.py:31
  113.7 0.5 second_tick.13.refs_2_
  114.3 11.4 %collective-permute-done.12.refs_3_ = bf16[128,1152]{1,0:T(8,128)(2,1)S(1)} collective-permute-done((bf16[128,1152]{1,0:T(8,128)(2,1)S(1)}, bf16[128,1152]{1,0:T(8,128)(2,1)S(1)}, u32[]{:S(2)}, u32[]{:S(2)}) %collective-permute-start.12) | collective-permute-done | bytes 294944 | tf_op jit(solution)/shard_map/second_tick/ppermute | solution.py:31
  125.7 0.8 second_tick.15
  (3 shorter events, 0.1 us)
Async XLA Ops:
  0.0 25.8 %copy-start.1 = (bf16[1,288,1152]{2,1,0:T(8,128)(2,1)S(1)}, bf16[1,288,1152]{2,1,0:T(8,128)(2,1)}, u32[]{:S(2)}) copy-start(bf16[1,288,1152]{2,1,0:T(8,128)(2,1)} %param.9) | copy-start | bytes 1990660
  0.0 25.8 %copy-start.2 = (bf16[1,1024,288]{1,2,0:T(8,128)(2,1)S(1)}, bf16[1,1024,288]{1,2,0:T(8,128)(2,1)}, u32[]{:S(2)}) copy-start(bf16[1,1024,288]{1,2,0:T(8,128)(2,1)} %param.11) | copy-start | bytes 1769476
  0.0 14.0 %collective-permute-start = (bf16[128,1152]{1,0:T(8,128)(2,1)}, bf16[128,1152]{1,0:T(8,128)(2,1)S(1)}, u32[]{:S(2)}, u32[]{:S(2)}) collective-permute-start(bf16[128,1152]{1,0:T(8,128)(2,1)} %bitcast.23), channel_id=1, source_target_pairs={{1,0},{0,1},{3,2},{2,3},{7,4},{6,5},{5,6},{4,7},{9,8},{8,9},{11,10... | collective-permute-start | bytes 884744 | tf_op jit(solution)/shard_map/first_gather/ppermute | solution.py:31
  6.2 1.0 copy-start.4
  14.0 18.3 %collective-permute-start.1 = (bf16[128,1152]{1,0:T(8,128)(2,1)S(1)}, bf16[128,1152]{1,0:T(8,128)(2,1)S(1)}, u32[]{:S(2)}, u32[]{:S(2)}) collective-permute-start(bf16[128,1152]{1,0:T(8,128)(2,1)S(1)} %first_gather.4), channel_id=1, source_target_pairs={{3,0},{2,1},{1,2},{0,3},{5,4},{4,5},{7,6},{6,7},{11,8},{10,9},{9,1... | collective-permute-start | bytes 884744 | tf_op jit(solution)/shard_map/first_gather/ppermute | solution.py:31
  23.1 13.7 %collective-permute-start.2 = (bf16[128,1152]{1,0:T(8,128)(2,1)S(1)}, bf16[128,1152]{1,0:T(8,128)(2,1)S(1)}, u32[]{:S(2)}, u32[]{:S(2)}) collective-permute-start(bf16[128,1152]{1,0:T(8,128)(2,1)S(1)} %first_gather.5), channel_id=1, source_target_pairs={{3,0},{2,1},{1,2},{0,3},{5,4},{4,5},{7,6},{6,7},{11,8},{10,9},{9,1... | collective-permute-start | bytes 884744 | tf_op jit(solution)/shard_map/first_gather/ppermute | solution.py:31
  25.8 1.6 %copy-start = (bf16[1,1152,3,288]{1,3,2,0:T(8,128)(2,1)S(1)}, bf16[1,1152,3,288]{1,3,2,0:T(8,128)(2,1)}, u32[]{:S(2)}) copy-start(bf16[1,1152,3,288]{1,3,2,0:T(8,128)(2,1)} %param.8) | copy-start | bytes 5971972
  27.3 1.1 copy-start.3
  28.4 0.7 copy-start.5
  29.9 22.8 %collective-permute-start.4 = (bf16[288,1152]{1,0:T(8,128)(2,1)S(1)}, bf16[288,1152]{1,0:T(8,128)(2,1)S(1)}, u32[]{:S(2)}, u32[]{:S(2)}) collective-permute-start(bf16[288,1152]{1,0:T(8,128)(2,1)S(1)} %bitcast.20), channel_id=1, source_target_pairs={{1,0},{0,1},{3,2},{2,3},{7,4},{6,5},{5,6},{4,7},{9,8},{8,9},{11,10... | collective-permute-start | bytes 1990664 | tf_op jit(solution)/shard_map/first_gather/ppermute | solution.py:31
  39.8 12.9 %collective-permute-start.3 = (bf16[288,256]{1,0:T(8,128)(2,1)S(1)}, bf16[288,256]{1,0:T(8,128)(2,1)S(1)}, u32[]{:S(2)}, u32[]{:S(2)}) collective-permute-start(bf16[288,256]{1,0:T(8,128)(2,1)S(1)} %get-tuple-element.56), channel_id=1, source_target_pairs={{1,0},{0,1},{3,2},{2,3},{7,4},{6,5},{5,6},{4,7},{9,8},{8,9},{11,10... | collective-permute-start | bytes 442376 | tf_op jit(solution)/shard_map/first_tick/ppermute | solution.py:31
  53.2 35.9 %copy-start.6 = (s32[1,2]{1,0:T(1,128)S(1)}, s32[1,2]{1,0:T(1,128)}, u32[]{:S(2)}) copy-start(s32[1,2]{1,0:T(1,128)} %param.13) | copy-start | bytes 28
  53.2 20.8 %collective-permute-start.7 = (bf16[128,1152]{1,0:T(8,128)(2,1)S(1)}, bf16[128,1152]{1,0:T(8,128)(2,1)S(1)}, u32[]{:S(2)}, u32[]{:S(2)}) collective-permute-start(bf16[128,1152]{1,0:T(8,128)(2,1)S(1)} %get-tuple-element.61), channel_id=1, source_target_pairs={{0,4},{1,5},{2,6},{3,7},{4,8},{5,9},{6,10},{7,11},{8,12},{9,13},{1... | collective-permute-start | bytes 884744 | tf_op jit(solution)/shard_map/second_tick/ppermute | solution.py:42
  55.2 18.9 %collective-permute-start.8 = (bf16[128,1152]{1,0:T(8,128)(2,1)S(1)}, bf16[128,1152]{1,0:T(8,128)(2,1)S(1)}, u32[]{:S(2)}, u32[]{:S(2)}) collective-permute-start(bf16[128,1152]{1,0:T(8,128)(2,1)S(1)} %get-tuple-element.62), channel_id=1, source_target_pairs={{0,7},{1,6},{2,5},{3,4},{4,9},{5,8},{6,11},{7,10},{8,15},{9,14},{1... | collective-permute-start | bytes 884744 | tf_op jit(solution)/shard_map/second_tick/ppermute | solution.py:42
  64.5 16.4 %collective-permute-start.5 = (bf16[128,1152]{1,0:T(8,128)(2,1)S(1)}, bf16[128,1152]{1,0:T(8,128)(2,1)S(1)}, u32[]{:S(2)}, u32[]{:S(2)}) collective-permute-start(bf16[128,1152]{1,0:T(8,128)(2,1)S(1)} %get-tuple-element.59), channel_id=1, source_target_pairs={{0,4},{1,5},{2,6},{3,7},{4,8},{5,9},{6,10},{7,11},{8,12},{9,13},{1... | collective-permute-start | bytes 884744 | tf_op jit(solution)/shard_map/second_tick/ppermute | solution.py:42
  67.1 15.0 %collective-permute-start.6 = (bf16[128,1152]{1,0:T(8,128)(2,1)S(1)}, bf16[128,1152]{1,0:T(8,128)(2,1)S(1)}, u32[]{:S(2)}, u32[]{:S(2)}) collective-permute-start(bf16[128,1152]{1,0:T(8,128)(2,1)S(1)} %get-tuple-element.60), channel_id=1, source_target_pairs={{0,7},{1,6},{2,5},{3,4},{4,9},{5,8},{6,11},{7,10},{8,15},{9,14},{1... | collective-permute-start | bytes 884744 | tf_op jit(solution)/shard_map/second_tick/ppermute | solution.py:42
  74.1 19.0 %collective-permute-start.10 = (bf16[128,1152]{1,0:T(8,128)(2,1)S(1)}, bf16[128,1152]{1,0:T(8,128)(2,1)S(1)}, u32[]{:S(2)}, u32[]{:S(2)}) collective-permute-start(bf16[128,1152]{1,0:T(8,128)(2,1)S(1)} %second_tick.9.refs_1_), channel_id=1, source_target_pairs={{3,0},{2,1},{1,2},{0,3},{5,4},{4,5},{7,6},{6,7},{11,8},{10,9},{9,1... | collective-permute-start | bytes 884744 | tf_op jit(solution)/shard_map/second_tick/ppermute | solution.py:31
  82.2 11.6 %collective-permute-start.9 = (bf16[128,1152]{1,0:T(8,128)(2,1)S(1)}, bf16[128,1152]{1,0:T(8,128)(2,1)S(1)}, u32[]{:S(2)}, u32[]{:S(2)}) collective-permute-start(bf16[128,1152]{1,0:T(8,128)(2,1)S(1)} %second_tick.8.refs_0_), channel_id=1, source_target_pairs={{3,0},{2,1},{1,2},{0,3},{5,4},{4,5},{7,6},{6,7},{11,8},{10,9},{9,1... | collective-permute-start | bytes 884744 | tf_op jit(solution)/shard_map/second_tick/ppermute | solution.py:31
  96.8 14.4 %collective-permute-start.11 = (bf16[288,256]{1,0:T(8,128)(2,1)S(1)}, bf16[288,256]{1,0:T(8,128)(2,1)S(1)}, u32[]{:S(2)}, u32[]{:S(2)}) collective-permute-start(bf16[288,256]{1,0:T(8,128)(2,1)S(1)} %get-tuple-element.76), channel_id=1, source_target_pairs={{1,0},{0,1},{3,2},{2,3},{7,4},{6,5},{5,6},{4,7},{9,8},{8,9},{11,10... | collective-permute-start | bytes 442376 | tf_op jit(solution)/shard_map/second_tick/ppermute | solution.py:31
  111.8 13.9 %collective-permute-start.12 = (bf16[128,1152]{1,0:T(8,128)(2,1)S(1)}, bf16[128,1152]{1,0:T(8,128)(2,1)S(1)}, u32[]{:S(2)}, u32[]{:S(2)}) collective-permute-start(bf16[128,1152]{1,0:T(8,128)(2,1)S(1)} %second_tick.14), channel_id=1, source_target_pairs={{3,0},{2,1},{1,2},{0,3},{5,4},{4,5},{7,6},{6,7},{11,8},{10,9},{9,1... | collective-permute-start | bytes 884744 | tf_op jit(solution)/shard_map/second_tick/ppermute | solution.py:31

commit v6 on v5

--- a/solution.py
+++ b/solution.py
@@ -10,6 +10,7 @@
 
 HEAD_DIM = 72
 AXES = ("pipe", "seq")
+SMALL_CHUNK = 6
 VMEM_BYTES = 24 * 2**20
 EXPONENT = math.log2(math.e) / math.sqrt(HEAD_DIM)
 
@@ -272,21 +273,28 @@
     return dot(mine, w_mine_ref[...], 0, 0) + dot(theirs, w_theirs_ref[...], 0, 0)
 
 
-def shift_kernel(chunk, own_ref, other_ref, mods_ref, *refs):
-    *refs, straight_ref, crossing_ref = refs
-    half = own_ref.shape[0]
-    added = mods_ref[2:3] * both_sums(2 * chunk * half, (2 * chunk + 2) * half, *refs)
-    straight_ref[:half] = (own_ref[...].astype(jnp.float32) + added[:half]).astype(jnp.bfloat16)
-    straight_ref[half:] = (other_ref[:half].astype(jnp.float32) + added[half:]).astype(jnp.bfloat16)
-    crossing_ref[:half] = added[half:].astype(jnp.bfloat16)
-    crossing_ref[half:] = added[:half].astype(jnp.bfloat16)
-
-
-def shift(chunk, own, other, mods, mine, theirs, w_mine, w_theirs):
-    rows, features, width = 2 * own.shape[0], w_mine.shape[1], mine.shape[0]
-    return call(
-        functools.partial(shift_kernel, chunk), [shape(jnp.bfloat16, rows, features)] * 2, [],
-        4 * rows * features * width, 0, (own, other, mods, mine, theirs, w_mine, w_theirs),
+def shift_kernel(spans, own_a, own_b, other_a, other_b, mods_ref, *refs):
+    refs, outs = refs[:4], refs[4:]
+    half = own_a.shape[0]
+    added = mods_ref[2:3] * both_sums(0, 4 * half, *refs)
+    own_added = jnp.concatenate([added[:half], added[2 * half : 3 * half]], axis=0)
+    one_added = jnp.concatenate([added[half : 2 * half], added[3 * half :]], axis=0)
+    own = jnp.concatenate([own_a[...], own_b[...]], axis=0).astype(jnp.float32) + own_added
+    one = jnp.concatenate([other_a[:half], other_b[:half]], axis=0).astype(jnp.float32) + one_added
+    for (first, last), straight_ref, crossing_ref in zip(spans, outs[::2], outs[1::2], strict=True):
+        size = last - first
+        straight_ref[:size] = own[first:last].astype(jnp.bfloat16)
+        straight_ref[size:] = one[first:last].astype(jnp.bfloat16)
+        crossing_ref[:size] = one_added[first:last].astype(jnp.bfloat16)
+        crossing_ref[size:] = own_added[first:last].astype(jnp.bfloat16)
+
+
+def shift(spans, owns, others, mods, mine, theirs, w_mine, w_theirs):
+    rows, features, width = mine.shape[1], w_mine.shape[1], mine.shape[0]
+    outs = [shape(jnp.bfloat16, 2 * (last - first), features) for first, last in spans for _ in range(2)]
+    return call(
+        functools.partial(shift_kernel, spans), outs, [],
+        4 * rows * features * width, 0, (*owns, *others, mods, mine, theirs, w_mine, w_theirs),
     )
 
 
@@ -380,20 +388,22 @@
         places = [((0, *span), (1, half, rows), (2, 0, half), (1, 0, half)) for span in spans]
         parts = [(zero, other, own_half) for other, own_half in zip(others, owns, strict=True)]
         mine, theirs, olds, _ = block(*parts, places, (), mods, w, ko, vo)
-        shifted = [
-            shift(i, own_half, other, mods, mine, theirs, w_mine, w_theirs)
-            for i, (own_half, other) in enumerate(zip(owns, others, strict=True))
-        ]
+        cut = rows * SMALL_CHUNK // 16
+        spans = ((0, cut), (cut, rows))
+        shifted = shift(spans, owns, others, mods, mine, theirs, w_mine, w_theirs)
     with jax.named_scope("second_tick"):
-        straights = [advance(straight, None) for straight, _ in shifted]
-        crossings = [advance(crossing, 1) for _, crossing in shifted]
+        straights = [advance(straight, None) for straight in shifted[::2]]
+        crossings = [advance(crossing, 1) for crossing in shifted[1::2]]
         here = [join(straight, crossing) for straight, crossing in zip(straights, crossings, strict=True)]
         others = [exchange(rows_here, 1) for rows_here in here]
-        places = [((0, half, rows), (1, half, rows), (0, 0, half), (1, 0, half))] * 2
+        sizes = [last - first for first, last in spans]
+        places = [(i, size, 2 * size) for i, size in enumerate(sizes)] + [(i, 0, size) for i, size in enumerate(sizes)]
+        places = [tuple(places)] * 2
         mine, theirs, *_ = block(here, others, places, (slots, *olds), mods, w, ko_next, vo_next)
         from_one = exchange(part(rows, jnp.bfloat16, mine, theirs, w_mine, w_theirs), 1)
         mine_own = part(0, jnp.float32, mine, theirs, w_mine, w_theirs)
-        return update(here, ((0, 0, half), (1, 0, half)), mods, mine_own, from_one)[None]
+        own_rows = tuple((i, 0, size) for i, size in enumerate(sizes))
+        return update(here, own_rows, mods, mine_own, from_one)[None]
 
 
 def solution(mesh):

time: 127 us -> 127 us (level)
  waiting for transfers between devices: 36.5 us -> 30.4 us
  starting transfers between devices: 65.4 us -> 71 us
    ppermute x9, starting transfers between devices: 45.2 us -> 50.8 us  [exchange(): return lax.ppermute(array, AXES, moves)]
    ppermute x9, waiting for transfers between devices: 35.3 us -> 30.4 us  [exchange(): return lax.ppermute(array, AXES, moves)]
    pallas_call x17 -> x16, Pallas kernels: 19.4 us -> 19.3 us  [call(): pl.pallas_call(kernel, out_shape=outs, in_specs=specs, scratch_shapes=scr...]
  transfers between devices with their start and end apart: 13 -> 13, of which waited for: 7 -> 6; matrix products, arithmetic and copies ran while one was open for 1% -> 1% of each run, Pallas kernels for 11% -> 11%
where the time goes in v6:
time: 127 us; the launch traced here: 126 us
  starting transfers between devices  71 us (56%)
  waiting for transfers between devices  30.4 us (24%)
  Pallas kernels  19.3 us (15%)
  local copies, waits for them, and re-layouts  4.96 us (4%)
    ppermute x9, starting transfers between devices, exchange(): return lax.ppermute(array, AXES, moves)  50.8 us
    ppermute x9, waiting for transfers between devices, exchange(): return lax.ppermute(array, AXES, moves)  30.4 us
    ppermute x4, starting transfers between devices, advance(): return lax.ppermute(array, AXES, moves)  20.2 us
    pallas_call x16, Pallas kernels, call(): pl.pallas_call(kernel, out_shape=outs, in_specs=specs, scratch_shapes=scr...  19.3 us
    unnamed x15, local copies, waits for them, and re-layouts  4.96 us
  transfers between devices with their start and end apart: 13, of which 6 were waited for; matrix products, arithmetic and copies ran while one was open for 1% of the time, Pallas kernels for 11%

profile of v6, /device:TPU:64, one launch (start us, length us, event | category | flops | bytes accessed | tf_op | source)
XLA Modules:
  0.0 125.9 jit_solution(3791038382442068942)
XLA Ops:
  0.0 0.0 copy-start.1
  0.0 0.0 copy-start.2
  0.0 6.2 %collective-permute-start = (bf16[128,1152]{1,0:T(8,128)(2,1)}, bf16[128,1152]{1,0:T(8,128)(2,1)S(1)}, u32[]{:S(2)}, u32[]{:S(2)}) collective-permute-start(bf16[128,1152]{1,0:T(8,128)(2,1)} %bitcast.23), channel_id=1, source_target_pairs={{1,0},{0,1},{3,2},{2,3},{7,4},{6,5},{5,6},{4,7},{9,8},{8,9},{11,10... | collective-permute-start | bytes 884744 | tf_op jit(solution)/shard_map/first_gather/ppermute | solution.py:32
  6.2 0.0 copy-start.4
  6.2 1.0 copy-done.4
  7.2 6.7 %collective-permute-done.zero_ref.refs_0_ = bf16[128,1152]{1,0:T(8,128)(2,1)S(1)} collective-permute-done((bf16[128,1152]{1,0:T(8,128)(2,1)}, bf16[128,1152]{1,0:T(8,128)(2,1)S(1)}, u32[]{:S(2)}, u32[]{:S(2)}) %collective-permute-start) | collective-permute-done | bytes 294944 | tf_op jit(solution)/shard_map/first_gather/ppermute | solution.py:32
  14.0 9.1 %collective-permute-start.1 = (bf16[128,1152]{1,0:T(8,128)(2,1)S(1)}, bf16[128,1152]{1,0:T(8,128)(2,1)S(1)}, u32[]{:S(2)}, u32[]{:S(2)}) collective-permute-start(bf16[128,1152]{1,0:T(8,128)(2,1)S(1)} %first_gather.4), channel_id=1, source_target_pairs={{3,0},{2,1},{1,2},{0,3},{5,4},{4,5},{7,6},{6,7},{11,8},{10,9},{9,1... | collective-permute-start | bytes 884744 | tf_op jit(solution)/shard_map/first_gather/ppermute | solution.py:32
  23.1 1.9 %collective-permute-start.2 = (bf16[128,1152]{1,0:T(8,128)(2,1)S(1)}, bf16[128,1152]{1,0:T(8,128)(2,1)S(1)}, u32[]{:S(2)}, u32[]{:S(2)}) collective-permute-start(bf16[128,1152]{1,0:T(8,128)(2,1)S(1)} %first_gather.5), channel_id=1, source_target_pairs={{3,0},{2,1},{1,2},{0,3},{5,4},{4,5},{7,6},{6,7},{11,8},{10,9},{9,1... | collective-permute-start | bytes 884744 | tf_op jit(solution)/shard_map/first_gather/ppermute | solution.py:32
  25.0 0.7 copy.10
  25.8 0.0 copy-done.1
  25.8 0.0 copy-done.2
  25.8 0.0 copy-start
  25.8 1.5 %copy-done = bf16[1,1152,3,288]{1,3,2,0:T(8,128)(2,1)S(1)} copy-done((bf16[1,1152,3,288]{1,3,2,0:T(8,128)(2,1)S(1)}, bf16[1,1152,3,288]{1,3,2,0:T(8,128)(2,1)}, u32[]{:S(2)}) %copy-start) | copy-done | bytes 1990680
  27.3 0.0 copy-start.3
  27.3 1.1 copy-done.3
  28.4 0.0 copy-start.5
  28.4 0.7 copy-done.5
  29.0 0.8 prepare.1
  29.9 2.4 %collective-permute-start.4 = (bf16[288,1152]{1,0:T(8,128)(2,1)S(1)}, bf16[288,1152]{1,0:T(8,128)(2,1)S(1)}, u32[]{:S(2)}, u32[]{:S(2)}) collective-permute-start(bf16[288,1152]{1,0:T(8,128)(2,1)S(1)} %bitcast.20), channel_id=1, source_target_pairs={{1,0},{0,1},{3,2},{2,3},{7,4},{6,5},{5,6},{4,7},{9,8},{8,9},{11,10... | collective-permute-start | bytes 1990664 | tf_op jit(solution)/shard_map/first_gather/ppermute | solution.py:32
  32.3 0.0 collective-permute-done.1.refs_1_.other_a
  32.3 3.1 %first_tick.4 = (bf16[4,72,256]{2,1,0:T(8,128)(2,1)S(1)}, bf16[4,72,256]{2,1,0:T(8,128)(2,1)S(1)}, bf16[4,72,256]{2,1,0:T(8,128)(2,1)S(1)}, f32[8,256]{1,0:T(8,1...) custom-call(bf16[128,1152]{1,0:T(8,128)(2,1)S(1)} %collective-permute-done.zero_ref.refs_0_, ...), custom_call_target="tpu_custom_call" | custom-call | flops 736100352 | bytes 4194304 | tf_op jit(solution)/shard_map/first_tick/pallas_call | solution.py:91
  35.4 1.4 %collective-permute-done.2.refs_1_.other_b = bf16[128,1152]{1,0:T(8,128)(2,1)S(1)} collective-permute-done((bf16[128,1152]{1,0:T(8,128)(2,1)S(1)}, bf16[128,1152]{1,0:T(8,128)(2,1)S(1)}, u32[]{:S(2)}, u32[]{:S(2)}) %collective-permute-start.2) | collective-permute-done | bytes 294944 | tf_op jit(solution)/shard_map/first_gather/ppermute | solution.py:32
  36.8 3.0 %first_tick.5 = (bf16[288,256]{1,0:T(8,128)(2,1)S(1)}, bf16[4,72,256]{2,1,0:T(8,128)(2,1)S(1)}, bf16[4,72,256]{2,1,0:T(8,128)(2,1)S(1)}, bf16[4,72,256]{2,1,0:T(8,128)(2,1)S(1)}) custom-call(bf16[128,1152]{1,0:T(8,128)(2,1)S(1)} %collective-permute-done.zero_ref.refs_0_, bf16[128,1152]{1,0:T(8,128)(2,1)S(1)} %collective-permute-done.2.refs_1_.other_b, ...), custom_call_target="tpu_custom_call" | custom-call | flops 660602880 | bytes 4194304 | tf_op jit(solution)/shard_map/first_tick/pallas_call | solution.py:91
  39.8 2.9 %collective-permute-start.3 = (bf16[288,256]{1,0:T(8,128)(2,1)S(1)}, bf16[288,256]{1,0:T(8,128)(2,1)S(1)}, u32[]{:S(2)}, u32[]{:S(2)}) collective-permute-start(bf16[288,256]{1,0:T(8,128)(2,1)S(1)} %get-tuple-element.56), channel_id=1, source_target_pairs={{1,0},{0,1},{3,2},{2,3},{7,4},{6,5},{5,6},{4,7},{9,8},{8,9},{11,10... | collective-permute-start | bytes 442376 | tf_op jit(solution)/shard_map/first_tick/ppermute | solution.py:32
  42.8 1.2 first_tick.6.refs_0_
  44.0 8.7 %collective-permute-done.3.refs_1_ = bf16[288,256]{1,0:T(8,128)(2,1)S(1)} collective-permute-done((bf16[288,256]{1,0:T(8,128)(2,1)S(1)}, bf16[288,256]{1,0:T(8,128)(2,1)S(1)}, u32[]{:S(2)}, u32[]{:S(2)}) %collective-permute-start.3) | collective-permute-done | bytes 147488 | tf_op jit(solution)/shard_map/first_tick/ppermute | solution.py:32
  52.7 0.0 collective-permute-done.4.refs_3_
  52.7 0.0 copy-start.6
  52.7 0.9 first_tick.7
  53.6 1.9 %collective-permute-start.7 = (bf16[160,1152]{1,0:T(8,128)(2,1)S(1)}, bf16[160,1152]{1,0:T(8,128)(2,1)S(1)}, u32[]{:S(2)}, u32[]{:S(2)}) collective-permute-start(bf16[160,1152]{1,0:T(8,128)(2,1)S(1)} %get-tuple-element.61), channel_id=1, source_target_pairs={{0,4},{1,5},{2,6},{3,7},{4,8},{5,9},{6,10},{7,11},{8,12},{9,13},{1... | collective-permute-start | bytes 1105928 | tf_op jit(solution)/shard_map/second_tick/ppermute | solution.py:43
  55.5 8.8 %collective-permute-start.8 = (bf16[160,1152]{1,0:T(8,128)(2,1)S(1)}, bf16[160,1152]{1,0:T(8,128)(2,1)S(1)}, u32[]{:S(2)}, u32[]{:S(2)}) collective-permute-start(bf16[160,1152]{1,0:T(8,128)(2,1)S(1)} %get-tuple-element.62), channel_id=1, source_target_pairs={{0,7},{1,6},{2,5},{3,4},{4,9},{5,8},{6,11},{7,10},{8,15},{9,14},{1... | collective-permute-start | bytes 1105928 | tf_op jit(solution)/shard_map/second_tick/ppermute | solution.py:43
  64.3 2.7 %collective-permute-start.5 = (bf16[96,1152]{1,0:T(8,128)(2,1)S(1)}, bf16[96,1152]{1,0:T(8,128)(2,1)S(1)}, u32[]{:S(2)}, u32[]{:S(2)}) collective-permute-start(bf16[96,1152]{1,0:T(8,128)(2,1)S(1)} %get-tuple-element.59), channel_id=1, source_target_pairs={{0,4},{1,5},{2,6},{3,7},{4,8},{5,9},{6,10},{7,11},{8,12},{9,13},{1... | collective-permute-start | bytes 663560 | tf_op jit(solution)/shard_map/second_tick/ppermute | solution.py:43
  66.9 6.8 %collective-permute-start.6 = (bf16[96,1152]{1,0:T(8,128)(2,1)S(1)}, bf16[96,1152]{1,0:T(8,128)(2,1)S(1)}, u32[]{:S(2)}, u32[]{:S(2)}) collective-permute-start(bf16[96,1152]{1,0:T(8,128)(2,1)S(1)} %get-tuple-element.60), channel_id=1, source_target_pairs={{0,7},{1,6},{2,5},{3,4},{4,9},{5,8},{6,11},{7,10},{8,15},{9,14},{1... | collective-permute-start | bytes 663560 | tf_op jit(solution)/shard_map/second_tick/ppermute | solution.py:43
  73.8 0.0 collective-permute-done.7.straight_ref
  73.8 0.0 collective-permute-done.8.crossing_ref
  73.8 0.1 second_tick.9.refs_1_
  73.9 10.5 %collective-permute-start.10 = (bf16[160,1152]{1,0:T(8,128)(2,1)S(1)}, bf16[160,1152]{1,0:T(8,128)(2,1)S(1)}, u32[]{:S(2)}, u32[]{:S(2)}) collective-permute-start(bf16[160,1152]{1,0:T(8,128)(2,1)S(1)} %second_tick.9.refs_1_), channel_id=1, source_target_pairs={{3,0},{2,1},{1,2},{0,3},{5,4},{4,5},{7,6},{6,7},{11,8},{10,9},{9,1... | collective-permute-start | bytes 1105928 | tf_op jit(solution)/shard_map/second_tick/ppermute | solution.py:32
  84.4 0.0 collective-permute-done.5.straight_ref
  84.4 0.0 collective-permute-done.6.crossing_ref
  84.4 0.1 second_tick.8.refs_0_
  84.5 6.8 %collective-permute-start.9 = (bf16[96,1152]{1,0:T(8,128)(2,1)S(1)}, bf16[96,1152]{1,0:T(8,128)(2,1)S(1)}, u32[]{:S(2)}, u32[]{:S(2)}) collective-permute-start(bf16[96,1152]{1,0:T(8,128)(2,1)S(1)} %second_tick.8.refs_0_), channel_id=1, source_target_pairs={{3,0},{2,1},{1,2},{0,3},{5,4},{4,5},{7,6},{6,7},{11,8},{10,9},{9,1... | collective-permute-start | bytes 663560 | tf_op jit(solution)/shard_map/second_tick/ppermute | solution.py:32
  91.3 0.0 copy-done.6
  91.3 4.0 %second_tick.10 = (bf16[4,72,256]{2,1,0:T(8,128)(2,1)S(1)}, bf16[4,72,256]{2,1,0:T(8,128)(2,1)S(1)}, bf16[4,72,256]{2,1,0:T(8,128)(2,1)S(1)}, f32[8,256]{1,0:T(8...) custom-call(bf16[96,1152]{1,0:T(8,128)(2,1)S(1)} %second_tick.8.refs, ...), custom_call_target="tpu_custom_call" | custom-call | flops 736100352 | bytes 4194304 | tf_op jit(solution)/shard_map/second_tick/pallas_call | solution.py:91
  95.3 2.4 %collective-permute-done.9.refs_0_ = bf16[96,1152]{1,0:T(8,128)(2,1)S(1)} collective-permute-done((bf16[96,1152]{1,0:T(8,128)(2,1)S(1)}, bf16[96,1152]{1,0:T(8,128)(2,1)S(1)}, u32[]{:S(2)}, u32[]{:S(2)}) %collective-permute-start.9) | collective-permute-done | bytes 221216 | tf_op jit(solution)/shard_map/second_tick/ppermute | solution.py:32
  97.7 0.0 collective-permute-done.10.refs_1_
  97.7 3.0 %second_tick.11 = (bf16[288,256]{1,0:T(8,128)(2,1)S(1)}, bf16[4,72,256]{2,1,0:T(8,128)(2,1)S(1)}, bf16[4,72,256]{2,1,0:T(8,128)(2,1)S(1)}, bf16[4,72,256]{2,1,0:T(8,128)(2,1)S(1)}) custom-call(bf16[96,1152]{1,0:T(8,128)(2,1)S(1)} %collective-permute-done.9.refs_0_, bf16[160,1152]{1,0:T(8,128)(2,1)S(1)} %collective-permute-done.10.refs_1_, ...), custom_call_target="tpu_custom_call" | custom-call | flops 660602880 | bytes 4194304 | tf_op jit(solution)/shard_map/second_tick/pallas_call | solution.py:91
  100.7 1.9 %collective-permute-start.11 = (bf16[288,256]{1,0:T(8,128)(2,1)S(1)}, bf16[288,256]{1,0:T(8,128)(2,1)S(1)}, u32[]{:S(2)}, u32[]{:S(2)}) collective-permute-start(bf16[288,256]{1,0:T(8,128)(2,1)S(1)} %get-tuple-element.76), channel_id=1, source_target_pairs={{1,0},{0,1},{3,2},{2,3},{7,4},{6,5},{5,6},{4,7},{9,8},{8,9},{11,10... | collective-permute-start | bytes 442376 | tf_op jit(solution)/shard_map/second_tick/ppermute | solution.py:32
  102.7 1.2 second_tick.12.refs_0_
  103.9 5.2 %collective-permute-done.11.refs_1_ = bf16[288,256]{1,0:T(8,128)(2,1)S(1)} collective-permute-done((bf16[288,256]{1,0:T(8,128)(2,1)S(1)}, bf16[288,256]{1,0:T(8,128)(2,1)S(1)}, u32[]{:S(2)}, u32[]{:S(2)}) %collective-permute-start.11) | collective-permute-done | bytes 147488 | tf_op jit(solution)/shard_map/second_tick/ppermute | solution.py:32
  109.0 0.5 second_tick.14
  109.6 9.0 %collective-permute-start.12 = (bf16[128,1152]{1,0:T(8,128)(2,1)S(1)}, bf16[128,1152]{1,0:T(8,128)(2,1)S(1)}, u32[]{:S(2)}, u32[]{:S(2)}) collective-permute-start(bf16[128,1152]{1,0:T(8,128)(2,1)S(1)} %second_tick.14), channel_id=1, source_target_pairs={{3,0},{2,1},{1,2},{0,3},{5,4},{4,5},{7,6},{6,7},{11,8},{10,9},{9,1... | collective-permute-start | bytes 884744 | tf_op jit(solution)/shard_map/second_tick/ppermute | solution.py:32
  118.6 0.5 second_tick.13.refs_2_
  119.1 6.0 %collective-permute-done.12.refs_3_ = bf16[128,1152]{1,0:T(8,128)(2,1)S(1)} collective-permute-done((bf16[128,1152]{1,0:T(8,128)(2,1)S(1)}, bf16[128,1152]{1,0:T(8,128)(2,1)S(1)}, u32[]{:S(2)}, u32[]{:S(2)}) %collective-permute-start.12) | collective-permute-done | bytes 294944 | tf_op jit(solution)/shard_map/second_tick/ppermute | solution.py:32
  125.1 0.8 second_tick.15
  (3 shorter events, 0.1 us)
Async XLA Ops:
  0.0 25.8 %copy-start.1 = (bf16[1,288,1152]{2,1,0:T(8,128)(2,1)S(1)}, bf16[1,288,1152]{2,1,0:T(8,128)(2,1)}, u32[]{:S(2)}) copy-start(bf16[1,288,1152]{2,1,0:T(8,128)(2,1)} %param.9) | copy-start | bytes 1990660
  0.0 25.8 %copy-start.2 = (bf16[1,1024,288]{1,2,0:T(8,128)(2,1)S(1)}, bf16[1,1024,288]{1,2,0:T(8,128)(2,1)}, u32[]{:S(2)}) copy-start(bf16[1,1024,288]{1,2,0:T(8,128)(2,1)} %param.11) | copy-start | bytes 1769476
  0.0 14.0 %collective-permute-start = (bf16[128,1152]{1,0:T(8,128)(2,1)}, bf16[128,1152]{1,0:T(8,128)(2,1)S(1)}, u32[]{:S(2)}, u32[]{:S(2)}) collective-permute-start(bf16[128,1152]{1,0:T(8,128)(2,1)} %bitcast.23), channel_id=1, source_target_pairs={{1,0},{0,1},{3,2},{2,3},{7,4},{6,5},{5,6},{4,7},{9,8},{8,9},{11,10... | collective-permute-start | bytes 884744 | tf_op jit(solution)/shard_map/first_gather/ppermute | solution.py:32
  6.2 1.0 copy-start.4
  14.0 18.3 %collective-permute-start.1 = (bf16[128,1152]{1,0:T(8,128)(2,1)S(1)}, bf16[128,1152]{1,0:T(8,128)(2,1)S(1)}, u32[]{:S(2)}, u32[]{:S(2)}) collective-permute-start(bf16[128,1152]{1,0:T(8,128)(2,1)S(1)} %first_gather.4), channel_id=1, source_target_pairs={{3,0},{2,1},{1,2},{0,3},{5,4},{4,5},{7,6},{6,7},{11,8},{10,9},{9,1... | collective-permute-start | bytes 884744 | tf_op jit(solution)/shard_map/first_gather/ppermute | solution.py:32
  23.1 13.7 %collective-permute-start.2 = (bf16[128,1152]{1,0:T(8,128)(2,1)S(1)}, bf16[128,1152]{1,0:T(8,128)(2,1)S(1)}, u32[]{:S(2)}, u32[]{:S(2)}) collective-permute-start(bf16[128,1152]{1,0:T(8,128)(2,1)S(1)} %first_gather.5), channel_id=1, source_target_pairs={{3,0},{2,1},{1,2},{0,3},{5,4},{4,5},{7,6},{6,7},{11,8},{10,9},{9,1... | collective-permute-start | bytes 884744 | tf_op jit(solution)/shard_map/first_gather/ppermute | solution.py:32
  25.8 1.6 %copy-start = (bf16[1,1152,3,288]{1,3,2,0:T(8,128)(2,1)S(1)}, bf16[1,1152,3,288]{1,3,2,0:T(8,128)(2,1)}, u32[]{:S(2)}) copy-start(bf16[1,1152,3,288]{1,3,2,0:T(8,128)(2,1)} %param.8) | copy-start | bytes 5971972
  27.3 1.1 copy-start.3
  28.4 0.7 copy-start.5
  29.9 22.8 %collective-permute-start.4 = (bf16[288,1152]{1,0:T(8,128)(2,1)S(1)}, bf16[288,1152]{1,0:T(8,128)(2,1)S(1)}, u32[]{:S(2)}, u32[]{:S(2)}) collective-permute-start(bf16[288,1152]{1,0:T(8,128)(2,1)S(1)} %bitcast.20), channel_id=1, source_target_pairs={{1,0},{0,1},{3,2},{2,3},{7,4},{6,5},{5,6},{4,7},{9,8},{8,9},{11,10... | collective-permute-start | bytes 1990664 | tf_op jit(solution)/shard_map/first_gather/ppermute | solution.py:32
  39.8 12.8 %collective-permute-start.3 = (bf16[288,256]{1,0:T(8,128)(2,1)S(1)}, bf16[288,256]{1,0:T(8,128)(2,1)S(1)}, u32[]{:S(2)}, u32[]{:S(2)}) collective-permute-start(bf16[288,256]{1,0:T(8,128)(2,1)S(1)} %get-tuple-element.56), channel_id=1, source_target_pairs={{1,0},{0,1},{3,2},{2,3},{7,4},{6,5},{5,6},{4,7},{9,8},{8,9},{11,10... | collective-permute-start | bytes 442376 | tf_op jit(solution)/shard_map/first_tick/ppermute | solution.py:32
  52.7 38.6 %copy-start.6 = (s32[1,2]{1,0:T(1,128)S(1)}, s32[1,2]{1,0:T(1,128)}, u32[]{:S(2)}) copy-start(s32[1,2]{1,0:T(1,128)} %param.13) | copy-start | bytes 28
  53.6 20.2 %collective-permute-start.7 = (bf16[160,1152]{1,0:T(8,128)(2,1)S(1)}, bf16[160,1152]{1,0:T(8,128)(2,1)S(1)}, u32[]{:S(2)}, u32[]{:S(2)}) collective-permute-start(bf16[160,1152]{1,0:T(8,128)(2,1)S(1)} %get-tuple-element.61), channel_id=1, source_target_pairs={{0,4},{1,5},{2,6},{3,7},{4,8},{5,9},{6,10},{7,11},{8,12},{9,13},{1... | collective-permute-start | bytes 1105928 | tf_op jit(solution)/shard_map/second_tick/ppermute | solution.py:43
  55.5 18.3 %collective-permute-start.8 = (bf16[160,1152]{1,0:T(8,128)(2,1)S(1)}, bf16[160,1152]{1,0:T(8,128)(2,1)S(1)}, u32[]{:S(2)}, u32[]{:S(2)}) collective-permute-start(bf16[160,1152]{1,0:T(8,128)(2,1)S(1)} %get-tuple-element.62), channel_id=1, source_target_pairs={{0,7},{1,6},{2,5},{3,4},{4,9},{5,8},{6,11},{7,10},{8,15},{9,14},{1... | collective-permute-start | bytes 1105928 | tf_op jit(solution)/shard_map/second_tick/ppermute | solution.py:43
  64.3 20.1 %collective-permute-start.5 = (bf16[96,1152]{1,0:T(8,128)(2,1)S(1)}, bf16[96,1152]{1,0:T(8,128)(2,1)S(1)}, u32[]{:S(2)}, u32[]{:S(2)}) collective-permute-start(bf16[96,1152]{1,0:T(8,128)(2,1)S(1)} %get-tuple-element.59), channel_id=1, source_target_pairs={{0,4},{1,5},{2,6},{3,7},{4,8},{5,9},{6,10},{7,11},{8,12},{9,13},{1... | collective-permute-start | bytes 663560 | tf_op jit(solution)/shard_map/second_tick/ppermute | solution.py:43
  66.9 17.5 %collective-permute-start.6 = (bf16[96,1152]{1,0:T(8,128)(2,1)S(1)}, bf16[96,1152]{1,0:T(8,128)(2,1)S(1)}, u32[]{:S(2)}, u32[]{:S(2)}) collective-permute-start(bf16[96,1152]{1,0:T(8,128)(2,1)S(1)} %get-tuple-element.60), channel_id=1, source_target_pairs={{0,7},{1,6},{2,5},{3,4},{4,9},{5,8},{6,11},{7,10},{8,15},{9,14},{1... | collective-permute-start | bytes 663560 | tf_op jit(solution)/shard_map/second_tick/ppermute | solution.py:43
  73.9 23.8 %collective-permute-start.10 = (bf16[160,1152]{1,0:T(8,128)(2,1)S(1)}, bf16[160,1152]{1,0:T(8,128)(2,1)S(1)}, u32[]{:S(2)}, u32[]{:S(2)}) collective-permute-start(bf16[160,1152]{1,0:T(8,128)(2,1)S(1)} %second_tick.9.refs_1_), channel_id=1, source_target_pairs={{3,0},{2,1},{1,2},{0,3},{5,4},{4,5},{7,6},{6,7},{11,8},{10,9},{9,1... | collective-permute-start | bytes 1105928 | tf_op jit(solution)/shard_map/second_tick/ppermute | solution.py:32
  84.5 13.2 %collective-permute-start.9 = (bf16[96,1152]{1,0:T(8,128)(2,1)S(1)}, bf16[96,1152]{1,0:T(8,128)(2,1)S(1)}, u32[]{:S(2)}, u32[]{:S(2)}) collective-permute-start(bf16[96,1152]{1,0:T(8,128)(2,1)S(1)} %second_tick.8.refs_0_), channel_id=1, source_target_pairs={{3,0},{2,1},{1,2},{0,3},{5,4},{4,5},{7,6},{6,7},{11,8},{10,9},{9,1... | collective-permute-start | bytes 663560 | tf_op jit(solution)/shard_map/second_tick/ppermute | solution.py:32
  100.7 8.3 %collective-permute-start.11 = (bf16[288,256]{1,0:T(8,128)(2,1)S(1)}, bf16[288,256]{1,0:T(8,128)(2,1)S(1)}, u32[]{:S(2)}, u32[]{:S(2)}) collective-permute-start(bf16[288,256]{1,0:T(8,128)(2,1)S(1)} %get-tuple-element.76), channel_id=1, source_target_pairs={{1,0},{0,1},{3,2},{2,3},{7,4},{6,5},{5,6},{4,7},{9,8},{8,9},{11,10... | collective-permute-start | bytes 442376 | tf_op jit(solution)/shard_map/second_tick/ppermute | solution.py:32
  109.6 15.5 %collective-permute-start.12 = (bf16[128,1152]{1,0:T(8,128)(2,1)S(1)}, bf16[128,1152]{1,0:T(8,128)(2,1)S(1)}, u32[]{:S(2)}, u32[]{:S(2)}) collective-permute-start(bf16[128,1152]{1,0:T(8,128)(2,1)S(1)} %second_tick.14), channel_id=1, source_target_pairs={{3,0},{2,1},{1,2},{0,3},{5,4},{4,5},{7,6},{6,7},{11,8},{10,9},{9,1... | collective-permute-start | bytes 884744 | tf_op jit(solution)/shard_map/second_tick/ppermute | solution.py:32

commit v7 on v6

--- a/solution.py
+++ b/solution.py
@@ -172,9 +172,13 @@
     )
 
 
+def late_caches(late_refs, h):
+    caches = late_refs[1:]
+    return [(k_ref[h], v_ref[h]) for k_ref, v_ref in zip(caches[::2], caches[1::2], strict=True)]
+
+
 def merge_job(mixed, at, span, early_refs, late_refs):
     q_ref, _, _, top_ref, total_ref, out_ref = early_refs
-    _, kl_ref, vl_ref = late_refs
     first, last = span
 
     def store(h, top, total, out):
@@ -182,7 +186,7 @@
 
     return (
         lambda h: q_ref[h, :, first:last],
-        lambda h: [(kl_ref[h], vl_ref[h])],
+        lambda h: late_caches(late_refs, h),
         lambda h: (top_ref[h : h + 1, first:last], total_ref[h : h + 1, first:last], out_ref[h, :, first:last]),
         store,
     )
@@ -190,15 +194,14 @@
 
 def whole_job(mixed, at, span, early_refs, late_refs, ko_ref, vo_ref):
     _, k_ref, v_ref, *_ = early_refs
-    ql_ref, kl_ref, vl_ref = late_refs
     first, last = span
 
     def store(h, top, total, out):
         mixed[h * HEAD_DIM : (h + 1) * HEAD_DIM, at : at + last - first] = out * (1.0 / total)
 
     return (
-        lambda h: ql_ref[h, :, first:last],
-        lambda h: [(k_ref[h], v_ref[h]), (ko_ref[h], vo_ref[h]), (kl_ref[h], vl_ref[h])],
+        lambda h: late_refs[0][h, :, first:last],
+        lambda h: [(k_ref[h], v_ref[h]), (ko_ref[h], vo_ref[h]), *late_caches(late_refs, h)],
         None,
         store,
     )
@@ -215,35 +218,64 @@
     )
 
 
-def late_kernel(places, n_parts, *refs):
+def ahead_kernel(places, part_ref, mods_ref, w_ref, q_ref, k_ref, v_ref, normed, qkv):
+    load_rows((part_ref,), places, mods_ref, w_ref, normed, qkv)
+    split_heads(qkv, (q_ref, k_ref, v_ref))
+
+
+def ahead(part, places, mods, w):
+    rows, features = part.shape
+    heads = w.shape[0] // HEAD_DIM // 3
+    return call(
+        functools.partial(ahead_kernel, places), [shape(jnp.bfloat16, heads, HEAD_DIM, rows)] * 3,
+        [pltpu.VMEM((rows, features), jnp.bfloat16), pltpu.VMEM((w.shape[0], rows), jnp.float32)],
+        2 * rows * features * w.shape[0], 0, (part, mods, w),
+    )
+
+
+def late_kernel(places, n_parts, n_ahead, *refs):
     parts, refs = refs[:n_parts], refs[n_parts:]
+    before, refs = refs[:n_ahead], refs[n_ahead:]
     mods_ref, w_ref, ko_ref, vo_ref, *early_refs = refs[:10]
     sent_ref, *late_refs, normed, qkv, mixed = refs[10:]
     load_rows(parts, places, mods_ref, w_ref, normed, qkv)
-    split_heads(qkv, late_refs)
+    if before:
+        q_ref, *late_refs = late_refs
+        heads = q_ref.shape[0]
+        new, old = qkv.shape[1] // 2, before[0].shape[2] // 2
+        for h in range(heads):
+            mine, theirs = qkv[h * HEAD_DIM : (h + 1) * HEAD_DIM], before[0][h].astype(jnp.float32)
+            columns = [mine[:, :new], theirs[:, :old], mine[:, new:], theirs[:, old:]]
+            q_ref[h] = jnp.concatenate(columns, axis=1).astype(jnp.bfloat16)
+        split_heads(qkv[heads * HEAD_DIM :], late_refs)
+        late_refs = (q_ref, *late_refs, *before[1:])
+    else:
+        split_heads(qkv, late_refs)
     finish(mixed, (0, mixed.shape[1] // 2), early_refs, late_refs, ko_ref, vo_ref)
     sent_ref[...] = mixed[...].astype(jnp.bfloat16)
 
 
-def late(parts, places, mods, w, ko, vo, early_state):
+def late(parts, places, mods, w, ko, vo, early_state, before=()):
     rows, features = sum(last - first for _, first, last in places), w.shape[1]
     heads, _, count = ko.shape
     width = heads * HEAD_DIM
-    return call(
-        functools.partial(late_kernel, places, len(parts)),
-        [shape(jnp.bfloat16, width, rows)] + [shape(jnp.bfloat16, heads, HEAD_DIM, rows)] * 3,
+    columns = rows + (before[0].shape[2] if before else 0)
+    return call(
+        functools.partial(late_kernel, places, len(parts), len(before)),
+        [shape(jnp.bfloat16, width, columns), shape(jnp.bfloat16, heads, HEAD_DIM, columns)]
+        + [shape(jnp.bfloat16, heads, HEAD_DIM, rows)] * 2,
         [
             pltpu.VMEM((rows, features), jnp.bfloat16),
             pltpu.VMEM((w.shape[0], rows), jnp.float32),
-            pltpu.VMEM((width, rows), jnp.float32),
+            pltpu.VMEM((width, columns), jnp.float32),
         ],
-        2 * rows * features * w.shape[0] + 4 * rows * count * width,
-        heads * rows * count, (*parts, mods, w, ko, vo, *early_state),
+        2 * rows * features * w.shape[0] + 4 * columns * count * width,
+        heads * columns * count, (*parts, *before, mods, w, ko, vo, *early_state),
     )
 
 
 def rest_kernel(ko_ref, vo_ref, *refs):
-    early_refs, late_refs, (kept_ref, mixed) = refs[:6], refs[6:9], refs[9:]
+    early_refs, (*late_refs, kept_ref, mixed) = refs[:6], refs[6:]
     columns = mixed.shape[1]
     finish(mixed, (columns // 2, columns), early_refs, late_refs, ko_ref, vo_ref)
     kept_ref[...] = mixed[...].astype(jnp.bfloat16)
@@ -258,14 +290,15 @@
     )
 
 
-def block(early_parts, late_parts, places, olds, mods, w, ko, vo, also=()):
+def block(early_parts, late_parts, places, olds, mods, w, ko, vo, first=None):
     state = early(early_parts, places[0], olds, mods, w, ko, vo)
     if olds:
         *state, ko, vo = state
-    sent, *late_state = late(late_parts, places[1], mods, w, ko, vo, state)
+    before = ahead(*first, mods, w) if first else ()
+    sent, *late_state = late(late_parts, places[1], mods, w, ko, vo, state, before)
     theirs = exchange(sent, 0)
-    mine = rest(ko, vo, state, late_state)
-    return mine, theirs, (state[1], late_state[1], state[2], late_state[2]), also
+    mine = rest(ko, vo, state, (*late_state, *before[1:]))
+    return mine, theirs, (state[1], late_state[1], state[2], late_state[2])
 
 
 def both_sums(first, last, mine_ref, theirs_ref, w_mine_ref, w_theirs_ref):
@@ -387,7 +420,7 @@
     with jax.named_scope("first_tick"):
         places = [((0, *span), (1, half, rows), (2, 0, half), (1, 0, half)) for span in spans]
         parts = [(zero, other, own_half) for other, own_half in zip(others, owns, strict=True)]
-        mine, theirs, olds, _ = block(*parts, places, (), mods, w, ko, vo)
+        mine, theirs, olds = block(*parts, places, (), mods, w, ko, vo)
         cut = rows * SMALL_CHUNK // 16
         spans = ((0, cut), (cut, rows))
         shifted = shift(spans, owns, others, mods, mine, theirs, w_mine, w_theirs)
@@ -398,8 +431,11 @@
         others = [exchange(rows_here, 1) for rows_here in here]
         sizes = [last - first for first, last in spans]
         places = [(i, size, 2 * size) for i, size in enumerate(sizes)] + [(i, 0, size) for i, size in enumerate(sizes)]
-        places = [tuple(places)] * 2
-        mine, theirs, *_ = block(here, others, places, (slots, *olds), mods, w, ko_next, vo_next)
+        late_places = [((0, size, 2 * size), (0, 0, size)) for size in sizes]
+        mine, theirs, _ = block(
+            here, others[:1], (tuple(places), late_places[0]), (slots, *olds), mods, w, ko_next, vo_next,
+            (others[1], late_places[1]),
+        )
         from_one = exchange(part(rows, jnp.bfloat16, mine, theirs, w_mine, w_theirs), 1)
         mine_own = part(0, jnp.float32, mine, theirs, w_mine, w_theirs)
         own_rows = tuple((i, 0, size) for i, size in enumerate(sizes))

time: 127 us -> 126 us (level)
    pallas_call x16 -> x17, Pallas kernels: 19.3 us -> 19.9 us  [call(): pl.pallas_call(kernel, out_shape=outs, in_specs=specs, scratch_shapes=scr...]
  transfers between devices with their start and end apart: 13 -> 13, of which waited for: 6 -> 6; matrix products, arithmetic and copies ran while one was open for 1% -> 1% of each run, Pallas kernels for 11% -> 12%
where the time goes in v7:
time: 126 us
  starting transfers between devices  71 us (56%)
  waiting for transfers between devices  29.4 us (23%)
  Pallas kernels  19.9 us (16%)
  local copies, waits for them, and re-layouts  4.96 us (4%)
    ppermute x9, starting transfers between devices, exchange(): return lax.ppermute(array, AXES, moves)  50.8 us
    ppermute x9, waiting for transfers between devices, exchange(): return lax.ppermute(array, AXES, moves)  29.4 us
    ppermute x4, starting transfers between devices, advance(): return lax.ppermute(array, AXES, moves)  20.2 us
    pallas_call x17, Pallas kernels, call(): pl.pallas_call(kernel, out_shape=outs, in_specs=specs, scratch_shapes=scr...  19.9 us
    unnamed x15, local copies, waits for them, and re-layouts  4.96 us
  transfers between devices with their start and end apart: 13, of which 6 were waited for; matrix products, arithmetic and copies ran while one was open for 1% of the time, Pallas kernels for 12%

profile of v7, /device:TPU:64, one launch (start us, length us, event | category | flops | bytes accessed | tf_op | source)
XLA Modules:
  0.0 125.5 jit_solution(16145861723527987705)
XLA Ops:
  0.0 0.0 copy-start.1
  0.0 0.0 copy-start.2
  0.0 6.2 %collective-permute-start = (bf16[128,1152]{1,0:T(8,128)(2,1)}, bf16[128,1152]{1,0:T(8,128)(2,1)S(1)}, u32[]{:S(2)}, u32[]{:S(2)}) collective-permute-start(bf16[128,1152]{1,0:T(8,128)(2,1)} %bitcast.23), channel_id=1, source_target_pairs={{1,0},{0,1},{3,2},{2,3},{7,4},{6,5},{5,6},{4,7},{9,8},{8,9},{11,10... | collective-permute-start | bytes 884744 | tf_op jit(solution)/shard_map/first_gather/ppermute | solution.py:32
  6.2 0.0 copy-start.4
  6.2 1.0 copy-done.4
  7.2 6.7 %collective-permute-done.zero_ref.refs_0_ = bf16[128,1152]{1,0:T(8,128)(2,1)S(1)} collective-permute-done((bf16[128,1152]{1,0:T(8,128)(2,1)}, bf16[128,1152]{1,0:T(8,128)(2,1)S(1)}, u32[]{:S(2)}, u32[]{:S(2)}) %collective-permute-start) | collective-permute-done | bytes 294944 | tf_op jit(solution)/shard_map/first_gather/ppermute | solution.py:32
  14.0 9.1 %collective-permute-start.1 = (bf16[128,1152]{1,0:T(8,128)(2,1)S(1)}, bf16[128,1152]{1,0:T(8,128)(2,1)S(1)}, u32[]{:S(2)}, u32[]{:S(2)}) collective-permute-start(bf16[128,1152]{1,0:T(8,128)(2,1)S(1)} %first_gather.4), channel_id=1, source_target_pairs={{3,0},{2,1},{1,2},{0,3},{5,4},{4,5},{7,6},{6,7},{11,8},{10,9},{9,1... | collective-permute-start | bytes 884744 | tf_op jit(solution)/shard_map/first_gather/ppermute | solution.py:32
  23.1 1.9 %collective-permute-start.2 = (bf16[128,1152]{1,0:T(8,128)(2,1)S(1)}, bf16[128,1152]{1,0:T(8,128)(2,1)S(1)}, u32[]{:S(2)}, u32[]{:S(2)}) collective-permute-start(bf16[128,1152]{1,0:T(8,128)(2,1)S(1)} %first_gather.5), channel_id=1, source_target_pairs={{3,0},{2,1},{1,2},{0,3},{5,4},{4,5},{7,6},{6,7},{11,8},{10,9},{9,1... | collective-permute-start | bytes 884744 | tf_op jit(solution)/shard_map/first_gather/ppermute | solution.py:32
  25.0 0.7 copy.10
  25.8 0.0 copy-done.1
  25.8 0.0 copy-done.2
  25.8 0.0 copy-start
  25.8 1.5 %copy-done = bf16[1,1152,3,288]{1,3,2,0:T(8,128)(2,1)S(1)} copy-done((bf16[1,1152,3,288]{1,3,2,0:T(8,128)(2,1)S(1)}, bf16[1,1152,3,288]{1,3,2,0:T(8,128)(2,1)}, u32[]{:S(2)}) %copy-start) | copy-done | bytes 1990680
  27.3 0.0 copy-start.3
  27.3 1.1 copy-done.3
  28.4 0.0 copy-start.5
  28.4 0.7 copy-done.5
  29.0 0.8 prepare.1
  29.9 2.4 %collective-permute-start.4 = (bf16[288,1152]{1,0:T(8,128)(2,1)S(1)}, bf16[288,1152]{1,0:T(8,128)(2,1)S(1)}, u32[]{:S(2)}, u32[]{:S(2)}) collective-permute-start(bf16[288,1152]{1,0:T(8,128)(2,1)S(1)} %bitcast.20), channel_id=1, source_target_pairs={{1,0},{0,1},{3,2},{2,3},{7,4},{6,5},{5,6},{4,7},{9,8},{8,9},{11,10... | collective-permute-start | bytes 1990664 | tf_op jit(solution)/shard_map/first_gather/ppermute | solution.py:32
  32.3 0.0 collective-permute-done.1.refs_1_.other_a
  32.3 3.1 %first_tick.4 = (bf16[4,72,256]{2,1,0:T(8,128)(2,1)S(1)}, bf16[4,72,256]{2,1,0:T(8,128)(2,1)S(1)}, bf16[4,72,256]{2,1,0:T(8,128)(2,1)S(1)}, f32[8,256]{1,0:T(8,1...) custom-call(bf16[128,1152]{1,0:T(8,128)(2,1)S(1)} %collective-permute-done.zero_ref.refs_0_, ...), custom_call_target="tpu_custom_call" | custom-call | flops 736100352 | bytes 4194304 | tf_op jit(solution)/shard_map/first_tick/pallas_call | solution.py:91
  35.4 1.4 %collective-permute-done.2.refs_1_.other_b = bf16[128,1152]{1,0:T(8,128)(2,1)S(1)} collective-permute-done((bf16[128,1152]{1,0:T(8,128)(2,1)S(1)}, bf16[128,1152]{1,0:T(8,128)(2,1)S(1)}, u32[]{:S(2)}, u32[]{:S(2)}) %collective-permute-start.2) | collective-permute-done | bytes 294944 | tf_op jit(solution)/shard_map/first_gather/ppermute | solution.py:32
  36.8 3.0 %first_tick.5 = (bf16[288,256]{1,0:T(8,128)(2,1)S(1)}, bf16[4,72,256]{2,1,0:T(8,128)(2,1)S(1)}, bf16[4,72,256]{2,1,0:T(8,128)(2,1)S(1)}, bf16[4,72,256]{2,1,0:T(8,128)(2,1)S(1)}) custom-call(bf16[128,1152]{1,0:T(8,128)(2,1)S(1)} %collective-permute-done.zero_ref.refs_0_, bf16[128,1152]{1,0:T(8,128)(2,1)S(1)} %collective-permute-done.2.refs_1_.other_b, ...), custom_call_target="tpu_custom_call" | custom-call | flops 660602880 | bytes 4194304 | tf_op jit(solution)/shard_map/first_tick/pallas_call | solution.py:91
  39.8 2.9 %collective-permute-start.3 = (bf16[288,256]{1,0:T(8,128)(2,1)S(1)}, bf16[288,256]{1,0:T(8,128)(2,1)S(1)}, u32[]{:S(2)}, u32[]{:S(2)}) collective-permute-start(bf16[288,256]{1,0:T(8,128)(2,1)S(1)} %get-tuple-element.59), channel_id=1, source_target_pairs={{1,0},{0,1},{3,2},{2,3},{7,4},{6,5},{5,6},{4,7},{9,8},{8,9},{11,10... | collective-permute-start | bytes 442376 | tf_op jit(solution)/shard_map/first_tick/ppermute | solution.py:32
  42.8 1.1 first_tick.6.refs_0_
  43.9 8.8 %collective-permute-done.3.refs_1_ = bf16[288,256]{1,0:T(8,128)(2,1)S(1)} collective-permute-done((bf16[288,256]{1,0:T(8,128)(2,1)S(1)}, bf16[288,256]{1,0:T(8,128)(2,1)S(1)}, u32[]{:S(2)}, u32[]{:S(2)}) %collective-permute-start.3) | collective-permute-done | bytes 147488 | tf_op jit(solution)/shard_map/first_tick/ppermute | solution.py:32
  52.7 0.0 collective-permute-done.4.refs_3_
  52.7 0.0 copy-start.6
  52.7 0.9 first_tick.7
  53.6 1.9 %collective-permute-start.7 = (bf16[160,1152]{1,0:T(8,128)(2,1)S(1)}, bf16[160,1152]{1,0:T(8,128)(2,1)S(1)}, u32[]{:S(2)}, u32[]{:S(2)}) collective-permute-start(bf16[160,1152]{1,0:T(8,128)(2,1)S(1)} %get-tuple-element.64), channel_id=1, source_target_pairs={{0,4},{1,5},{2,6},{3,7},{4,8},{5,9},{6,10},{7,11},{8,12},{9,13},{1... | collective-permute-start | bytes 1105928 | tf_op jit(solution)/shard_map/second_tick/ppermute | solution.py:43
  55.5 8.8 %collective-permute-start.8 = (bf16[160,1152]{1,0:T(8,128)(2,1)S(1)}, bf16[160,1152]{1,0:T(8,128)(2,1)S(1)}, u32[]{:S(2)}, u32[]{:S(2)}) collective-permute-start(bf16[160,1152]{1,0:T(8,128)(2,1)S(1)} %get-tuple-element.65), channel_id=1, source_target_pairs={{0,7},{1,6},{2,5},{3,4},{4,9},{5,8},{6,11},{7,10},{8,15},{9,14},{1... | collective-permute-start | bytes 1105928 | tf_op jit(solution)/shard_map/second_tick/ppermute | solution.py:43
  64.3 2.6 %collective-permute-start.5 = (bf16[96,1152]{1,0:T(8,128)(2,1)S(1)}, bf16[96,1152]{1,0:T(8,128)(2,1)S(1)}, u32[]{:S(2)}, u32[]{:S(2)}) collective-permute-start(bf16[96,1152]{1,0:T(8,128)(2,1)S(1)} %get-tuple-element.62), channel_id=1, source_target_pairs={{0,4},{1,5},{2,6},{3,7},{4,8},{5,9},{6,10},{7,11},{8,12},{9,13},{1... | collective-permute-start | bytes 663560 | tf_op jit(solution)/shard_map/second_tick/ppermute | solution.py:43
  66.9 6.8 %collective-permute-start.6 = (bf16[96,1152]{1,0:T(8,128)(2,1)S(1)}, bf16[96,1152]{1,0:T(8,128)(2,1)S(1)}, u32[]{:S(2)}, u32[]{:S(2)}) collective-permute-start(bf16[96,1152]{1,0:T(8,128)(2,1)S(1)} %get-tuple-element.63), channel_id=1, source_target_pairs={{0,7},{1,6},{2,5},{3,4},{4,9},{5,8},{6,11},{7,10},{8,15},{9,14},{1... | collective-permute-start | bytes 663560 | tf_op jit(solution)/shard_map/second_tick/ppermute | solution.py:43
  73.8 0.0 collective-permute-done.7.straight_ref
  73.8 0.0 collective-permute-done.8.crossing_ref
  73.8 0.1 second_tick.10.refs_1_
  73.9 10.5 %collective-permute-start.10 = (bf16[160,1152]{1,0:T(8,128)(2,1)S(1)}, bf16[160,1152]{1,0:T(8,128)(2,1)S(1)}, u32[]{:S(2)}, u32[]{:S(2)}) collective-permute-start(bf16[160,1152]{1,0:T(8,128)(2,1)S(1)} %second_tick.10.refs_1_), channel_id=1, source_target_pairs={{3,0},{2,1},{1,2},{0,3},{5,4},{4,5},{7,6},{6,7},{11,8},{10,9},{9,1... | collective-permute-start | bytes 1105928 | tf_op jit(solution)/shard_map/second_tick/ppermute | solution.py:32
  84.4 0.0 collective-permute-done.5.straight_ref
  84.4 0.0 collective-permute-done.6.crossing_ref
  84.4 0.1 second_tick.9.refs_0_
  84.5 6.8 %collective-permute-start.9 = (bf16[96,1152]{1,0:T(8,128)(2,1)S(1)}, bf16[96,1152]{1,0:T(8,128)(2,1)S(1)}, u32[]{:S(2)}, u32[]{:S(2)}) collective-permute-start(bf16[96,1152]{1,0:T(8,128)(2,1)S(1)} %second_tick.9.refs_0_), channel_id=1, source_target_pairs={{3,0},{2,1},{1,2},{0,3},{5,4},{4,5},{7,6},{6,7},{11,8},{10,9},{9,1... | collective-permute-start | bytes 663560 | tf_op jit(solution)/shard_map/second_tick/ppermute | solution.py:32
  91.3 0.0 copy-done.6
  91.3 4.0 %second_tick.11 = (bf16[4,72,256]{2,1,0:T(8,128)(2,1)S(1)}, bf16[4,72,256]{2,1,0:T(8,128)(2,1)S(1)}, bf16[4,72,256]{2,1,0:T(8,128)(2,1)S(1)}, f32[8,256]{1,0:T(8...) custom-call(bf16[96,1152]{1,0:T(8,128)(2,1)S(1)} %second_tick.9.refs, ...), custom_call_target="tpu_custom_call" | custom-call | flops 736100352 | bytes 4194304 | tf_op jit(solution)/shard_map/second_tick/pallas_call | solution.py:91
  95.3 0.0 collective-permute-done.10.part_ref
  95.3 1.1 second_tick.12
  96.4 1.3 %collective-permute-done.9.refs_0_ = bf16[96,1152]{1,0:T(8,128)(2,1)S(1)} collective-permute-done((bf16[96,1152]{1,0:T(8,128)(2,1)S(1)}, bf16[96,1152]{1,0:T(8,128)(2,1)S(1)}, u32[]{:S(2)}, u32[]{:S(2)}) %collective-permute-start.9) | collective-permute-done | bytes 221216 | tf_op jit(solution)/shard_map/second_tick/ppermute | solution.py:32
  97.7 2.6 %second_tick.13 = (bf16[288,256]{1,0:T(8,128)(2,1)S(1)}, bf16[4,72,256]{2,1,0:T(8,128)(2,1)S(1)}, bf16[4,72,96]{2,1,0:T(8,128)(2,1)S(1)}, bf16[4,72,96]{2,1,0:T(8,128)(2,1)S(1)}) custom-call(bf16[96,1152]{1,0:T(8,128)(2,1)S(1)} %collective-permute-done.9.refs_0_, bf16[4,72,160]{2,1,0:T(8,128)(2,1)S(1)} %get-tuple-element.76.refs_1_, ...), custom_call_target="tpu_custom_call" | custom-call | flops 342097920 | bytes 4194304 | tf_op jit(solution)/shard_map/second_tick/pallas_call | solution.py:91
  100.4 1.9 %collective-permute-start.11 = (bf16[288,256]{1,0:T(8,128)(2,1)S(1)}, bf16[288,256]{1,0:T(8,128)(2,1)S(1)}, u32[]{:S(2)}, u32[]{:S(2)}) collective-permute-start(bf16[288,256]{1,0:T(8,128)(2,1)S(1)} %get-tuple-element.82), channel_id=1, source_target_pairs={{1,0},{0,1},{3,2},{2,3},{7,4},{6,5},{5,6},{4,7},{9,8},{8,9},{11,10... | collective-permute-start | bytes 442376 | tf_op jit(solution)/shard_map/second_tick/ppermute | solution.py:32
  102.3 1.2 second_tick.14.refs_0_
  103.5 5.2 %collective-permute-done.11.refs_1_ = bf16[288,256]{1,0:T(8,128)(2,1)S(1)} collective-permute-done((bf16[288,256]{1,0:T(8,128)(2,1)S(1)}, bf16[288,256]{1,0:T(8,128)(2,1)S(1)}, u32[]{:S(2)}, u32[]{:S(2)}) %collective-permute-start.11) | collective-permute-done | bytes 147488 | tf_op jit(solution)/shard_map/second_tick/ppermute | solution.py:32
  108.7 0.5 second_tick.16
  109.2 9.0 %collective-permute-start.12 = (bf16[128,1152]{1,0:T(8,128)(2,1)S(1)}, bf16[128,1152]{1,0:T(8,128)(2,1)S(1)}, u32[]{:S(2)}, u32[]{:S(2)}) collective-permute-start(bf16[128,1152]{1,0:T(8,128)(2,1)S(1)} %second_tick.16), channel_id=1, source_target_pairs={{3,0},{2,1},{1,2},{0,3},{5,4},{4,5},{7,6},{6,7},{11,8},{10,9},{9,1... | collective-permute-start | bytes 884744 | tf_op jit(solution)/shard_map/second_tick/ppermute | solution.py:32
  118.2 0.5 second_tick.15.refs_2_
  118.8 5.9 %collective-permute-done.12.refs_3_ = bf16[128,1152]{1,0:T(8,128)(2,1)S(1)} collective-permute-done((bf16[128,1152]{1,0:T(8,128)(2,1)S(1)}, bf16[128,1152]{1,0:T(8,128)(2,1)S(1)}, u32[]{:S(2)}, u32[]{:S(2)}) %collective-permute-start.12) | collective-permute-done | bytes 294944 | tf_op jit(solution)/shard_map/second_tick/ppermute | solution.py:32
  124.7 0.8 second_tick.17
  (3 shorter events, 0.1 us)
Async XLA Ops:
  0.0 25.8 %copy-start.1 = (bf16[1,288,1152]{2,1,0:T(8,128)(2,1)S(1)}, bf16[1,288,1152]{2,1,0:T(8,128)(2,1)}, u32[]{:S(2)}) copy-start(bf16[1,288,1152]{2,1,0:T(8,128)(2,1)} %param.9) | copy-start | bytes 1990660
  0.0 25.8 %copy-start.2 = (bf16[1,1024,288]{1,2,0:T(8,128)(2,1)S(1)}, bf16[1,1024,288]{1,2,0:T(8,128)(2,1)}, u32[]{:S(2)}) copy-start(bf16[1,1024,288]{1,2,0:T(8,128)(2,1)} %param.11) | copy-start | bytes 1769476
  0.0 14.0 %collective-permute-start = (bf16[128,1152]{1,0:T(8,128)(2,1)}, bf16[128,1152]{1,0:T(8,128)(2,1)S(1)}, u32[]{:S(2)}, u32[]{:S(2)}) collective-permute-start(bf16[128,1152]{1,0:T(8,128)(2,1)} %bitcast.23), channel_id=1, source_target_pairs={{1,0},{0,1},{3,2},{2,3},{7,4},{6,5},{5,6},{4,7},{9,8},{8,9},{11,10... | collective-permute-start | bytes 884744 | tf_op jit(solution)/shard_map/first_gather/ppermute | solution.py:32
  6.2 1.0 copy-start.4
  14.0 18.3 %collective-permute-start.1 = (bf16[128,1152]{1,0:T(8,128)(2,1)S(1)}, bf16[128,1152]{1,0:T(8,128)(2,1)S(1)}, u32[]{:S(2)}, u32[]{:S(2)}) collective-permute-start(bf16[128,1152]{1,0:T(8,128)(2,1)S(1)} %first_gather.4), channel_id=1, source_target_pairs={{3,0},{2,1},{1,2},{0,3},{5,4},{4,5},{7,6},{6,7},{11,8},{10,9},{9,1... | collective-permute-start | bytes 884744 | tf_op jit(solution)/shard_map/first_gather/ppermute | solution.py:32
  23.1 13.7 %collective-permute-start.2 = (bf16[128,1152]{1,0:T(8,128)(2,1)S(1)}, bf16[128,1152]{1,0:T(8,128)(2,1)S(1)}, u32[]{:S(2)}, u32[]{:S(2)}) collective-permute-start(bf16[128,1152]{1,0:T(8,128)(2,1)S(1)} %first_gather.5), channel_id=1, source_target_pairs={{3,0},{2,1},{1,2},{0,3},{5,4},{4,5},{7,6},{6,7},{11,8},{10,9},{9,1... | collective-permute-start | bytes 884744 | tf_op jit(solution)/shard_map/first_gather/ppermute | solution.py:32
  25.8 1.6 %copy-start = (bf16[1,1152,3,288]{1,3,2,0:T(8,128)(2,1)S(1)}, bf16[1,1152,3,288]{1,3,2,0:T(8,128)(2,1)}, u32[]{:S(2)}) copy-start(bf16[1,1152,3,288]{1,3,2,0:T(8,128)(2,1)} %param.8) | copy-start | bytes 5971972
  27.3 1.1 copy-start.3
  28.4 0.7 copy-start.5
  29.9 22.8 %collective-permute-start.4 = (bf16[288,1152]{1,0:T(8,128)(2,1)S(1)}, bf16[288,1152]{1,0:T(8,128)(2,1)S(1)}, u32[]{:S(2)}, u32[]{:S(2)}) collective-permute-start(bf16[288,1152]{1,0:T(8,128)(2,1)S(1)} %bitcast.20), channel_id=1, source_target_pairs={{1,0},{0,1},{3,2},{2,3},{7,4},{6,5},{5,6},{4,7},{9,8},{8,9},{11,10... | collective-permute-start | bytes 1990664 | tf_op jit(solution)/shard_map/first_gather/ppermute | solution.py:32
  39.8 12.9 %collective-permute-start.3 = (bf16[288,256]{1,0:T(8,128)(2,1)S(1)}, bf16[288,256]{1,0:T(8,128)(2,1)S(1)}, u32[]{:S(2)}, u32[]{:S(2)}) collective-permute-start(bf16[288,256]{1,0:T(8,128)(2,1)S(1)} %get-tuple-element.59), channel_id=1, source_target_pairs={{1,0},{0,1},{3,2},{2,3},{7,4},{6,5},{5,6},{4,7},{9,8},{8,9},{11,10... | collective-permute-start | bytes 442376 | tf_op jit(solution)/shard_map/first_tick/ppermute | solution.py:32
  52.7 38.6 %copy-start.6 = (s32[1,2]{1,0:T(1,128)S(1)}, s32[1,2]{1,0:T(1,128)}, u32[]{:S(2)}) copy-start(s32[1,2]{1,0:T(1,128)} %param.13) | copy-start | bytes 28
  53.6 20.2 %collective-permute-start.7 = (bf16[160,1152]{1,0:T(8,128)(2,1)S(1)}, bf16[160,1152]{1,0:T(8,128)(2,1)S(1)}, u32[]{:S(2)}, u32[]{:S(2)}) collective-permute-start(bf16[160,1152]{1,0:T(8,128)(2,1)S(1)} %get-tuple-element.64), channel_id=1, source_target_pairs={{0,4},{1,5},{2,6},{3,7},{4,8},{5,9},{6,10},{7,11},{8,12},{9,13},{1... | collective-permute-start | bytes 1105928 | tf_op jit(solution)/shard_map/second_tick/ppermute | solution.py:43
  55.5 18.3 %collective-permute-start.8 = (bf16[160,1152]{1,0:T(8,128)(2,1)S(1)}, bf16[160,1152]{1,0:T(8,128)(2,1)S(1)}, u32[]{:S(2)}, u32[]{:S(2)}) collective-permute-start(bf16[160,1152]{1,0:T(8,128)(2,1)S(1)} %get-tuple-element.65), channel_id=1, source_target_pairs={{0,7},{1,6},{2,5},{3,4},{4,9},{5,8},{6,11},{7,10},{8,15},{9,14},{1... | collective-permute-start | bytes 1105928 | tf_op jit(solution)/shard_map/second_tick/ppermute | solution.py:43
  64.3 20.1 %collective-permute-start.5 = (bf16[96,1152]{1,0:T(8,128)(2,1)S(1)}, bf16[96,1152]{1,0:T(8,128)(2,1)S(1)}, u32[]{:S(2)}, u32[]{:S(2)}) collective-permute-start(bf16[96,1152]{1,0:T(8,128)(2,1)S(1)} %get-tuple-element.62), channel_id=1, source_target_pairs={{0,4},{1,5},{2,6},{3,7},{4,8},{5,9},{6,10},{7,11},{8,12},{9,13},{1... | collective-permute-start | bytes 663560 | tf_op jit(solution)/shard_map/second_tick/ppermute | solution.py:43
  66.9 17.5 %collective-permute-start.6 = (bf16[96,1152]{1,0:T(8,128)(2,1)S(1)}, bf16[96,1152]{1,0:T(8,128)(2,1)S(1)}, u32[]{:S(2)}, u32[]{:S(2)}) collective-permute-start(bf16[96,1152]{1,0:T(8,128)(2,1)S(1)} %get-tuple-element.63), channel_id=1, source_target_pairs={{0,7},{1,6},{2,5},{3,4},{4,9},{5,8},{6,11},{7,10},{8,15},{9,14},{1... | collective-permute-start | bytes 663560 | tf_op jit(solution)/shard_map/second_tick/ppermute | solution.py:43
  73.9 21.4 %collective-permute-start.10 = (bf16[160,1152]{1,0:T(8,128)(2,1)S(1)}, bf16[160,1152]{1,0:T(8,128)(2,1)S(1)}, u32[]{:S(2)}, u32[]{:S(2)}) collective-permute-start(bf16[160,1152]{1,0:T(8,128)(2,1)S(1)} %second_tick.10.refs_1_), channel_id=1, source_target_pairs={{3,0},{2,1},{1,2},{0,3},{5,4},{4,5},{7,6},{6,7},{11,8},{10,9},{9,1... | collective-permute-start | bytes 1105928 | tf_op jit(solution)/shard_map/second_tick/ppermute | solution.py:32
  84.5 13.3 %collective-permute-start.9 = (bf16[96,1152]{1,0:T(8,128)(2,1)S(1)}, bf16[96,1152]{1,0:T(8,128)(2,1)S(1)}, u32[]{:S(2)}, u32[]{:S(2)}) collective-permute-start(bf16[96,1152]{1,0:T(8,128)(2,1)S(1)} %second_tick.9.refs_0_), channel_id=1, source_target_pairs={{3,0},{2,1},{1,2},{0,3},{5,4},{4,5},{7,6},{6,7},{11,8},{10,9},{9,1... | collective-permute-start | bytes 663560 | tf_op jit(solution)/shard_map/second_tick/ppermute | solution.py:32
  100.4 8.3 %collective-permute-start.11 = (bf16[288,256]{1,0:T(8,128)(2,1)S(1)}, bf16[288,256]{1,0:T(8,128)(2,1)S(1)}, u32[]{:S(2)}, u32[]{:S(2)}) collective-permute-start(bf16[288,256]{1,0:T(8,128)(2,1)S(1)} %get-tuple-element.82), channel_id=1, source_target_pairs={{1,0},{0,1},{3,2},{2,3},{7,4},{6,5},{5,6},{4,7},{9,8},{8,9},{11,10... | collective-permute-start | bytes 442376 | tf_op jit(solution)/shard_map/second_tick/ppermute | solution.py:32
  109.2 15.5 %collective-permute-start.12 = (bf16[128,1152]{1,0:T(8,128)(2,1)S(1)}, bf16[128,1152]{1,0:T(8,128)(2,1)S(1)}, u32[]{:S(2)}, u32[]{:S(2)}) collective-permute-start(bf16[128,1152]{1,0:T(8,128)(2,1)S(1)} %second_tick.16), channel_id=1, source_target_pairs={{3,0},{2,1},{1,2},{0,3},{5,4},{4,5},{7,6},{6,7},{11,8},{10,9},{9,1... | collective-permute-start | bytes 884744 | tf_op jit(solution)/shard_map/second_tick/ppermute | solution.py:32

commit v8 on v6

--- a/solution.py
+++ b/solution.py
@@ -320,22 +320,30 @@
     )
 
 
-def update_kernel(places, n_parts, mods_ref, *refs):
-    parts, (mine_ref, theirs_ref, out_ref) = refs[:n_parts], refs[n_parts:]
-    attended = mine_ref[...].astype(jnp.float32) + theirs_ref[...].astype(jnp.float32)
+def base_kernel(places, n_parts, mods_ref, *refs):
+    parts, (*refs, out_ref) = refs[:n_parts], refs[n_parts:]
+    added = mods_ref[2:3] * both_sums(0, out_ref.shape[0], *refs)
     at = 0
     for i, first, last in places:
         here = slice(at, at + last - first)
-        new = parts[i][first:last].astype(jnp.float32) + mods_ref[2:3] * attended[here]
-        out_ref[here] = new.astype(jnp.bfloat16)
+        out_ref[here] = parts[i][first:last].astype(jnp.float32) + added[here]
         at += last - first
 
 
-def update(parts, places, mods, mine, theirs):
-    return call(
-        functools.partial(update_kernel, places, len(parts)),
-        shape(jnp.bfloat16, *mine.shape), [], 4 * mine.size, 0, (mods, *parts, mine, theirs),
-    )
+def base(parts, places, mods, mine, theirs, w_mine, w_theirs):
+    rows, features, width = mine.shape[1] // 2, w_mine.shape[1], mine.shape[0]
+    return call(
+        functools.partial(base_kernel, places, len(parts)), shape(jnp.float32, rows, features), [],
+        4 * rows * features * width, 0, (mods, *parts, mine, theirs, w_mine, w_theirs),
+    )
+
+
+def update_kernel(base_ref, mods_ref, theirs_ref, out_ref):
+    out_ref[...] = (base_ref[...] + mods_ref[2:3] * theirs_ref[...].astype(jnp.float32)).astype(jnp.bfloat16)
+
+
+def update(hidden, mods, theirs):
+    return call(update_kernel, shape(jnp.bfloat16, *hidden.shape), [], 2 * hidden.size, 0, (hidden, mods, theirs))
 
 
 def halve_kernel(own_ref, a_ref, b_ref):
@@ -401,9 +409,8 @@
         places = [tuple(places)] * 2
         mine, theirs, *_ = block(here, others, places, (slots, *olds), mods, w, ko_next, vo_next)
         from_one = exchange(part(rows, jnp.bfloat16, mine, theirs, w_mine, w_theirs), 1)
-        mine_own = part(0, jnp.float32, mine, theirs, w_mine, w_theirs)
         own_rows = tuple((i, 0, size) for i, size in enumerate(sizes))
-        return update(here, own_rows, mods, mine_own, from_one)[None]
+        return update(base(here, own_rows, mods, mine, theirs, w_mine, w_theirs), mods, from_one)[None]
 
 
 def solution(mesh):

time: 127 us -> 126 us (level)
  no operation moved by 1% of the time
where the time goes in v8:
time: 126 us
  starting transfers between devices  71 us (56%)
  waiting for transfers between devices  30.4 us (24%)
  Pallas kernels  19.2 us (15%)
  local copies, waits for them, and re-layouts  4.96 us (4%)
    ppermute x9, starting transfers between devices, exchange(): return lax.ppermute(array, AXES, moves)  50.8 us
    ppermute x9, waiting for transfers between devices, exchange(): return lax.ppermute(array, AXES, moves)  30.4 us
    ppermute x4, starting transfers between devices, advance(): return lax.ppermute(array, AXES, moves)  20.2 us
    pallas_call x16, Pallas kernels, call(): pl.pallas_call(kernel, out_shape=outs, in_specs=specs, scratch_shapes=scr...  19.2 us
    unnamed x15, local copies, waits for them, and re-layouts  4.96 us
  transfers between devices with their start and end apart: 13, of which 6 were waited for; matrix products, arithmetic and copies ran while one was open for 1% of the time, Pallas kernels for 11%

profile of v8, /device:TPU:64, one launch (start us, length us, event | category | flops | bytes accessed | tf_op | source)
XLA Modules:
  0.0 125.8 jit_solution(4093315776714949942)
XLA Ops:
  0.0 0.0 copy-start.1
  0.0 0.0 copy-start.2
  0.0 6.2 %collective-permute-start = (bf16[128,1152]{1,0:T(8,128)(2,1)}, bf16[128,1152]{1,0:T(8,128)(2,1)S(1)}, u32[]{:S(2)}, u32[]{:S(2)}) collective-permute-start(bf16[128,1152]{1,0:T(8,128)(2,1)} %bitcast.23), channel_id=1, source_target_pairs={{1,0},{0,1},{3,2},{2,3},{7,4},{6,5},{5,6},{4,7},{9,8},{8,9},{11,10... | collective-permute-start | bytes 884744 | tf_op jit(solution)/shard_map/first_gather/ppermute | solution.py:32
  6.2 0.0 copy-start.4
  6.2 1.0 copy-done.4
  7.2 6.7 %collective-permute-done.zero_ref.refs_0_ = bf16[128,1152]{1,0:T(8,128)(2,1)S(1)} collective-permute-done((bf16[128,1152]{1,0:T(8,128)(2,1)}, bf16[128,1152]{1,0:T(8,128)(2,1)S(1)}, u32[]{:S(2)}, u32[]{:S(2)}) %collective-permute-start) | collective-permute-done | bytes 294944 | tf_op jit(solution)/shard_map/first_gather/ppermute | solution.py:32
  14.0 9.1 %collective-permute-start.1 = (bf16[128,1152]{1,0:T(8,128)(2,1)S(1)}, bf16[128,1152]{1,0:T(8,128)(2,1)S(1)}, u32[]{:S(2)}, u32[]{:S(2)}) collective-permute-start(bf16[128,1152]{1,0:T(8,128)(2,1)S(1)} %first_gather.4), channel_id=1, source_target_pairs={{3,0},{2,1},{1,2},{0,3},{5,4},{4,5},{7,6},{6,7},{11,8},{10,9},{9,1... | collective-permute-start | bytes 884744 | tf_op jit(solution)/shard_map/first_gather/ppermute | solution.py:32
  23.1 1.9 %collective-permute-start.2 = (bf16[128,1152]{1,0:T(8,128)(2,1)S(1)}, bf16[128,1152]{1,0:T(8,128)(2,1)S(1)}, u32[]{:S(2)}, u32[]{:S(2)}) collective-permute-start(bf16[128,1152]{1,0:T(8,128)(2,1)S(1)} %first_gather.5), channel_id=1, source_target_pairs={{3,0},{2,1},{1,2},{0,3},{5,4},{4,5},{7,6},{6,7},{11,8},{10,9},{9,1... | collective-permute-start | bytes 884744 | tf_op jit(solution)/shard_map/first_gather/ppermute | solution.py:32
  25.0 0.7 copy.10
  25.8 0.0 copy-done.1
  25.8 0.0 copy-done.2
  25.8 0.0 copy-start
  25.8 1.5 %copy-done = bf16[1,1152,3,288]{1,3,2,0:T(8,128)(2,1)S(1)} copy-done((bf16[1,1152,3,288]{1,3,2,0:T(8,128)(2,1)S(1)}, bf16[1,1152,3,288]{1,3,2,0:T(8,128)(2,1)}, u32[]{:S(2)}) %copy-start) | copy-done | bytes 1990680
  27.3 0.0 copy-start.3
  27.3 1.1 copy-done.3
  28.4 0.0 copy-start.5
  28.4 0.7 copy-done.5
  29.0 0.8 prepare.1
  29.9 2.4 %collective-permute-start.4 = (bf16[288,1152]{1,0:T(8,128)(2,1)S(1)}, bf16[288,1152]{1,0:T(8,128)(2,1)S(1)}, u32[]{:S(2)}, u32[]{:S(2)}) collective-permute-start(bf16[288,1152]{1,0:T(8,128)(2,1)S(1)} %bitcast.20), channel_id=1, source_target_pairs={{1,0},{0,1},{3,2},{2,3},{7,4},{6,5},{5,6},{4,7},{9,8},{8,9},{11,10... | collective-permute-start | bytes 1990664 | tf_op jit(solution)/shard_map/first_gather/ppermute | solution.py:32
  32.3 0.0 collective-permute-done.1.refs_1_.other_a
  32.3 3.1 %first_tick.4 = (bf16[4,72,256]{2,1,0:T(8,128)(2,1)S(1)}, bf16[4,72,256]{2,1,0:T(8,128)(2,1)S(1)}, bf16[4,72,256]{2,1,0:T(8,128)(2,1)S(1)}, f32[8,256]{1,0:T(8,1...) custom-call(bf16[128,1152]{1,0:T(8,128)(2,1)S(1)} %collective-permute-done.zero_ref.refs_0_, ...), custom_call_target="tpu_custom_call" | custom-call | flops 736100352 | bytes 4194304 | tf_op jit(solution)/shard_map/first_tick/pallas_call | solution.py:91
  35.4 1.4 %collective-permute-done.2.refs_1_.other_b = bf16[128,1152]{1,0:T(8,128)(2,1)S(1)} collective-permute-done((bf16[128,1152]{1,0:T(8,128)(2,1)S(1)}, bf16[128,1152]{1,0:T(8,128)(2,1)S(1)}, u32[]{:S(2)}, u32[]{:S(2)}) %collective-permute-start.2) | collective-permute-done | bytes 294944 | tf_op jit(solution)/shard_map/first_gather/ppermute | solution.py:32
  36.8 3.0 %first_tick.5 = (bf16[288,256]{1,0:T(8,128)(2,1)S(1)}, bf16[4,72,256]{2,1,0:T(8,128)(2,1)S(1)}, bf16[4,72,256]{2,1,0:T(8,128)(2,1)S(1)}, bf16[4,72,256]{2,1,0:T(8,128)(2,1)S(1)}) custom-call(bf16[128,1152]{1,0:T(8,128)(2,1)S(1)} %collective-permute-done.zero_ref.refs_0_, bf16[128,1152]{1,0:T(8,128)(2,1)S(1)} %collective-permute-done.2.refs_1_.other_b, ...), custom_call_target="tpu_custom_call" | custom-call | flops 660602880 | bytes 4194304 | tf_op jit(solution)/shard_map/first_tick/pallas_call | solution.py:91
  39.8 2.9 %collective-permute-start.3 = (bf16[288,256]{1,0:T(8,128)(2,1)S(1)}, bf16[288,256]{1,0:T(8,128)(2,1)S(1)}, u32[]{:S(2)}, u32[]{:S(2)}) collective-permute-start(bf16[288,256]{1,0:T(8,128)(2,1)S(1)} %get-tuple-element.56), channel_id=1, source_target_pairs={{1,0},{0,1},{3,2},{2,3},{7,4},{6,5},{5,6},{4,7},{9,8},{8,9},{11,10... | collective-permute-start | bytes 442376 | tf_op jit(solution)/shard_map/first_tick/ppermute | solution.py:32
  42.8 1.2 first_tick.6.refs_0_
  44.0 8.7 %collective-permute-done.3.refs_1_ = bf16[288,256]{1,0:T(8,128)(2,1)S(1)} collective-permute-done((bf16[288,256]{1,0:T(8,128)(2,1)S(1)}, bf16[288,256]{1,0:T(8,128)(2,1)S(1)}, u32[]{:S(2)}, u32[]{:S(2)}) %collective-permute-start.3) | collective-permute-done | bytes 147488 | tf_op jit(solution)/shard_map/first_tick/ppermute | solution.py:32
  52.7 0.0 collective-permute-done.4.refs_3_.refs_5_
  52.7 0.0 copy-start.6
  52.7 0.9 first_tick.7
  53.6 1.9 %collective-permute-start.7 = (bf16[160,1152]{1,0:T(8,128)(2,1)S(1)}, bf16[160,1152]{1,0:T(8,128)(2,1)S(1)}, u32[]{:S(2)}, u32[]{:S(2)}) collective-permute-start(bf16[160,1152]{1,0:T(8,128)(2,1)S(1)} %get-tuple-element.61), channel_id=1, source_target_pairs={{0,4},{1,5},{2,6},{3,7},{4,8},{5,9},{6,10},{7,11},{8,12},{9,13},{1... | collective-permute-start | bytes 1105928 | tf_op jit(solution)/shard_map/second_tick/ppermute | solution.py:43
  55.5 8.8 %collective-permute-start.8 = (bf16[160,1152]{1,0:T(8,128)(2,1)S(1)}, bf16[160,1152]{1,0:T(8,128)(2,1)S(1)}, u32[]{:S(2)}, u32[]{:S(2)}) collective-permute-start(bf16[160,1152]{1,0:T(8,128)(2,1)S(1)} %get-tuple-element.62), channel_id=1, source_target_pairs={{0,7},{1,6},{2,5},{3,4},{4,9},{5,8},{6,11},{7,10},{8,15},{9,14},{1... | collective-permute-start | bytes 1105928 | tf_op jit(solution)/shard_map/second_tick/ppermute | solution.py:43
  64.3 2.7 %collective-permute-start.5 = (bf16[96,1152]{1,0:T(8,128)(2,1)S(1)}, bf16[96,1152]{1,0:T(8,128)(2,1)S(1)}, u32[]{:S(2)}, u32[]{:S(2)}) collective-permute-start(bf16[96,1152]{1,0:T(8,128)(2,1)S(1)} %get-tuple-element.59), channel_id=1, source_target_pairs={{0,4},{1,5},{2,6},{3,7},{4,8},{5,9},{6,10},{7,11},{8,12},{9,13},{1... | collective-permute-start | bytes 663560 | tf_op jit(solution)/shard_map/second_tick/ppermute | solution.py:43
  66.9 6.8 %collective-permute-start.6 = (bf16[96,1152]{1,0:T(8,128)(2,1)S(1)}, bf16[96,1152]{1,0:T(8,128)(2,1)S(1)}, u32[]{:S(2)}, u32[]{:S(2)}) collective-permute-start(bf16[96,1152]{1,0:T(8,128)(2,1)S(1)} %get-tuple-element.60), channel_id=1, source_target_pairs={{0,7},{1,6},{2,5},{3,4},{4,9},{5,8},{6,11},{7,10},{8,15},{9,14},{1... | collective-permute-start | bytes 663560 | tf_op jit(solution)/shard_map/second_tick/ppermute | solution.py:43
  73.8 0.0 collective-permute-done.7.straight_ref
  73.8 0.0 collective-permute-done.8.crossing_ref
  73.8 0.1 second_tick.9.refs_1_
  73.9 10.5 %collective-permute-start.10 = (bf16[160,1152]{1,0:T(8,128)(2,1)S(1)}, bf16[160,1152]{1,0:T(8,128)(2,1)S(1)}, u32[]{:S(2)}, u32[]{:S(2)}) collective-permute-start(bf16[160,1152]{1,0:T(8,128)(2,1)S(1)} %second_tick.9.refs_1_), channel_id=1, source_target_pairs={{3,0},{2,1},{1,2},{0,3},{5,4},{4,5},{7,6},{6,7},{11,8},{10,9},{9,1... | collective-permute-start | bytes 1105928 | tf_op jit(solution)/shard_map/second_tick/ppermute | solution.py:32
  84.4 0.0 collective-permute-done.5.straight_ref
  84.4 0.0 collective-permute-done.6.crossing_ref
  84.4 0.1 second_tick.8.refs_0_
  84.5 6.8 %collective-permute-start.9 = (bf16[96,1152]{1,0:T(8,128)(2,1)S(1)}, bf16[96,1152]{1,0:T(8,128)(2,1)S(1)}, u32[]{:S(2)}, u32[]{:S(2)}) collective-permute-start(bf16[96,1152]{1,0:T(8,128)(2,1)S(1)} %second_tick.8.refs_0_), channel_id=1, source_target_pairs={{3,0},{2,1},{1,2},{0,3},{5,4},{4,5},{7,6},{6,7},{11,8},{10,9},{9,1... | collective-permute-start | bytes 663560 | tf_op jit(solution)/shard_map/second_tick/ppermute | solution.py:32
  91.3 0.0 copy-done.6
  91.3 3.9 %second_tick.10 = (bf16[4,72,256]{2,1,0:T(8,128)(2,1)S(1)}, bf16[4,72,256]{2,1,0:T(8,128)(2,1)S(1)}, bf16[4,72,256]{2,1,0:T(8,128)(2,1)S(1)}, f32[8,256]{1,0:T(8...) custom-call(bf16[96,1152]{1,0:T(8,128)(2,1)S(1)} %second_tick.8.refs, ...), custom_call_target="tpu_custom_call" | custom-call | flops 736100352 | bytes 4194304 | tf_op jit(solution)/shard_map/second_tick/pallas_call | solution.py:91
  95.3 2.5 %collective-permute-done.9.refs_0_ = bf16[96,1152]{1,0:T(8,128)(2,1)S(1)} collective-permute-done((bf16[96,1152]{1,0:T(8,128)(2,1)S(1)}, bf16[96,1152]{1,0:T(8,128)(2,1)S(1)}, u32[]{:S(2)}, u32[]{:S(2)}) %collective-permute-start.9) | collective-permute-done | bytes 221216 | tf_op jit(solution)/shard_map/second_tick/ppermute | solution.py:32
  97.7 0.0 collective-permute-done.10.refs_1_
  97.7 3.0 %second_tick.11 = (bf16[288,256]{1,0:T(8,128)(2,1)S(1)}, bf16[4,72,256]{2,1,0:T(8,128)(2,1)S(1)}, bf16[4,72,256]{2,1,0:T(8,128)(2,1)S(1)}, bf16[4,72,256]{2,1,0:T(8,128)(2,1)S(1)}) custom-call(bf16[96,1152]{1,0:T(8,128)(2,1)S(1)} %collective-permute-done.9.refs_0_, bf16[160,1152]{1,0:T(8,128)(2,1)S(1)} %collective-permute-done.10.refs_1_, ...), custom_call_target="tpu_custom_call" | custom-call | flops 660602880 | bytes 4194304 | tf_op jit(solution)/shard_map/second_tick/pallas_call | solution.py:91
  100.7 1.9 %collective-permute-start.11 = (bf16[288,256]{1,0:T(8,128)(2,1)S(1)}, bf16[288,256]{1,0:T(8,128)(2,1)S(1)}, u32[]{:S(2)}, u32[]{:S(2)}) collective-permute-start(bf16[288,256]{1,0:T(8,128)(2,1)S(1)} %get-tuple-element.76), channel_id=1, source_target_pairs={{1,0},{0,1},{3,2},{2,3},{7,4},{6,5},{5,6},{4,7},{9,8},{8,9},{11,10... | collective-permute-start | bytes 442376 | tf_op jit(solution)/shard_map/second_tick/ppermute | solution.py:32
  102.7 1.2 second_tick.12.refs_2_.refs_0_
  103.9 5.2 %collective-permute-done.11.refs_3_.refs_1_ = bf16[288,256]{1,0:T(8,128)(2,1)S(1)} collective-permute-done((bf16[288,256]{1,0:T(8,128)(2,1)S(1)}, bf16[288,256]{1,0:T(8,128)(2,1)S(1)}, u32[]{:S(2)}, u32[]{:S(2)}) %collective-permute-start.11) | collective-permute-done | bytes 147488 | tf_op jit(solution)/shard_map/second_tick/ppermute | solution.py:32
  109.0 0.5 second_tick.14
  109.6 9.0 %collective-permute-start.12 = (bf16[128,1152]{1,0:T(8,128)(2,1)S(1)}, bf16[128,1152]{1,0:T(8,128)(2,1)S(1)}, u32[]{:S(2)}, u32[]{:S(2)}) collective-permute-start(bf16[128,1152]{1,0:T(8,128)(2,1)S(1)} %second_tick.14), channel_id=1, source_target_pairs={{3,0},{2,1},{1,2},{0,3},{5,4},{4,5},{7,6},{6,7},{11,8},{10,9},{9,1... | collective-permute-start | bytes 884744 | tf_op jit(solution)/shard_map/second_tick/ppermute | solution.py:32
  118.6 0.5 second_tick.13.base_ref
  119.1 5.9 %collective-permute-done.12.theirs_ref = bf16[128,1152]{1,0:T(8,128)(2,1)S(1)} collective-permute-done((bf16[128,1152]{1,0:T(8,128)(2,1)S(1)}, bf16[128,1152]{1,0:T(8,128)(2,1)S(1)}, u32[]{:S(2)}, u32[]{:S(2)}) %collective-permute-start.12) | collective-permute-done | bytes 294944 | tf_op jit(solution)/shard_map/second_tick/ppermute | solution.py:32
  125.1 0.8 second_tick.15
  (3 shorter events, 0.1 us)
Async XLA Ops:
  0.0 25.8 %copy-start.1 = (bf16[1,288,1152]{2,1,0:T(8,128)(2,1)S(1)}, bf16[1,288,1152]{2,1,0:T(8,128)(2,1)}, u32[]{:S(2)}) copy-start(bf16[1,288,1152]{2,1,0:T(8,128)(2,1)} %param.9) | copy-start | bytes 1990660
  0.0 25.8 %copy-start.2 = (bf16[1,1024,288]{1,2,0:T(8,128)(2,1)S(1)}, bf16[1,1024,288]{1,2,0:T(8,128)(2,1)}, u32[]{:S(2)}) copy-start(bf16[1,1024,288]{1,2,0:T(8,128)(2,1)} %param.11) | copy-start | bytes 1769476
  0.0 14.0 %collective-permute-start = (bf16[128,1152]{1,0:T(8,128)(2,1)}, bf16[128,1152]{1,0:T(8,128)(2,1)S(1)}, u32[]{:S(2)}, u32[]{:S(2)}) collective-permute-start(bf16[128,1152]{1,0:T(8,128)(2,1)} %bitcast.23), channel_id=1, source_target_pairs={{1,0},{0,1},{3,2},{2,3},{7,4},{6,5},{5,6},{4,7},{9,8},{8,9},{11,10... | collective-permute-start | bytes 884744 | tf_op jit(solution)/shard_map/first_gather/ppermute | solution.py:32
  6.2 1.0 copy-start.4
  14.0 18.3 %collective-permute-start.1 = (bf16[128,1152]{1,0:T(8,128)(2,1)S(1)}, bf16[128,1152]{1,0:T(8,128)(2,1)S(1)}, u32[]{:S(2)}, u32[]{:S(2)}) collective-permute-start(bf16[128,1152]{1,0:T(8,128)(2,1)S(1)} %first_gather.4), channel_id=1, source_target_pairs={{3,0},{2,1},{1,2},{0,3},{5,4},{4,5},{7,6},{6,7},{11,8},{10,9},{9,1... | collective-permute-start | bytes 884744 | tf_op jit(solution)/shard_map/first_gather/ppermute | solution.py:32
  23.1 13.7 %collective-permute-start.2 = (bf16[128,1152]{1,0:T(8,128)(2,1)S(1)}, bf16[128,1152]{1,0:T(8,128)(2,1)S(1)}, u32[]{:S(2)}, u32[]{:S(2)}) collective-permute-start(bf16[128,1152]{1,0:T(8,128)(2,1)S(1)} %first_gather.5), channel_id=1, source_target_pairs={{3,0},{2,1},{1,2},{0,3},{5,4},{4,5},{7,6},{6,7},{11,8},{10,9},{9,1... | collective-permute-start | bytes 884744 | tf_op jit(solution)/shard_map/first_gather/ppermute | solution.py:32
  25.8 1.6 %copy-start = (bf16[1,1152,3,288]{1,3,2,0:T(8,128)(2,1)S(1)}, bf16[1,1152,3,288]{1,3,2,0:T(8,128)(2,1)}, u32[]{:S(2)}) copy-start(bf16[1,1152,3,288]{1,3,2,0:T(8,128)(2,1)} %param.8) | copy-start | bytes 5971972
  27.3 1.1 copy-start.3
  28.4 0.7 copy-start.5
  29.9 22.8 %collective-permute-start.4 = (bf16[288,1152]{1,0:T(8,128)(2,1)S(1)}, bf16[288,1152]{1,0:T(8,128)(2,1)S(1)}, u32[]{:S(2)}, u32[]{:S(2)}) collective-permute-start(bf16[288,1152]{1,0:T(8,128)(2,1)S(1)} %bitcast.20), channel_id=1, source_target_pairs={{1,0},{0,1},{3,2},{2,3},{7,4},{6,5},{5,6},{4,7},{9,8},{8,9},{11,10... | collective-permute-start | bytes 1990664 | tf_op jit(solution)/shard_map/first_gather/ppermute | solution.py:32
  39.8 12.8 %collective-permute-start.3 = (bf16[288,256]{1,0:T(8,128)(2,1)S(1)}, bf16[288,256]{1,0:T(8,128)(2,1)S(1)}, u32[]{:S(2)}, u32[]{:S(2)}) collective-permute-start(bf16[288,256]{1,0:T(8,128)(2,1)S(1)} %get-tuple-element.56), channel_id=1, source_target_pairs={{1,0},{0,1},{3,2},{2,3},{7,4},{6,5},{5,6},{4,7},{9,8},{8,9},{11,10... | collective-permute-start | bytes 442376 | tf_op jit(solution)/shard_map/first_tick/ppermute | solution.py:32
  52.7 38.6 %copy-start.6 = (s32[1,2]{1,0:T(1,128)S(1)}, s32[1,2]{1,0:T(1,128)}, u32[]{:S(2)}) copy-start(s32[1,2]{1,0:T(1,128)} %param.13) | copy-start | bytes 28
  53.6 20.2 %collective-permute-start.7 = (bf16[160,1152]{1,0:T(8,128)(2,1)S(1)}, bf16[160,1152]{1,0:T(8,128)(2,1)S(1)}, u32[]{:S(2)}, u32[]{:S(2)}) collective-permute-start(bf16[160,1152]{1,0:T(8,128)(2,1)S(1)} %get-tuple-element.61), channel_id=1, source_target_pairs={{0,4},{1,5},{2,6},{3,7},{4,8},{5,9},{6,10},{7,11},{8,12},{9,13},{1... | collective-permute-start | bytes 1105928 | tf_op jit(solution)/shard_map/second_tick/ppermute | solution.py:43
  55.5 18.3 %collective-permute-start.8 = (bf16[160,1152]{1,0:T(8,128)(2,1)S(1)}, bf16[160,1152]{1,0:T(8,128)(2,1)S(1)}, u32[]{:S(2)}, u32[]{:S(2)}) collective-permute-start(bf16[160,1152]{1,0:T(8,128)(2,1)S(1)} %get-tuple-element.62), channel_id=1, source_target_pairs={{0,7},{1,6},{2,5},{3,4},{4,9},{5,8},{6,11},{7,10},{8,15},{9,14},{1... | collective-permute-start | bytes 1105928 | tf_op jit(solution)/shard_map/second_tick/ppermute | solution.py:43
  64.3 20.1 %collective-permute-start.5 = (bf16[96,1152]{1,0:T(8,128)(2,1)S(1)}, bf16[96,1152]{1,0:T(8,128)(2,1)S(1)}, u32[]{:S(2)}, u32[]{:S(2)}) collective-permute-start(bf16[96,1152]{1,0:T(8,128)(2,1)S(1)} %get-tuple-element.59), channel_id=1, source_target_pairs={{0,4},{1,5},{2,6},{3,7},{4,8},{5,9},{6,10},{7,11},{8,12},{9,13},{1... | collective-permute-start | bytes 663560 | tf_op jit(solution)/shard_map/second_tick/ppermute | solution.py:43
  66.9 17.5 %collective-permute-start.6 = (bf16[96,1152]{1,0:T(8,128)(2,1)S(1)}, bf16[96,1152]{1,0:T(8,128)(2,1)S(1)}, u32[]{:S(2)}, u32[]{:S(2)}) collective-permute-start(bf16[96,1152]{1,0:T(8,128)(2,1)S(1)} %get-tuple-element.60), channel_id=1, source_target_pairs={{0,7},{1,6},{2,5},{3,4},{4,9},{5,8},{6,11},{7,10},{8,15},{9,14},{1... | collective-permute-start | bytes 663560 | tf_op jit(solution)/shard_map/second_tick/ppermute | solution.py:43
  73.9 23.8 %collective-permute-start.10 = (bf16[160,1152]{1,0:T(8,128)(2,1)S(1)}, bf16[160,1152]{1,0:T(8,128)(2,1)S(1)}, u32[]{:S(2)}, u32[]{:S(2)}) collective-permute-start(bf16[160,1152]{1,0:T(8,128)(2,1)S(1)} %second_tick.9.refs_1_), channel_id=1, source_target_pairs={{3,0},{2,1},{1,2},{0,3},{5,4},{4,5},{7,6},{6,7},{11,8},{10,9},{9,1... | collective-permute-start | bytes 1105928 | tf_op jit(solution)/shard_map/second_tick/ppermute | solution.py:32
  84.5 13.2 %collective-permute-start.9 = (bf16[96,1152]{1,0:T(8,128)(2,1)S(1)}, bf16[96,1152]{1,0:T(8,128)(2,1)S(1)}, u32[]{:S(2)}, u32[]{:S(2)}) collective-permute-start(bf16[96,1152]{1,0:T(8,128)(2,1)S(1)} %second_tick.8.refs_0_), channel_id=1, source_target_pairs={{3,0},{2,1},{1,2},{0,3},{5,4},{4,5},{7,6},{6,7},{11,8},{10,9},{9,1... | collective-permute-start | bytes 663560 | tf_op jit(solution)/shard_map/second_tick/ppermute | solution.py:32
  100.7 8.3 %collective-permute-start.11 = (bf16[288,256]{1,0:T(8,128)(2,1)S(1)}, bf16[288,256]{1,0:T(8,128)(2,1)S(1)}, u32[]{:S(2)}, u32[]{:S(2)}) collective-permute-start(bf16[288,256]{1,0:T(8,128)(2,1)S(1)} %get-tuple-element.76), channel_id=1, source_target_pairs={{1,0},{0,1},{3,2},{2,3},{7,4},{6,5},{5,6},{4,7},{9,8},{8,9},{11,10... | collective-permute-start | bytes 442376 | tf_op jit(solution)/shard_map/second_tick/ppermute | solution.py:32
  109.6 15.5 %collective-permute-start.12 = (bf16[128,1152]{1,0:T(8,128)(2,1)S(1)}, bf16[128,1152]{1,0:T(8,128)(2,1)S(1)}, u32[]{:S(2)}, u32[]{:S(2)}) collective-permute-start(bf16[128,1152]{1,0:T(8,128)(2,1)S(1)} %second_tick.14), channel_id=1, source_target_pairs={{3,0},{2,1},{1,2},{0,3},{5,4},{4,5},{7,6},{6,7},{11,8},{10,9},{9,1... | collective-permute-start | bytes 884744 | tf_op jit(solution)/shard_map/second_tick/ppermute | solution.py:32
